TPU v7x, 128 devices: a whole 4x4x4 slice. The times are simulated.
128 devices in a mesh: slab: 8 (over z, core), row: 16 (over x, y).
Axes of the slice: x: 4, y: 4, z: 4, core: 2. Of those that a mesh axis runs over, the one named last changes fastest.
Arguments:
- moving: bfloat16 [16, 1024, 1024], P('slab', 'row'), may hold values from -6 to 6
- fixed: float32 [16, 1024, 1024], P('slab', 'row'), may hold values from -18 to 18
- requests: int32 [8, 16, 128, 2], P('slab', 'row'), may hold values from -1 to 31, as said below
- footpoints: int32 [8, 16, 32, 8], P('slab', 'row'), may hold values from 0 to 255, as said below
- offset_x: int32 [8, 16, 32], P('slab', 'row'), may hold values from 0 to 1
- offset_y: int32 [8, 16, 32], P('slab', 'row'), may hold values from 0 to 15
- offset_z: int32 [8, 16, 32], P('slab', 'row'), may hold values from 0 to 127
- fractions: float32 [8, 16, 32, 3], P('slab', 'row'), may hold values from 0 to 1
Outputs:
- solution: float32 [3, 16, 1024, 1024], P(None, 'slab', 'row')
- residual: float32 [3, 16, 1024, 1024], P(None, 'slab', 'row')
Inputs may be any that keep to these rules, and one draw needn't show every extreme that they name: `requests`: used slots come first for each device and peer, empty ones hold -1; every device asks some peer for all 2 slots. `footpoints`: entries are slots p * 2 + c with requests[device, p, c] not -1, and every such slot of the device is named.
All inputs are finite; a program needn't handle non-finite values.
Results may differ from a plain program's by a relative error of at most 0.0095.
Values may be sent and summed in bfloat16 or wider, within the bound.
No kernel may reach another device: no remote copies, remote signals or barrier semaphores. Data moves between devices by JAX's collectives and lax.ppermute only.
A program may use at most 64 MiB of HBM per device.

v0:
```python
import jax
import jax.numpy as jnp
from jax import lax
from jax.sharding import PartitionSpec as P

TY = 16
TZ = 128
ITERS = 4


smoothing = 0.02
damping = 0.1
stencil_diag = 42.0


def padded_2(cells, sides, width):
    for axis, dim in sides:
        count = lax.axis_size(axis)
        ends = count - 1
        head = lax.slice_in_dim(cells, 0, width, axis=dim)
        tail = lax.slice_in_dim(cells, cells.shape[dim] - width, cells.shape[dim], axis=dim)
        cells = jnp.concatenate(
            [
                lax.ppermute(tail, axis, [(i, (i + 1) % count) for i in range(ends)]),
                cells,
                lax.ppermute(head, axis, [((i + 1) % count, i) for i in range(ends)]),
            ],
            axis=dim,
        )
    return cells


def weights(offset, fraction, length):
    inside = jnp.arange(length, dtype=jnp.int32)[None, :, None]
    source = jnp.arange(2 * length, dtype=jnp.int32)[None, None, :]
    anchor = offset[:, None, None] + inside
    portion = fraction[:, None, None]
    table = jnp.where(source == anchor, 1.0 - portion, 0.0) + jnp.where(
        source == anchor + 1, portion, 0.0
    )
    return table.astype(jnp.bfloat16)


def assemble(arrived, corner):
    count = corner.shape[0]
    depth, height, width = (arrived.shape[1], arrived.shape[2], arrived.shape[3])
    picked = jnp.take(arrived, corner.reshape(-1), axis=0)
    picked = picked.reshape(count, 2, 2, 2, depth, height, width).transpose(0, 1, 4, 2, 5, 3, 6)
    return picked.reshape(count, 2 * depth, 2 * height, 2 * width)


def interpolate(patch, shift_x, shift_y, shift_z, fraction):
    depth = patch.shape[1] // 2
    height = patch.shape[2] // 2
    width = patch.shape[3] // 2
    weight_z = weights(shift_z, fraction[:, 2], width)
    weight_y = weights(shift_y, fraction[:, 1], height)
    weight_x = weights(shift_x, fraction[:, 0], depth)
    first = jnp.einsum(
        "tabk,tzk->tabz", patch, weight_z, preferred_element_type=jnp.float32
    ).astype(jnp.bfloat16)
    second = jnp.einsum(
        "tabz,tyb->tayz", first, weight_y, preferred_element_type=jnp.float32
    ).astype(jnp.bfloat16)
    return jnp.einsum("tayz,txa->txyz", second, weight_x, preferred_element_type=jnp.float32)


def laplace_core(padded):
    full = jnp.pad(padded, ((0, 0), (0, 0), (0, 0), (1, 1)))
    centre = full[:, 1:-1, 1:-1, 1:-1]
    beside = full[:, 2:, 1:-1, 1:-1] + full[:, :-2, 1:-1, 1:-1]
    beside = beside + full[:, 1:-1, 2:, 1:-1] + full[:, 1:-1, :-2, 1:-1]
    beside = beside + full[:, 1:-1, 1:-1, 2:] + full[:, 1:-1, 1:-1, :-2]
    return 6.0 * centre - beside


def bilaplace(field):
    first = laplace_core(padded_2(field, (("slab", 1), ("row", 2)), 1))
    return laplace_core(padded_2(first, (("slab", 1), ("row", 2)), 1))


def squares(residual, prepared):
    return lax.psum(jnp.sum(residual * prepared), ("slab", "row"))


def per_device(moving, fixed, requests, footpoints, offset_x, offset_y, offset_z, fractions):
    depth, height, width = moving.shape
    across = height // TY
    along = width // TZ
    tile_set = moving.reshape(depth, across, TY, along, TZ).transpose(1, 3, 0, 2, 4)
    tile_set = tile_set.reshape(across * along, depth, TY, TZ)
    asked = lax.all_to_all(requests[0, 0], ("slab", "row"), split_axis=0, concat_axis=0, tiled=True)
    peer_count, slots = (asked.shape[0], asked.shape[1])
    picked = jnp.take(tile_set, jnp.maximum(asked, 0).reshape(-1), axis=0)
    picked = picked.reshape(peer_count, slots, depth, TY, TZ)
    outgoing = jnp.where((asked >= 0)[:, :, None, None, None], picked, jnp.zeros_like(picked))
    arrived = lax.all_to_all(outgoing, ("slab", "row"), split_axis=0, concat_axis=0, tiled=True)
    arrived = arrived.reshape(peer_count * slots, depth, TY, TZ)
    patch = assemble(arrived, footpoints[0, 0])
    warped_tiles = interpolate(
        patch, offset_x[0, 0], offset_y[0, 0], offset_z[0, 0], fractions[0, 0]
    )
    warped = (
        warped_tiles.reshape(across, along, depth, TY, TZ)
        .transpose(2, 0, 3, 1, 4)
        .reshape(depth, height, width)
    )
    rimmed = padded_2(warped, (("slab", 0), ("row", 1)), 1)
    rimmed = jnp.pad(rimmed, ((0, 0), (0, 0), (1, 1)))
    slope = jnp.stack(
        [
            (rimmed[2:, 1:-1, 1:-1] - rimmed[:-2, 1:-1, 1:-1]) * 0.5,
            (rimmed[1:-1, 2:, 1:-1] - rimmed[1:-1, :-2, 1:-1]) * 0.5,
            (rimmed[1:-1, 1:-1, 2:] - rimmed[1:-1, 1:-1, :-2]) * 0.5,
        ]
    )
    rhs = -slope * (warped - fixed)[None]
    precond = slope * slope + stencil_diag * smoothing + damping
    solution = jnp.zeros_like(rhs)
    residual = rhs
    prepared = residual / precond
    direction = prepared
    norm_now = squares(residual, prepared)
    for step in range(ITERS):
        image = (
            slope * jnp.sum(slope * direction, axis=0)[None]
            + smoothing * bilaplace(direction)
            + damping * direction
        )
        alpha = norm_now / lax.psum(jnp.sum(direction * image), ("slab", "row"))
        solution = solution + alpha * direction
        residual = residual - alpha * image
        prepared = residual / precond
        norm_next = squares(residual, prepared)
        direction = prepared + norm_next / norm_now * direction
        norm_now = norm_next
    return (solution, residual)


def solution(mesh):
    return jax.shard_map(
        per_device,
        mesh=mesh,
        in_specs=(
            P("slab", "row", None),
            P("slab", "row", None),
            P("slab", "row", None, None),
            P("slab", "row", None, None),
            P("slab", "row", None),
            P("slab", "row", None),
            P("slab", "row", None),
            P("slab", "row", None, None),
        ),
        out_specs=(P(None, "slab", "row", None), P(None, "slab", "row", None)),
        check_vma=False,
    )
```

profile of v0, /device:TPU:1, one launch (start us, length us, event | category | flops | bytes accessed | tf_op | source)
XLA Modules:
  0.0 811.6 jit_solution(12415856314955365225)
XLA Ops:
  2.0 11.5 %all-to-all-start = ((s32[128,1,2]{2,1,0:T(1,128)}), s32[128,1,2]{2,1,0:T(1,128)S(1)}, u32[]{:S(2)}, u32[]{:S(2)}) async-start(s32[128,1,2]{2,1,0:T(1,128)} %bitcast.9), calls=%async_computation | async-start | bytes 131072 | tf_op jit(solution)/shard_map/all_to_all | solution.py:92
  14.6 8.4 %all-to-all-done = s32[128,1,2]{2,1,0:T(1,128)S(1)} async-done(((s32[128,1,2]{2,1,0:T(1,128)}), s32[128,1,2]{2,1,0:T(1,128)S(1)}, u32[]{:S(2)}, u32[]{:S(2)}) %all-to-all-start) | async-done | bytes 1056 | tf_op jit(solution)/shard_map/all_to_all | solution.py:92
  27.0 4.6 all-to-all-start.1
  32.3 29.2 %all-to-all-done.1 = bf16[128,2,2,16,128]{4,3,2,1,0:T(8,128)(2,1)S(1)} async-done(((bf16[128,2,2,16,128]{4,3,2,1,0:T(8,128)(2,1)}), bf16[128,2,2,16,128]{4,3,2,1,0:T(8,128)(2,1)S(1)}, u32[]{:S(2)}, u32[]{:S(2)}) %all-to-all-start.1) | async-done | bytes 2097184 | tf_op jit(solution)/shard_map/all_to_all | solution.py:97
  81.2 4.7 collective-permute-done
  99.8 7.0 collective-permute-done.5
  106.8 4.4 collective-permute-done.4
  125.8 7.0 collective-permute-done.9
  132.8 4.4 collective-permute-done.8
  137.3 6.0 collective-permute-start.11
  152.3 66.5 %all-reduce.9 = (f32[]{:T(128)}, f32[]{:T(128)}) all-reduce(f32[]{:T(128)} %get-tuple-element.3, f32[]{:T(128)} %get-tuple-element.2), channel_id=1, replica_groups=mesh['slab'=8,'row'=16] {'slab','row'}, use_global_device_ids=true, to_apply=%region_1.2 | all-reduce | flops 2 | bytes 16 | tf_op jit(solution)/shard_map/psum | solution.py:83
  222.2 62.6 %psum.58 = f32[]{:T(128)} all-reduce(f32[]{:T(128)} %multiply_reduce_fusion.8), channel_id=1, replica_groups=mesh['slab'=8,'row'=16] {'slab','row'}, use_global_device_ids=true, to_apply=%region_6.7 | all-reduce | flops 1 | bytes 8 | tf_op jit(solution)/shard_map/psum | solution.py:83
  294.0 7.0 collective-permute-done.13
  301.0 4.4 collective-permute-done.12
  319.4 7.0 collective-permute-done.17
  326.4 4.7 collective-permute-done.16
  331.2 3.7 collective-permute-start.19
  344.6 66.6 %psum.59 = f32[]{:T(128)} all-reduce(f32[]{:T(128)} %get-tuple-element.16), channel_id=1, replica_groups=mesh['slab'=8,'row'=16] {'slab','row'}, use_global_device_ids=true, to_apply=%region_9.10 | all-reduce | flops 1 | bytes 8 | tf_op jit(solution)/shard_map/psum | solution.py:130
  415.7 63.6 %psum.60 = f32[]{:T(128)} all-reduce(f32[]{:T(128)} %multiply_reduce_fusion.5), channel_id=1, replica_groups=mesh['slab'=8,'row'=16] {'slab','row'}, use_global_device_ids=true, to_apply=%region_11.12 | all-reduce | flops 1 | bytes 8 | tf_op jit(solution)/shard_map/psum | solution.py:83
  489.0 7.0 collective-permute-done.21
  495.9 4.4 collective-permute-done.20
  515.5 7.0 collective-permute-done.25
  522.5 4.4 collective-permute-done.24
  539.6 67.7 %psum.61 = f32[]{:T(128)} all-reduce(f32[]{:T(128)} %get-tuple-element.12), channel_id=1, replica_groups=mesh['slab'=8,'row'=16] {'slab','row'}, use_global_device_ids=true, to_apply=%region_14.15 | all-reduce | flops 1 | bytes 8 | tf_op jit(solution)/shard_map/psum | solution.py:130
  608.5 5.7 multiply_reduce_fusion.2
  614.1 62.9 %psum.62 = f32[]{:T(128)} all-reduce(f32[]{:T(128)} %get-tuple-element.10), channel_id=1, replica_groups=mesh['slab'=8,'row'=16] {'slab','row'}, use_global_device_ids=true, to_apply=%region_16.17 | all-reduce | flops 1 | bytes 8 | tf_op jit(solution)/shard_map/psum | solution.py:83
  686.2 7.0 collective-permute-done.29
  693.2 4.4 collective-permute-done.28
  712.1 7.0 collective-permute-done.33
  719.1 4.7 collective-permute-done.32
  736.9 67.4 %psum.63 = f32[]{:T(128)} all-reduce(f32[]{:T(128)} %get-tuple-element.6), channel_id=1, replica_groups=mesh['slab'=8,'row'=16] {'slab','row'}, use_global_device_ids=true, to_apply=%region_19.20 | all-reduce | flops 1 | bytes 8 | tf_op jit(solution)/shard_map/psum | solution.py:130
  805.6 4.1 multiply_add_fusion
  (176 shorter events, 173.9 us)
Async XLA Ops:
  2.0 21.0 %all-to-all-start = ((s32[128,1,2]{2,1,0:T(1,128)}), s32[128,1,2]{2,1,0:T(1,128)S(1)}, u32[]{:S(2)}, u32[]{:S(2)}) async-start(s32[128,1,2]{2,1,0:T(1,128)} %bitcast.9), calls=%async_computation | async-start | bytes 131072 | tf_op jit(solution)/shard_map/all_to_all | solution.py:92
  27.0 34.5 %all-to-all-start.1 = ((bf16[128,2,2,16,128]{4,3,2,1,0:T(8,128)(2,1)}), bf16[128,2,2,16,128]{4,3,2,1,0:T(8,128)(2,1)S(1)}, u32[]{:S(2)}, u32[]{:S(2)}) async-start(bf16[128,2,2,16,128]{4,3,2,1,0:T(8,128)(2,1)} %select_select_fusion), calls=%async_computation.1 | async-start | bytes 4194304 | tf_op jit(solution)/shard_map/all_to_all | solution.py:97
  74.6 6.7 collective-permute-start.1
  78.1 7.8 collective-permute-start
  88.8 4.5 collective-permute-start.2
  94.7 12.1 %collective-permute-start.5 = (f32[3,1,64,1024]{3,2,1,0:T(8,128)S(1)}, f32[3,1,64,1024]{3,2,1,0:T(8,128)S(1)}, u32[]{:S(2)}, u32[]{:S(2)}) collective-permute-start(f32[3,1,64,1024]{3,2,1,0:T(8,128)S(1)} %get-tuple-element.53), channel_id=1, source_target_pairs={{0,16},{16,32},{32,48},{48,64},{64,80},{80,96},{96,112},{1,17},{17... | collective-permute-start | bytes 2359304 | tf_op jit(solution)/shard_map/ppermute | solution.py:24
  97.9 13.3 %collective-permute-start.4 = (f32[3,1,64,1024]{3,2,1,0:T(8,128)S(1)}, f32[3,1,64,1024]{3,2,1,0:T(8,128)S(1)}, u32[]{:S(2)}, u32[]{:S(2)}) collective-permute-start(f32[3,1,64,1024]{3,2,1,0:T(8,128)S(1)} %get-tuple-element.54), channel_id=1, source_target_pairs={{16,0},{32,16},{48,32},{64,48},{80,64},{96,80},{112,96},{17,1},{33... | collective-permute-start | bytes 2359304 | tf_op jit(solution)/shard_map/ppermute | solution.py:26
  112.9 4.8 collective-permute-start.6
  120.7 12.1 %collective-permute-start.9 = (f32[3,1,64,1024]{3,2,1,0:T(8,128)S(1)}, f32[3,1,64,1024]{3,2,1,0:T(8,128)S(1)}, u32[]{:S(2)}, u32[]{:S(2)}) collective-permute-start(f32[3,1,64,1024]{3,2,1,0:T(8,128)S(1)} %get-tuple-element.51), channel_id=1, source_target_pairs={{0,16},{16,32},{32,48},{48,64},{64,80},{80,96},{96,112},{1,17},{17... | collective-permute-start | bytes 2359304 | tf_op jit(solution)/shard_map/ppermute | solution.py:24
  123.9 13.3 %collective-permute-start.8 = (f32[3,1,64,1024]{3,2,1,0:T(8,128)S(1)}, f32[3,1,64,1024]{3,2,1,0:T(8,128)S(1)}, u32[]{:S(2)}, u32[]{:S(2)}) collective-permute-start(f32[3,1,64,1024]{3,2,1,0:T(8,128)S(1)} %get-tuple-element.52), channel_id=1, source_target_pairs={{16,0},{32,16},{48,32},{64,48},{80,64},{96,80},{112,96},{17,1},{33... | collective-permute-start | bytes 2359304 | tf_op jit(solution)/shard_map/ppermute | solution.py:26
  137.3 7.3 collective-permute-start.11
  143.3 4.8 collective-permute-start.10
  288.5 12.5 %collective-permute-start.13 = (f32[3,1,64,1024]{3,2,1,0:T(8,128)S(1)}, f32[3,1,64,1024]{3,2,1,0:T(8,128)S(1)}, u32[]{:S(2)}, u32[]{:S(2)}) collective-permute-start(f32[3,1,64,1024]{3,2,1,0:T(8,128)S(1)} %get-tuple-element.49), channel_id=1, source_target_pairs={{0,16},{16,32},{32,48},{48,64},{64,80},{80,96},{96,112},{1,17},{17... | collective-permute-start | bytes 2359304 | tf_op jit(solution)/shard_map/ppermute | solution.py:24
  292.1 13.3 %collective-permute-start.12 = (f32[3,1,64,1024]{3,2,1,0:T(8,128)S(1)}, f32[3,1,64,1024]{3,2,1,0:T(8,128)S(1)}, u32[]{:S(2)}, u32[]{:S(2)}) collective-permute-start(f32[3,1,64,1024]{3,2,1,0:T(8,128)S(1)} %get-tuple-element.50), channel_id=1, source_target_pairs={{16,0},{32,16},{48,32},{64,48},{80,64},{96,80},{112,96},{17,1},{33... | collective-permute-start | bytes 2359304 | tf_op jit(solution)/shard_map/ppermute | solution.py:26
  306.8 4.9 collective-permute-start.14
  314.6 11.8 %collective-permute-start.17 = (f32[3,1,64,1024]{3,2,1,0:T(8,128)S(1)}, f32[3,1,64,1024]{3,2,1,0:T(8,128)S(1)}, u32[]{:S(2)}, u32[]{:S(2)}) collective-permute-start(f32[3,1,64,1024]{3,2,1,0:T(8,128)S(1)} %get-tuple-element.47), channel_id=1, source_target_pairs={{0,16},{16,32},{32,48},{48,64},{64,80},{80,96},{96,112},{1,17},{17... | collective-permute-start | bytes 2359304 | tf_op jit(solution)/shard_map/ppermute | solution.py:24
  317.5 13.6 %collective-permute-start.16 = (f32[3,1,64,1024]{3,2,1,0:T(8,128)S(1)}, f32[3,1,64,1024]{3,2,1,0:T(8,128)S(1)}, u32[]{:S(2)}, u32[]{:S(2)}) collective-permute-start(f32[3,1,64,1024]{3,2,1,0:T(8,128)S(1)} %get-tuple-element.48), channel_id=1, source_target_pairs={{16,0},{32,16},{48,32},{64,48},{80,64},{96,80},{112,96},{17,1},{33... | collective-permute-start | bytes 2359304 | tf_op jit(solution)/shard_map/ppermute | solution.py:26
  331.2 5.1 collective-permute-start.19
  334.9 4.8 collective-permute-start.18
  484.1 11.9 %collective-permute-start.21 = (f32[3,1,64,1024]{3,2,1,0:T(8,128)S(1)}, f32[3,1,64,1024]{3,2,1,0:T(8,128)S(1)}, u32[]{:S(2)}, u32[]{:S(2)}) collective-permute-start(f32[3,1,64,1024]{3,2,1,0:T(8,128)S(1)} %get-tuple-element.45), channel_id=1, source_target_pairs={{0,16},{16,32},{32,48},{48,64},{64,80},{80,96},{96,112},{1,17},{17... | collective-permute-start | bytes 2359304 | tf_op jit(solution)/shard_map/ppermute | solution.py:24
  487.0 13.3 %collective-permute-start.20 = (f32[3,1,64,1024]{3,2,1,0:T(8,128)S(1)}, f32[3,1,64,1024]{3,2,1,0:T(8,128)S(1)}, u32[]{:S(2)}, u32[]{:S(2)}) collective-permute-start(f32[3,1,64,1024]{3,2,1,0:T(8,128)S(1)} %get-tuple-element.46), channel_id=1, source_target_pairs={{16,0},{32,16},{48,32},{64,48},{80,64},{96,80},{112,96},{17,1},{33... | collective-permute-start | bytes 2359304 | tf_op jit(solution)/shard_map/ppermute | solution.py:26
  502.1 4.8 collective-permute-start.22
  509.9 12.6 %collective-permute-start.25 = (f32[3,1,64,1024]{3,2,1,0:T(8,128)S(1)}, f32[3,1,64,1024]{3,2,1,0:T(8,128)S(1)}, u32[]{:S(2)}, u32[]{:S(2)}) collective-permute-start(f32[3,1,64,1024]{3,2,1,0:T(8,128)S(1)} %get-tuple-element.43), channel_id=1, source_target_pairs={{0,16},{16,32},{32,48},{48,64},{64,80},{80,96},{96,112},{1,17},{17... | collective-permute-start | bytes 2359304 | tf_op jit(solution)/shard_map/ppermute | solution.py:24
  513.6 13.3 %collective-permute-start.24 = (f32[3,1,64,1024]{3,2,1,0:T(8,128)S(1)}, f32[3,1,64,1024]{3,2,1,0:T(8,128)S(1)}, u32[]{:S(2)}, u32[]{:S(2)}) collective-permute-start(f32[3,1,64,1024]{3,2,1,0:T(8,128)S(1)} %get-tuple-element.44), channel_id=1, source_target_pairs={{16,0},{32,16},{48,32},{64,48},{80,64},{96,80},{112,96},{17,1},{33... | collective-permute-start | bytes 2359304 | tf_op jit(solution)/shard_map/ppermute | solution.py:26
  529.7 5.0 collective-permute-start.26
  681.0 12.2 %collective-permute-start.29 = (f32[3,1,64,1024]{3,2,1,0:T(8,128)S(1)}, f32[3,1,64,1024]{3,2,1,0:T(8,128)S(1)}, u32[]{:S(2)}, u32[]{:S(2)}) collective-permute-start(f32[3,1,64,1024]{3,2,1,0:T(8,128)S(1)} %get-tuple-element.41), channel_id=1, source_target_pairs={{0,16},{16,32},{32,48},{48,64},{64,80},{80,96},{96,112},{1,17},{17... | collective-permute-start | bytes 2359304 | tf_op jit(solution)/shard_map/ppermute | solution.py:24
  684.3 13.3 %collective-permute-start.28 = (f32[3,1,64,1024]{3,2,1,0:T(8,128)S(1)}, f32[3,1,64,1024]{3,2,1,0:T(8,128)S(1)}, u32[]{:S(2)}, u32[]{:S(2)}) collective-permute-start(f32[3,1,64,1024]{3,2,1,0:T(8,128)S(1)} %get-tuple-element.42), channel_id=1, source_target_pairs={{16,0},{32,16},{48,32},{64,48},{80,64},{96,80},{112,96},{17,1},{33... | collective-permute-start | bytes 2359304 | tf_op jit(solution)/shard_map/ppermute | solution.py:26
  699.2 4.8 collective-permute-start.30
  707.1 11.9 %collective-permute-start.33 = (f32[3,1,64,1024]{3,2,1,0:T(8,128)S(1)}, f32[3,1,64,1024]{3,2,1,0:T(8,128)S(1)}, u32[]{:S(2)}, u32[]{:S(2)}) collective-permute-start(f32[3,1,64,1024]{3,2,1,0:T(8,128)S(1)} %get-tuple-element.39), channel_id=1, source_target_pairs={{0,16},{16,32},{32,48},{48,64},{64,80},{80,96},{96,112},{1,17},{17... | collective-permute-start | bytes 2359304 | tf_op jit(solution)/shard_map/ppermute | solution.py:24
  710.1 13.6 %collective-permute-start.32 = (f32[3,1,64,1024]{3,2,1,0:T(8,128)S(1)}, f32[3,1,64,1024]{3,2,1,0:T(8,128)S(1)}, u32[]{:S(2)}, u32[]{:S(2)}) collective-permute-start(f32[3,1,64,1024]{3,2,1,0:T(8,128)S(1)} %get-tuple-element.40), channel_id=1, source_target_pairs={{16,0},{32,16},{48,32},{64,48},{80,64},{96,80},{112,96},{17,1},{33... | collective-permute-start | bytes 2359304 | tf_op jit(solution)/shard_map/ppermute | solution.py:26
  723.8 4.7 collective-permute-start.35
  727.1 5.0 collective-permute-start.34
  (26 other events, 1250.0 us)
where the time goes:
time: 822 us; the launch traced here: 812 us
  blocking collectives  457 us (56%)
  waiting for transfers between devices  165 us (20%)
  starting transfers between devices  99.8 us (12%)
  other arithmetic  61.2 us (7%)
  local copies, waits for them, and re-layouts  13.8 us (2%)
  between operations  10.9 us (1%)
    psum x4, blocking collectives, squares(): return lax.psum(jnp.sum(residual * prepared), ('slab', 'row'))  256 us
    psum x3, blocking collectives, per_device(): alpha = norm_now / lax.psum(jnp.sum(direction * image), ('slab', 'row'))  202 us
    ppermute x18, waiting for transfers between devices, padded_2(): lax.ppermute(head, axis, [((i + 1) % count, i) for i in range(ends)])  70.7 us
    ppermute x18, waiting for transfers between devices, padded_2(): lax.ppermute(tail, axis, [(i, (i + 1) % count) for i in range(ends)])  56.6 us
    ppermute x18, starting transfers between devices, padded_2(): lax.ppermute(tail, axis, [(i, (i + 1) % count) for i in range(ends)])  53.3 us
    ppermute x18, starting transfers between devices, padded_2(): lax.ppermute(head, axis, [((i + 1) % count, i) for i in range(ends)])  30.4 us
    all_to_all x1, waiting for transfers between devices, per_device(): lax.all_to_all(outgoing, ('slab', 'row'), split_axis=0, concat_axis=0, ti...  29.2 us
  transfers between devices with their start and end apart: 38, of which 29 were waited for; matrix products, arithmetic and copies ran while one was open for 0% of the time, Pallas kernels for 0%

commit v1 on v0

v1 whole, which is shorter than its diff:
```python
import functools

import jax
import jax.numpy as jnp
from jax import lax
from jax.experimental import pallas as pl
from jax.experimental.pallas import tpu as pltpu
from jax.sharding import PartitionSpec as P

TY = 16
TZ = 128
ITERS = 4

smoothing = 0.02
damping = 0.1
stencil_diag = 42.0

LOW = 0.1
HIGH = 3.2
CENTRE = (HIGH + LOW) / 2
HALF = (HIGH - LOW) / 2

BOTH = ("slab", "row")
F32 = jnp.float32
BF16 = jnp.bfloat16


def spread(width):
    source = lax.broadcasted_iota(jnp.int32, (width, width), 0)
    target = lax.broadcasted_iota(jnp.int32, (width, width), 1)
    return (target == (source % 8) * (width // 8) + source // 8).astype(BF16)


def warp_kernel(foot, ox, oy, oz, wts, arrived, fixed, perm, out, nat):
    base_z = lax.broadcasted_iota(jnp.int32, (256, 128), 0) - lax.broadcasted_iota(jnp.int32, (256, 128), 1)
    ro = lax.broadcasted_iota(jnp.int32, (64, 128), 0)
    ci = lax.broadcasted_iota(jnp.int32, (64, 128), 1)
    same = (ro // 32 == ci // 64) & ((ro // 16) % 2 == (ci // 16) % 2)
    base_y = jnp.where(same, ((ci // 32) % 2) * 16 + ci % 16 - ro % 16, -1000)

    def band(base, shift, here, after):
        return jnp.where(base == shift, here, jnp.where(base == shift + 1, after, 0.0)).astype(BF16)

    def tile_row(j, carry):
        for k in range(8):
            t = j * 8 + k
            sides = []
            for c in range(2):
                sides.append(
                    jnp.concatenate(
                        [arrived[foot[t * 8 + 4 * a + 2 * b + c]] for a in range(2) for b in range(2)], axis=0
                    )
                )
            patch = jnp.concatenate(sides, axis=1)
            wz = band(base_z, oz[t], wts[t * 6 + 4], wts[t * 6 + 5])
            first = jnp.dot(patch, wz, preferred_element_type=F32).astype(BF16)
            wy = band(base_y, oy[t], wts[t * 6 + 2], wts[t * 6 + 3])
            second = jnp.dot(wy, first, preferred_element_type=F32).astype(BF16).astype(F32)
            shift = ox[t]
            for xo in range(2):
                total = None
                for p in range(xo, xo + 3):
                    weight = jnp.where(
                        p - xo == shift, wts[t * 6], jnp.where(p - xo == shift + 1, wts[t * 6 + 1], 0.0)
                    )
                    term = weight * second[p * 16 : (p + 1) * 16]
                    total = term if total is None else total + term
                rows = pl.ds(pl.multiple_of(j * 16, 16), 16)
                lanes = slice(k * 128, (k + 1) * 128)
                nat[xo, rows, lanes] = total.astype(BF16)
                nat[2 + xo, rows, lanes] = (total - fixed[xo, rows, lanes]).astype(BF16)
        return carry

    lax.fori_loop(0, 4, tile_row, 0)
    mixed = jnp.dot(nat[...].reshape(256, 1024), perm[...], preferred_element_type=F32)
    out[...] = mixed.astype(BF16).reshape(4, 64, 1024)


def warp(arrived, footpoints, offset_x, offset_y, offset_z, fractions, fixed, perm):
    near = lax.reduce_precision(1.0 - fractions, 8, 7)
    far = lax.reduce_precision(fractions, 8, 7)
    wts = jnp.stack([near, far], axis=-1).reshape(-1)
    smem = pl.BlockSpec(memory_space=pltpu.SMEM)
    vmem = pl.BlockSpec(memory_space=pltpu.VMEM)
    return pl.pallas_call(
        warp_kernel,
        out_shape=jax.ShapeDtypeStruct((4, 64, 1024), BF16),
        in_specs=[smem] * 5 + [vmem] * 3,
        out_specs=vmem,
        scratch_shapes=[pltpu.VMEM((4, 64, 1024), BF16)],
        compiler_params=pltpu.CompilerParams(vmem_limit_bytes=32 * 1024 * 1024),
        name="warp",
    )(footpoints.reshape(-1), offset_x, offset_y, offset_z, wts, arrived, fixed, perm)


def edge_masks():
    sub = lax.broadcasted_iota(jnp.int32, (1, 8, 128), 1)
    lane = lax.broadcasted_iota(jnp.int32, (1, 8, 128), 2)
    one = lambda flag: jnp.where(flag, 1.0, 0.0).astype(F32)
    return one(sub != 0), one(sub != 7), one(lane != 0), one(lane != 127)


def x_pair(v0, v1, masks):
    return pltpu.roll(v1, 1, 1) * masks[0], pltpu.roll(v0, 7, 1) * masks[1]


def z_pair(v, masks):
    before = jnp.concatenate([pltpu.roll(v[7:8], 1, 2) * masks[2], v[:7]], axis=0)
    after = jnp.concatenate([v[1:], pltpu.roll(v[:1], 127, 2) * masks[3]], axis=0)
    return before, after


def beside(v0, v1, masks):
    before, after = x_pair(v0, v1, masks)
    a0, b0 = z_pair(v0, masks)
    a1, b1 = z_pair(v1, masks)
    return (v1 + before) + (a0 + b0), (v0 + after) + (a1 + b1)


K_LO = slice(0, 8)
K_HI = slice(8, 16)


def krylov_kernel(rowmask, arr, mom, vout, sout, d_s, w_s, s_s, im_s, u_s, v0, v1, v2, v3, v4, sems):
    vs = [v0, v1, v2, v3, v4]
    masks = edge_masks()
    for src in range(8):
        lines = arr[src].astype(F32).reshape(104, 1024)
        for kz in range(8):
            d_s[kz, src * 104 : (src + 1) * 104, :] = lines[:, kz * 128 : (kz + 1) * 128]

    def fetch(row):
        return [d_s[kz, pl.ds(row, 8, stride=104), :] for kz in range(8)]

    def put_w(i, row0, row1):
        for kx, row in ((0, row0), (1, row1)):
            for kz, vreg in enumerate(fetch(row)):
                w_s[i, kx * 8 + kz] = vreg

    put_w(0, 96, 98)
    put_w(25, 97, 99)

    def fill(n, carry):
        put_w(n + 1, 48 + n, 72 + n)
        return carry

    lax.fori_loop(0, 24, fill, 0)

    def begin(n, carry):
        w0, w1 = w_s[n + 1, K_LO], w_s[n + 1, K_HI]
        before, after = x_pair(w0, w1, masks)
        keep = rowmask[n]
        for kx, w, xs in ((0, w0, w1 - before), (1, w1, after - w0)):
            part = slice(kx * 8, kx * 8 + 8)
            diff = jnp.stack(fetch(n + 24 * kx))
            zb, za = z_pair(w, masks)
            ys = w_s[n + 2, part] - w_s[n, part]
            for c, s in enumerate((xs * 0.5, ys * 0.5, (za - zb) * 0.5)):
                im = keep / (s * s + (stencil_diag * smoothing + damping))
                s_s[c, n, part] = s
                im_s[c, n, part] = im
                v0[c, n, part] = -s * diff * im
        return carry

    lax.fori_loop(0, 24, begin, 0)

    def copy(j):
        return pltpu.make_async_copy(vs[j].at[:, pl.ds(8 - 2 * j, 8)], vout.at[j], sems.at[j])

    s_copy = pltpu.make_async_copy(s_s.at[:, pl.ds(8, 8)], sout, sems.at[5])
    s_copy.start()
    copy(0).start()

    for j in range(4):
        gain = (1.0 if j == 0 else 2.0) / HALF
        old, new = vs[j], vs[j + 1]
        off = 2 * j

        def first(n, carry):
            scale = rowmask[n] * (gain * smoothing)
            for c in range(3):
                a0, a1 = old[c, n - off, K_LO], old[c, n - off, K_HI]
                b0, b1 = beside(a0, a1, masks)
                for part, a, b in ((K_LO, a0, b0), (K_HI, a1, b1)):
                    total = b + (old[c, n - off - 1, part] + old[c, n - off + 1, part])
                    u_s[c, n - 1, part] = (6.0 * a - total) * scale
            return carry

        lax.fori_loop(off + 1, 23 - off, first, 0)

        def second(n, carry):
            dots = []
            for part in (K_LO, K_HI):
                dot = s_s[0, n, part] * old[0, n - off, part]
                dot = dot + s_s[1, n, part] * old[1, n - off, part]
                dots.append((dot + s_s[2, n, part] * old[2, n - off, part]) * gain)
            for c in range(3):
                a0, a1 = u_s[c, n - 1, K_LO], u_s[c, n - 1, K_HI]
                b0, b1 = beside(a0, a1, masks)
                for part, a, b, dot in ((K_LO, a0, b0, dots[0]), (K_HI, a1, b1, dots[1])):
                    total = b + (u_s[c, n - 2, part] + u_s[c, n, part])
                    v = old[c, n - off, part]
                    image = s_s[c, n, part] * dot + (6.0 * a - total) + (gain * damping) * v
                    value = im_s[c, n, part] * image - (gain * CENTRE) * v
                    if j > 0:
                        value = value - vs[j - 1][c, n - off + 2, part]
                    new[c, n - off - 2, part] = value
            return carry

        lax.fori_loop(off + 2, 22 - off, second, 0)
        copy(j + 1).start()

    def products(n, sums):
        sums = list(sums)
        for c in range(3):
            for part in (K_LO, K_HI):
                s = s_s[c, n, part]
                m = s * s + (stencil_diag * smoothing + damping)
                v = [vs[j][c, n - 2 * j, part] for j in range(5)]
                for j in range(4):
                    t = m * v[j]
                    for k, other in ((2 * j, v[j]), (2 * j + 1, v[j + 1])):
                        sums[k] = sums[k] + jnp.sum(t * other, axis=0)
        return tuple(sums)

    sums = lax.fori_loop(8, 16, products, tuple(jnp.zeros((8, 128), F32) for _ in range(8)))
    lane = lax.broadcasted_iota(jnp.int32, (1, 128), 1)
    line = jnp.zeros((1, 128), F32)
    for k in range(8):
        line = jnp.where(lane == k, jnp.sum(sums[k], keepdims=True), line)
    mom[...] = jnp.broadcast_to(line, mom.shape)
    s_copy.wait()
    for j in range(5):
        copy(j).wait()


def krylov(received, rowmask, peers):
    vmem = pl.BlockSpec(memory_space=pltpu.VMEM)
    hbm = pl.BlockSpec(memory_space=pl.ANY)

    def field(rows):
        return pltpu.VMEM((3, rows, 16, 8, 128), F32)

    return pl.pallas_call(
        krylov_kernel,
        out_shape=(
            jax.ShapeDtypeStruct((peers, 128), F32),
            jax.ShapeDtypeStruct((5, 3, 8, 16, 8, 128), F32),
            jax.ShapeDtypeStruct((3, 8, 16, 8, 128), F32),
        ),
        in_specs=[pl.BlockSpec(memory_space=pltpu.SMEM), vmem],
        out_specs=(vmem, hbm, hbm),
        scratch_shapes=[
            pltpu.VMEM((8, 832, 128), F32),
            pltpu.VMEM((26, 16, 8, 128), F32),
            field(24),
            field(24),
            field(22),
            field(24),
            field(20),
            field(16),
            field(12),
            field(8),
            pltpu.SemaphoreType.DMA((6,)),
        ],
        compiler_params=pltpu.CompilerParams(vmem_limit_bytes=50 * 1024 * 1024),
        name="krylov",
    )(rowmask, received)


def coefficients(m):
    def lam(k):
        if k == 0:
            return CENTRE * m[0] + HALF * m[1]
        return CENTRE * m[k] + (HALF / 2) * (m[k + 1] + m[k - 1])

    lams = [lam(k) for k in range(7)]
    rows = [[0.5 * (lams[i + j] + lams[abs(i - j)]) for j in range(4)] + [m[i]] for i in range(4)]
    for p in range(4):
        inverse = 1.0 / rows[p][p]
        for q in range(p + 1, 4):
            factor = rows[q][p] * inverse
            rows[q] = [rows[q][k] - factor * rows[p][k] if k > p else rows[q][k] for k in range(5)]
    part = [None] * 4
    for p in reversed(range(4)):
        value = rows[p][4]
        for q in range(p + 1, 4):
            value = value - rows[p][q] * part[q]
        part[p] = value / rows[p][p]
    rest = [1.0 - CENTRE * part[0] - (HALF / 2) * part[1]]
    rest.append(-CENTRE * part[1] - HALF * part[0] - (HALF / 2) * part[2])
    rest.append(-CENTRE * part[2] - (HALF / 2) * (part[1] + part[3]))
    rest.append(-CENTRE * part[3] - (HALF / 2) * part[2])
    rest.append(-(HALF / 2) * part[3])
    return part, rest


def combine_kernel(mom, v, s, out, turn):
    line = jnp.sum(mom[...], axis=0, keepdims=True)
    lane = lax.broadcasted_iota(jnp.int32, (1, 128), 1)
    p = [jnp.sum(jnp.where(lane == k, line, 0.0), axis=1, keepdims=True) for k in range(8)]
    m = [p[0], p[1]] + [2.0 * p[k] - p[k % 2] for k in range(2, 8)]
    part, rest = coefficients(m)
    part = [jnp.broadcast_to(x, (8, 128)) for x in part]
    rest = [jnp.broadcast_to(x, (8, 128)) for x in rest]

    def row(i, carry):
        for kx in range(2):
            at = pl.ds(pl.multiple_of((kx * 8 + i) * 8, 8), 8)
            for kz in range(8):
                k = kx * 8 + kz
                vecs = [v[j, 0, i, k] for j in range(5)]
                slope = s[0, i, k]
                weight = slope * slope + (stencil_diag * smoothing + damping)
                turn[0, kz, at, :] = sum(part[j] * vecs[j] for j in range(4))
                turn[1, kz, at, :] = weight * sum(rest[j] * vecs[j] for j in range(5))
        return carry

    lax.fori_loop(0, 8, row, 0)
    for q in range(2):
        for dest in range(8):
            for kz in range(8):
                lanes = slice(kz * 128, kz * 128 + 128)
                out[dest, q, 0, :, lanes] = turn[q, kz, pl.ds(dest, 16, stride=8), :].astype(BF16)


def combine(moments, vectors, slopes):
    peers = moments.shape[0]
    return pl.pallas_call(
        combine_kernel,
        grid=(3,),
        out_shape=jax.ShapeDtypeStruct((8, 2, 3, 16, 1024), BF16),
        in_specs=[
            pl.BlockSpec((peers, 128), lambda c: (0, 0)),
            pl.BlockSpec((5, 1, 8, 16, 8, 128), lambda c: (0, c, 0, 0, 0, 0)),
            pl.BlockSpec((1, 8, 16, 8, 128), lambda c: (c, 0, 0, 0, 0)),
        ],
        out_specs=pl.BlockSpec((8, 2, 1, 16, 1024), lambda c: (0, 0, c, 0, 0)),
        scratch_shapes=[pltpu.VMEM((2, 8, 128, 128), F32)],
        compiler_params=pltpu.CompilerParams(vmem_limit_bytes=32 * 1024 * 1024),
        name="combine",
    )(moments, vectors, slopes)


def finish_kernel(back, perm, sol, res):
    for q, out in ((0, sol), (1, res)):
        lines = jnp.concatenate([back[src, q, 0] for src in range(8)], axis=0)
        cells = lax.dot_general(lines, perm[...], (((1,), (1,)), ((), ())), preferred_element_type=F32)
        for src in range(8):
            for kx in range(2):
                out[0, kx, src * 8 : src * 8 + 8, :] = cells[src * 16 + kx * 8 : src * 16 + kx * 8 + 8]


def finish(back, perm):
    shape = jax.ShapeDtypeStruct((3, 2, 64, 1024), F32)
    spec = pl.BlockSpec((1, 2, 64, 1024), lambda c: (c, 0, 0, 0))
    return pl.pallas_call(
        finish_kernel,
        grid=(3,),
        out_shape=(shape, shape),
        in_specs=[
            pl.BlockSpec((8, 2, 1, 16, 1024), lambda c: (0, 0, c, 0, 0)),
            pl.BlockSpec((1024, 1024), lambda c: (0, 0)),
        ],
        out_specs=(spec, spec),
        compiler_params=pltpu.CompilerParams(vmem_limit_bytes=32 * 1024 * 1024),
        name="finish",
    )(back, perm)


def windows(own):
    count = lax.axis_size("row")
    down = [(i, i + 1) for i in range(count - 1)]
    up = [(i + 1, i) for i in range(count - 1)]
    top = lax.ppermute(own[:, 55:64], "row", down)
    bottom = lax.ppermute(own[:, 0:9], "row", up)
    whole = jnp.concatenate([top, own, bottom], axis=1)
    pieces = []
    for s in range(8):
        body = whole[:, 8 * s + 1 : 8 * s + 25]
        ends = jnp.stack([whole[0, 8 * s], whole[0, 8 * s + 25], whole[1, 8 * s], whole[1, 8 * s + 25]])
        ends = jnp.concatenate([ends, jnp.zeros_like(ends)])
        pieces.append(
            jnp.concatenate([body[2:4].reshape(48, 1024), body[0:2].reshape(48, 1024), ends]).reshape(13, 8, 1024)
        )
    return jnp.stack(pieces)


def per_device(moving, fixed, requests, footpoints, offset_x, offset_y, offset_z, fractions):
    depth, height, width = moving.shape
    across = height // TY
    along = width // TZ
    perm = spread(width)
    tile_set = moving.reshape(depth, across, TY, along, TZ).transpose(1, 3, 0, 2, 4)
    tile_set = tile_set.reshape(across * along, depth, TY, TZ)
    asked = lax.all_to_all(requests[0, 0], BOTH, split_axis=0, concat_axis=0, tiled=True)
    peers, slots = asked.shape
    picked = jnp.take(tile_set, jnp.maximum(asked, 0).reshape(-1), axis=0)
    picked = picked.reshape(peers, slots, depth, TY, TZ)
    outgoing = jnp.where((asked >= 0)[:, :, None, None, None], picked, jnp.zeros_like(picked))
    arrived = lax.all_to_all(outgoing, BOTH, split_axis=0, concat_axis=0, tiled=True)
    arrived = arrived.reshape(peers * slots, depth * TY, TZ)
    own = warp(
        arrived, footpoints[0, 0], offset_x[0, 0], offset_y[0, 0], offset_z[0, 0], fractions[0, 0], fixed, perm
    )
    received = lax.all_to_all(windows(own), "slab", split_axis=0, concat_axis=0, tiled=True)
    start = lax.axis_index("row") * height + lax.axis_index("slab") * 8 - 8
    rows = start + jnp.arange(24, dtype=jnp.int32)
    rowmask = ((rows >= 0) & (rows < height * lax.axis_size("row"))).astype(F32)
    moments, vectors, slopes = krylov(received, rowmask, peers)
    moments = lax.all_to_all(moments, BOTH, split_axis=0, concat_axis=0, tiled=True)
    back = combine(moments, vectors, slopes)
    back = lax.all_to_all(back, "slab", split_axis=0, concat_axis=0, tiled=True)
    return finish(back, perm)


def solution(mesh):
    return jax.shard_map(
        per_device,
        mesh=mesh,
        in_specs=(
            P("slab", "row", None),
            P("slab", "row", None),
            P("slab", "row", None, None),
            P("slab", "row", None, None),
            P("slab", "row", None),
            P("slab", "row", None),
            P("slab", "row", None),
            P("slab", "row", None, None),
        ),
        out_specs=(P(None, "slab", "row", None), P(None, "slab", "row", None)),
        check_vma=False,
    )
```

time: 822 us -> 197 us (0.24); the launches traced: 812 us -> 196 us
  blocking collectives: 457 us -> 41.7 us
  waiting for transfers between devices: 165 us -> 62 us
  starting transfers between devices: 99.8 us -> 27.7 us
  other arithmetic: 61.2 us -> 4.58 us
  Pallas kernels: 0 us -> 35.6 us
  between operations: 10.9 us -> 0.88 us
  local copies, waits for them, and re-layouts: 13.8 us -> 23.4 us
    psum x7 -> x0, blocking collectives: 457 us -> none  [the longest x4 256 us: squares(): return lax.psum(jnp.sum(residual * prepared), ('slab', 'row'))]
    ppermute x36 -> x2, waiting for transfers between devices: 127 us -> 3.79 us  [the longest x1 3.79 us: windows(): bottom = lax.ppermute(own[:, 0:9], 'row', up)]
    ppermute x36 -> x2, starting transfers between devices: 83.7 us -> 3.73 us  [the longest x1 2.45 us: windows(): top = lax.ppermute(own[:, 55:64], 'row', down)]
    all_to_all x0 -> x2, blocking collectives: none -> 41.7 us  [the longest x1 24.2 us: per_device(): back = lax.all_to_all(back, 'slab', split_axis=0, concat_axis=0, tiled=True)]
    pallas_call x0 -> x4, Pallas kernels: none -> 35.6 us  [the longest x1 19.1 us: krylov(): pl.pallas_call(krylov_kernel, out_shape=(jax.ShapeDtypeStruct((peers, 128...]
    reduce_sum x11 -> x0, other arithmetic: 32.1 us -> none  [the longest x4 12.4 us: per_device(): alpha = norm_now / lax.psum(jnp.sum(direction * image), ('slab', 'row'))]
    all_to_all x2 -> x3, waiting for transfers between devices: 37.6 us -> 58.3 us  [the longest x1 27.6 us: per_device(): lax.all_to_all(outgoing, BOTH, split_axis=0, concat_axis=0, tiled=True)]
    concatenate x17 -> x1, other arithmetic: 13.4 us -> 0.85 us  [windows(): whole = jnp.concatenate([top, own, bottom], axis=1)]
  transfers between devices with their start and end apart: 38 -> 5, of which waited for: 29 -> 4; matrix products, arithmetic and copies ran while one was open for 0% -> 2% of each run, Pallas kernels for 0% -> 0%
where the time goes in v1:
time: 197 us; the launch traced here: 196 us
  waiting for transfers between devices  62 us (31%)
  blocking collectives  41.7 us (21%)
  Pallas kernels  35.6 us (18%)
  starting transfers between devices  27.7 us (14%)
  local copies, waits for them, and re-layouts  23.4 us (12%)
  other arithmetic  4.58 us (2%)
    all_to_all x1, waiting for transfers between devices, per_device(): lax.all_to_all(outgoing, BOTH, split_axis=0, concat_axis=0, tiled=True)  27.6 us
    all_to_all x1, blocking collectives, per_device(): back = lax.all_to_all(back, 'slab', split_axis=0, concat_axis=0, tiled=True)  24.2 us
    all_to_all x1, waiting for transfers between devices, per_device(): lax.all_to_all(windows(own), 'slab', split_axis=0, concat_axis=0, tiled=T...  22.2 us
    pallas_call x1, Pallas kernels, krylov(): pl.pallas_call(krylov_kernel, out_shape=(jax.ShapeDtypeStruct((peers, 128...  19.1 us
    all_to_all x1, blocking collectives, per_device(): lax.all_to_all(moments, BOTH, split_axis=0, concat_axis=0, tiled=True)  17.5 us
    all_to_all x1, starting transfers between devices, per_device(): lax.all_to_all(requests[0, 0], BOTH, split_axis=0, concat_axis=0, tiled=T...  11.5 us
    unnamed x26, local copies, waits for them, and re-layouts  10.6 us
    all_to_all x1, waiting for transfers between devices, per_device(): lax.all_to_all(requests[0, 0], BOTH, split_axis=0, concat_axis=0, tiled=T...  8.45 us
  transfers between devices with their start and end apart: 5, of which 4 were waited for; matrix products, arithmetic and copies ran while one was open for 2% of the time, Pallas kernels for 0%

profile of v1, /device:TPU:1, one launch (start us, length us, event | category | flops | bytes accessed | tf_op | source)
XLA Modules:
  0.0 195.9 jit_solution(4069049192462779607)
XLA Ops:
  0.6 1.4 copy.39
  2.0 11.5 %all-to-all-start = ((s32[128,1,2]{2,1,0:T(1,128)}), s32[128,1,2]{2,1,0:T(1,128)S(1)}, u32[]{:S(2)}, u32[]{:S(2)}) async-start(s32[128,1,2]{2,1,0:T(1,128)} %bitcast.5), calls=%async_computation | async-start | bytes 131072 | tf_op jit(solution)/shard_map/all_to_all | solution.py:396
  13.5 1.0 copy.47
  14.6 8.4 %all-to-all-done = s32[128,1,2]{2,1,0:T(1,128)S(1)} async-done(((s32[128,1,2]{2,1,0:T(1,128)}), s32[128,1,2]{2,1,0:T(1,128)S(1)}, u32[]{:S(2)}, u32[]{:S(2)}) %all-to-all-start) | async-done | bytes 1056 | tf_op jit(solution)/shard_map/all_to_all | solution.py:396
  23.7 1.0 gather_fusion
  24.7 2.3 %select_select_fusion = bf16[128,2,2,16,128]{4,3,2,1,0:T(8,128)(2,1)} fusion(bf16[128,2,2,16,128]{4,3,2,1,0:T(8,128)(2,1)S(1)} %bitcast.131, pred[128,2]{1,0:T(8,128)(4,1)S(1)} %copy.43, pred[128,2]{1,0:T(8,128)(4,1)S(1)} %copy.41), kind=kLoop, calls=%fused_computation.3 | loop fusion | flops 2097152 | bytes 4194816 | tf_op jit(solution)/shard_map/jit(_where)/select_n | solution.py:400
  26.9 5.6 %all-to-all-start.1 = ((bf16[128,2,2,16,128]{4,3,2,1,0:T(8,128)(2,1)}), bf16[128,2,2,16,128]{4,3,2,1,0:T(8,128)(2,1)}, u32[]{:S(2)}, u32[]{:S(2)}) async-start(bf16[128,2,2,16,128]{4,3,2,1,0:T(8,128)(2,1)} %select_select_fusion), calls=%async_computation.1 | async-start | bytes 4194304 | tf_op jit(solution)/shard_map/all_to_all | solution.py:401
  33.1 1.4 fusion.perm
  34.5 27.6 %all-to-all-done.1 = bf16[128,2,2,16,128]{4,3,2,1,0:T(8,128)(2,1)} async-done(((bf16[128,2,2,16,128]{4,3,2,1,0:T(8,128)(2,1)}), bf16[128,2,2,16,128]{4,3,2,1,0:T(8,128)(2,1)}, u32[]{:S(2)}, u32[]{:S(2)}) %all-to-all-start.1) | async-done | bytes 2097184 | tf_op jit(solution)/shard_map/all_to_all | solution.py:401
  62.1 8.2 %warp.1 = bf16[4,64,1024]{2,1,0:T(8,128)(2,1)S(1)} custom-call(s32[256]{0:T(256)S(1)} %reshape_squeeze.3.foot, s32[32]{0:T(128)S(1)} %bitcast.127, s32[32]{0:T(128)S(1)} %bitcast.128, s32[32]{0:T(128)S(1)} %bitcast.129, f32[192]{0:T(256)S(1)} %reshape.131.wts, bf16[256,32,128]{2,1,0:T(8,128)(2,1)} %bitcast.11.arrived, f32[2,64,1024]{2,1,0:T(8,128)S(1)} %copy-done.1, ...), custom_call_target="tpu_custom_call" | custom-call | tf_op jit(solution)/shard_map/warp/pallas_call | solution.py:85
  71.0 2.5 %collective-permute-start = (bf16[4,9,1024]{2,1,0:T(8,128)(2,1)S(1)}, bf16[4,9,1024]{2,1,0:T(8,128)(2,1)S(1)}, u32[]{:S(2)}, u32[]{:S(2)}) collective-permute-start(bf16[4,9,1024]{2,1,0:T(8,128)(2,1)S(1)} %get-tuple-element.45), channel_id=1, source_target_pairs={{0,1},{1,2},{2,3},{3,4},{4,5},{5,6},{6,7},{7,8},{8,9},{9,10},{10,1... | collective-permute-start | bytes 221192 | tf_op jit(solution)/shard_map/ppermute | solution.py:375
  74.8 1.3 collective-permute-start.1
  76.7 3.8 %collective-permute-done.1 = bf16[4,9,1024]{2,1,0:T(8,128)(2,1)S(1)} collective-permute-done((bf16[4,9,1024]{2,1,0:T(8,128)(2,1)S(1)}, bf16[4,9,1024]{2,1,0:T(8,128)(2,1)S(1)}, u32[]{:S(2)}, u32[]{:S(2)}) %collective-permute-start.1) | collective-permute-done | bytes 73760 | tf_op jit(solution)/shard_map/ppermute | solution.py:376
  80.5 0.8 pad_maximum_fusion
  81.3 2.5 %concatenate.32 = bf16[104,1024]{1,0:T(8,128)(2,1)S(1)} concatenate(bf16[48,1024]{1,0:T(8,128)(2,1)} %bitcast.146, bf16[48,1024]{1,0:T(8,128)(2,1)} %bitcast.147, bf16[1,1024]{1,0:T(2,128)(2,1)} %get-tuple-element.58, bf16[1,1024]{1,0:T(2,128)(2,1)} %get-tuple-element.50, bf16[1,1024]{1,0:T(2,128)(2,1)} %get-tuple-element.57, bf16[1,1024]{1,0:T(2,128)(2,1)} %get-tuple-element.49, ...), dimensions={0} | concatenate | bytes 425984 | tf_op jit(solution)/shard_map/concatenate | solution.py:384
  83.9 0.7 bitcast_dynamic-update-slice_fusion.7
  84.6 2.5 %concatenate.33 = bf16[104,1024]{1,0:T(8,128)(2,1)S(1)} concatenate(bf16[48,1024]{1,0:T(8,128)(2,1)} %bitcast.148, bf16[48,1024]{1,0:T(8,128)(2,1)} %bitcast.145, bf16[1,1024]{1,0:T(2,128)(2,1)} %get-tuple-element.56, bf16[1,1024]{1,0:T(2,128)(2,1)} %get-tuple-element.48, bf16[1,1024]{1,0:T(2,128)(2,1)} %get-tuple-element.55, bf16[1,1024]{1,0:T(2,128)(2,1)} %get-tuple-element.47, ...), dimensions={0} | concatenate | bytes 425984 | tf_op jit(solution)/shard_map/concatenate | solution.py:384
  87.1 0.7 bitcast_dynamic-update-slice_fusion.6
  87.8 0.7 concatenate.34
  88.5 0.7 bitcast_dynamic-update-slice_fusion.5
  89.2 0.7 concatenate.35
  90.0 0.7 bitcast_dynamic-update-slice_fusion.4
  90.7 0.7 bitcast_dynamic-update-slice_fusion.3
  92.2 0.8 slice_bitcast_fusion
  94.5 6.8 %all-to-all-start.2 = ((bf16[8,13,8,1024]{3,2,1,0:T(8,128)(2,1)}), bf16[8,13,8,1024]{3,2,1,0:T(8,128)(2,1)}, u32[]{:S(2)}, u32[]{:S(2)}) async-start(bf16[8,13,8,1024]{3,2,1,0:T(8,128)(2,1)} %bitcast_dynamic-update-slice_fusion), calls=%async_computation.2 | async-start | bytes 3407872 | tf_op jit(solution)/shard_map/all_to_all | solution.py:406
  101.3 22.2 %all-to-all-done.2.arr = bf16[8,13,8,1024]{3,2,1,0:T(8,128)(2,1)} async-done(((bf16[8,13,8,1024]{3,2,1,0:T(8,128)(2,1)}), bf16[8,13,8,1024]{3,2,1,0:T(8,128)(2,1)}, u32[]{:S(2)}, u32[]{:S(2)}) %all-to-all-start.2) | async-done | bytes 1703968 | tf_op jit(solution)/shard_map/all_to_all | solution.py:406
  123.5 19.1 %krylov.1 = (f32[128,128]{1,0:T(8,128)S(1)}, f32[5,3,8,16,8,128]{5,4,3,2,1,0:T(8,128)}, f32[3,8,16,8,128]{4,3,2,1,0:T(8,128)S(1)}) custom-call(f32[24]{0:T(128)S(1)} %and_convert_fusion.rowmask, bf16[8,13,8,1024]{3,2,1,0:T(8,128)(2,1)} %all-to-all-done.2.arr), custom_call_target="tpu_custom_call" | custom-call | tf_op jit(solution)/shard_map/krylov/pallas_call | solution.py:244
  142.7 17.5 %all_to_all.35 = f32[128,1,128]{2,1,0:T(1,128)S(1)} all-to-all(f32[128,1,128]{2,1,0:T(1,128)S(1)} %bitcast.126), channel_id=1, replica_groups=mesh['slab'=8,'row'=16] {'slab','row'}, dimensions={0} | all-to-all | bytes 131072 | tf_op jit(solution)/shard_map/all_to_all | solution.py:411
  160.2 3.2 %copy-done = f32[5,3,8,16,8,128]{5,4,3,2,1,0:T(8,128)S(1)} copy-done((f32[5,3,8,16,8,128]{5,4,3,2,1,0:T(8,128)S(1)}, f32[5,3,8,16,8,128]{5,4,3,2,1,0:T(8,128)}, u32[]{:S(2)}) %copy-start) | copy-done | bytes 7864344
  163.4 2.8 %combine.1 = bf16[8,2,3,16,1024]{4,3,2,1,0:T(8,128)(2,1)S(1)} custom-call(f32[128,128]{1,0:T(8,128)S(1)} %bitcast.125, f32[5,3,8,16,8,128]{5,4,3,2,1,0:T(8,128)S(1)} %copy-done, f32[3,8,16,8,128]{4,3,2,1,0:T(8,128)S(1)} %get-tuple-element.7.s), custom_call_target="tpu_custom_call" | custom-call | tf_op jit(solution)/shard_map/combine/pallas_call | solution.py:329
  166.2 24.2 %all_to_all.36.back = bf16[8,2,3,16,1024]{4,3,2,1,0:T(8,128)(2,1)S(1)} all-to-all(bf16[8,2,3,16,1024]{4,3,2,1,0:T(8,128)(2,1)S(1)} %combine.1), channel_id=1, replica_groups=mesh['slab'=8,'row'=16] {'slab'}, dimensions={0} | all-to-all | bytes 3145728 | tf_op jit(solution)/shard_map/all_to_all | solution.py:413
  190.4 5.4 %finish.1 = (f32[3,2,64,1024]{3,2,1,0:T(8,128)}, f32[3,2,64,1024]{3,2,1,0:T(8,128)}) custom-call(bf16[8,2,3,16,1024]{4,3,2,1,0:T(8,128)(2,1)S(1)} %all_to_all.36.back, bf16[1024,1024]{1,0:T(8,128)(2,1)S(1)} %fusion.perm), custom_call_target="tpu_custom_call" | custom-call | tf_op jit(solution)/shard_map/finish/pallas_call | solution.py:357
  (48 shorter events, 6.0 us)
Async XLA Ops:
  2.0 21.0 %all-to-all-start = ((s32[128,1,2]{2,1,0:T(1,128)}), s32[128,1,2]{2,1,0:T(1,128)S(1)}, u32[]{:S(2)}, u32[]{:S(2)}) async-start(s32[128,1,2]{2,1,0:T(1,128)} %bitcast.5), calls=%async_computation | async-start | bytes 131072 | tf_op jit(solution)/shard_map/all_to_all | solution.py:396
  26.9 5.6 %copy-start.6 = (s32[1,1,32,8]{2,3,1,0:T(8,128)S(1)}, s32[1,1,32,8]{2,3,1,0:T(8,128)}, u32[]{:S(2)}) copy-start(s32[1,1,32,8]{2,3,1,0:T(8,128)} %param.11) | copy-start | bytes 3076
  26.9 5.8 %copy-start.7 = (f32[1,1,32,3]{2,1,3,0:T(1,128)S(1)}, f32[1,1,32,3]{2,1,3,0:T(1,128)}, u32[]{:S(2)}) copy-start(f32[1,1,32,3]{2,1,3,0:T(1,128)} %param.15) | copy-start | bytes 1156
  26.9 35.2 %all-to-all-start.1 = ((bf16[128,2,2,16,128]{4,3,2,1,0:T(8,128)(2,1)}), bf16[128,2,2,16,128]{4,3,2,1,0:T(8,128)(2,1)}, u32[]{:S(2)}, u32[]{:S(2)}) async-start(bf16[128,2,2,16,128]{4,3,2,1,0:T(8,128)(2,1)} %select_select_fusion), calls=%async_computation.1 | async-start | bytes 4194304 | tf_op jit(solution)/shard_map/all_to_all | solution.py:401
  32.6 29.5 %copy-start.1 = (f32[2,64,1024]{2,1,0:T(8,128)S(1)}, f32[2,64,1024]{2,1,0:T(8,128)}, u32[]{:S(2)}) copy-start(f32[2,64,1024]{2,1,0:T(8,128)} %fixed.1) | copy-start | bytes 1572868
  32.6 29.5 %copy-start.2 = (s32[1,1,32]{2,1,0:T(1,128)S(1)}, s32[1,1,32]{2,1,0:T(1,128)}, u32[]{:S(2)}) copy-start(s32[1,1,32]{2,1,0:T(1,128)} %param.12) | copy-start | bytes 388
  32.6 29.5 %copy-start.3 = (s32[1,1,32]{2,1,0:T(1,128)S(1)}, s32[1,1,32]{2,1,0:T(1,128)}, u32[]{:S(2)}) copy-start(s32[1,1,32]{2,1,0:T(1,128)} %param.13) | copy-start | bytes 388
  32.6 29.5 %copy-start.4 = (s32[1,1,32]{2,1,0:T(1,128)S(1)}, s32[1,1,32]{2,1,0:T(1,128)}, u32[]{:S(2)}) copy-start(s32[1,1,32]{2,1,0:T(1,128)} %param.14) | copy-start | bytes 388
  71.0 5.0 %collective-permute-start = (bf16[4,9,1024]{2,1,0:T(8,128)(2,1)S(1)}, bf16[4,9,1024]{2,1,0:T(8,128)(2,1)S(1)}, u32[]{:S(2)}, u32[]{:S(2)}) collective-permute-start(bf16[4,9,1024]{2,1,0:T(8,128)(2,1)S(1)} %get-tuple-element.45), channel_id=1, source_target_pairs={{0,1},{1,2},{2,3},{3,4},{4,5},{5,6},{6,7},{7,8},{8,9},{9,10},{10,1... | collective-permute-start | bytes 221192 | tf_op jit(solution)/shard_map/ppermute | solution.py:375
  74.8 5.7 %collective-permute-start.1 = (bf16[4,9,1024]{2,1,0:T(8,128)(2,1)S(1)}, bf16[4,9,1024]{2,1,0:T(8,128)(2,1)S(1)}, u32[]{:S(2)}, u32[]{:S(2)}) collective-permute-start(bf16[4,9,1024]{2,1,0:T(8,128)(2,1)S(1)} %get-tuple-element.44), channel_id=1, source_target_pairs={{1,0},{2,1},{3,2},{4,3},{5,4},{6,5},{7,6},{8,7},{9,8},{10,9},{11,1... | collective-permute-start | bytes 221192 | tf_op jit(solution)/shard_map/ppermute | solution.py:376
  80.5 0.9 copy-start.5
  94.5 29.1 %all-to-all-start.2 = ((bf16[8,13,8,1024]{3,2,1,0:T(8,128)(2,1)}), bf16[8,13,8,1024]{3,2,1,0:T(8,128)(2,1)}, u32[]{:S(2)}, u32[]{:S(2)}) async-start(bf16[8,13,8,1024]{3,2,1,0:T(8,128)(2,1)} %bitcast_dynamic-update-slice_fusion), calls=%async_computation.2 | async-start | bytes 3407872 | tf_op jit(solution)/shard_map/all_to_all | solution.py:406
  160.2 3.2 %copy-start = (f32[5,3,8,16,8,128]{5,4,3,2,1,0:T(8,128)S(1)}, f32[5,3,8,16,8,128]{5,4,3,2,1,0:T(8,128)}, u32[]{:S(2)}) copy-start(f32[5,3,8,16,8,128]{5,4,3,2,1,0:T(8,128)} %get-tuple-element.6.v) | copy-start | bytes 23592964

commit v2 on v1

v2 whole, which is shorter than its diff:
```python
import functools

import jax
import jax.numpy as jnp
from jax import lax
from jax.experimental import pallas as pl
from jax.experimental.pallas import tpu as pltpu
from jax.sharding import PartitionSpec as P

TY = 16
TZ = 128
ITERS = 4

smoothing = 0.02
damping = 0.1
stencil_diag = 42.0

LOW = 0.1
HIGH = 3.2
CENTRE = (HIGH + LOW) / 2
HALF = (HIGH - LOW) / 2
REACH = (smoothing / HALF) ** 4 * 8

FINE = 4
WIDE = 8 // FINE
SPAN = 128 * FINE

BOTH = ("slab", "row")
F32 = jnp.float32
BF16 = jnp.bfloat16


def spread():
    source = lax.broadcasted_iota(jnp.int32, (SPAN, SPAN), 0)
    target = lax.broadcasted_iota(jnp.int32, (SPAN, SPAN), 1)
    return (target == (source % FINE) * 128 + source // FINE).astype(BF16)


def pick_kernel(asked, moving, out):
    depth = moving.shape[0]
    along = moving.shape[2] // TZ

    def peer(p, carry):
        for slot in range(out.shape[1]):
            number = asked[p, slot]
            tile = jnp.maximum(number, 0)
            rows = pl.ds(pl.multiple_of(lax.div(tile, along) * TY, TY), TY)
            lanes = pl.ds(pl.multiple_of(lax.rem(tile, along) * TZ, TZ), TZ)
            for x in range(depth):
                cells = moving[x, rows, lanes]
                out[p, slot, x] = jnp.where(number >= 0, cells, jnp.zeros_like(cells))
        return carry

    lax.fori_loop(0, out.shape[0], peer, 0, unroll=8)


def pick(asked, moving, slots):
    vmem = pl.BlockSpec(memory_space=pltpu.VMEM)
    return pl.pallas_call(
        pick_kernel,
        out_shape=jax.ShapeDtypeStruct((asked.shape[0], slots, moving.shape[0], TY, TZ), BF16),
        in_specs=[pl.BlockSpec(memory_space=pltpu.SMEM), vmem],
        out_specs=vmem,
        compiler_params=pltpu.CompilerParams(vmem_limit_bytes=8 * 1024 * 1024),
        name="pick",
    )(asked, moving)


def warp_kernel(foot, ox, oy, oz, wts, flip, arrived, fixed, perm, out, nat):
    base_z = lax.broadcasted_iota(jnp.int32, (256, 128), 0) - lax.broadcasted_iota(jnp.int32, (256, 128), 1)
    ro = lax.broadcasted_iota(jnp.int32, (64, 128), 0)
    ci = lax.broadcasted_iota(jnp.int32, (64, 128), 1)
    same = (ro // 32 == ci // 64) & ((ro // 16) % 2 == (ci // 16) % 2)
    base_y = jnp.where(same, ((ci // 32) % 2) * 16 + ci % 16 - ro % 16, -1000)

    def band(base, shift, here, after):
        return jnp.where(base == shift, here, jnp.where(base == shift + 1, after, 0.0)).astype(BF16)

    def tile_row(j, carry):
        for k in range(8):
            t = j * 8 + k
            sides = []
            for c in range(2):
                sides.append(
                    jnp.concatenate(
                        [arrived[foot[t * 8 + 4 * a + 2 * b + c]] for a in range(2) for b in range(2)], axis=0
                    )
                )
            patch = jnp.concatenate(sides, axis=1)
            wz = band(base_z, oz[t], wts[t * 6 + 4], wts[t * 6 + 5])
            first = jnp.dot(patch, wz, preferred_element_type=F32).astype(BF16)
            wy = band(base_y, oy[t], wts[t * 6 + 2], wts[t * 6 + 3])
            second = jnp.dot(wy, first, preferred_element_type=F32).astype(BF16).astype(F32)
            shift = ox[t]
            for xo in range(2):
                total = None
                for p in range(xo, xo + 3):
                    weight = jnp.where(
                        p - xo == shift, wts[t * 6], jnp.where(p - xo == shift + 1, wts[t * 6 + 1], 0.0)
                    )
                    term = weight * second[p * 16 : (p + 1) * 16]
                    total = term if total is None else total + term
                rows = pl.ds(pl.multiple_of(j * 16, 16), 16)
                lanes = slice(k * 128, (k + 1) * 128)
                nat[xo, rows, lanes] = total.astype(BF16)
                nat[2 + xo, rows, lanes] = (total - fixed[xo, rows, lanes]).astype(BF16)
        return carry

    lax.fori_loop(0, 4, tile_row, 0)
    for b in range(WIDE):
        lanes = slice(b * SPAN, b * SPAN + SPAN)
        mixed = jnp.dot(nat[:, :, lanes].reshape(256, SPAN), perm[...], preferred_element_type=F32)
        for place in range(8):
            dest = place + flip[0] * (7 - 2 * place)
            for m in range(4):
                out[dest, m, :, lanes] = mixed[m * 64 + place * 8 : m * 64 + place * 8 + 8].astype(BF16)


def warp(arrived, footpoints, offset_x, offset_y, offset_z, fractions, flip, fixed, perm):
    near = lax.reduce_precision(1.0 - fractions, 8, 7)
    far = lax.reduce_precision(fractions, 8, 7)
    wts = jnp.stack([near, far], axis=-1).reshape(-1)
    smem = pl.BlockSpec(memory_space=pltpu.SMEM)
    vmem = pl.BlockSpec(memory_space=pltpu.VMEM)
    return pl.pallas_call(
        warp_kernel,
        out_shape=jax.ShapeDtypeStruct((8, 4, 8, 1024), BF16),
        in_specs=[smem] * 6 + [vmem] * 3,
        out_specs=vmem,
        scratch_shapes=[pltpu.VMEM((4, 64, 1024), BF16)],
        compiler_params=pltpu.CompilerParams(vmem_limit_bytes=10 * 1024 * 1024),
        name="warp",
    )(footpoints.reshape(-1), offset_x, offset_y, offset_z, wts, flip, arrived, fixed, perm)


PARTS = [
    (kx, k, slice(kx * 8 + k * WIDE, kx * 8 + k * WIDE + WIDE)) for kx in range(2) for k in range(FINE)
]


def edge_masks():
    sub = lax.broadcasted_iota(jnp.int32, (1, 8, 128), 1)
    lane = lax.broadcasted_iota(jnp.int32, (WIDE, 8, 128), 2)
    one = lambda flag: jnp.where(flag, 1.0, 0.0).astype(F32)
    return one(sub != 0), one(sub != 7), lane == 0, lane == 127


def load(ref, *at):
    return {(kx, k): ref[(*at, tiles)] for kx, k, tiles in PARTS}


def x_pair(v, kx, k, masks):
    other = v[1 - kx, k]
    if kx == 0:
        return pltpu.roll(other, 1, 1) * masks[0], other
    return other, pltpu.roll(other, 7, 1) * masks[1]


def z_pair(v, kx, k, masks):
    nothing = jnp.zeros((1, 8, 128), F32)
    if k > 0:
        before = v[kx, k - 1]
    else:
        turned = pltpu.roll(v[kx, FINE - 1], 1, 2)
        carried = jnp.concatenate([nothing, turned[: WIDE - 1]], axis=0) if WIDE > 1 else nothing
        before = jnp.where(masks[2], carried, turned)
    if k < FINE - 1:
        after = v[kx, k + 1]
    else:
        turned = pltpu.roll(v[kx, 0], 127, 2)
        carried = jnp.concatenate([turned[1:], nothing], axis=0) if WIDE > 1 else nothing
        after = jnp.where(masks[3], carried, turned)
    return before, after


def beside(v, kx, k, masks):
    x0, x1 = x_pair(v, kx, k, masks)
    z0, z1 = z_pair(v, kx, k, masks)
    return (x0 + x1) + (z0 + z1)


def field(rows):
    return pltpu.VMEM((3, rows, 16, 8, 128), F32)


def krylov_kernel(rowmask, chunk3, mom, vout, sout, ends, s_s, im_s, v0, v1, v2, sems):
    masks = edge_masks()

    def chain(c, tiles, end, step):
        one = im_s[c, end, tiles] * im_s[c, end - step, tiles]
        return one * (im_s[c, end - 2 * step, tiles] * im_s[c, end - 3 * step, tiles]) * REACH

    def prepare(in_s, d_s, w_s, in_sems):
        chunks = [pltpu.make_async_copy(ref, in_s.at[g], in_sems.at[g]) for g, ref in enumerate((chunk3.at[0], chunk3.at[1], chunk3.at[2]))]
        for chunk in chunks:
            chunk.start()
        for g in (1, 0, 2):
            chunks[g].wait()
            for src in range(8):
                lines = in_s[g, src].astype(F32).reshape(32, 1024)
                for kz in range(8):
                    d_s[kz, src * 96 + g * 32 : src * 96 + g * 32 + 32, :] = lines[:, kz * 128 : kz * 128 + 128]

        def fetch(row, k, b):
            return d_s[FINE * b + k, pl.ds(row, 8, stride=96), :]

        def line(n, m):
            return lax.shift_right_logical(n, 3) * 32 + m * 8 + lax.bitwise_and(n, 7)

        def put_w(i, row_of):
            for kx, k, tiles in PARTS:
                for b in range(WIDE):
                    w_s[i, tiles.start + b] = fetch(row_of(kx), k, b)

        def fill(n, carry):
            put_w(n, lambda kx: line(n, kx))
            return carry

        lax.fori_loop(0, 24, fill, 0)

        def begin(n, carry):
            w = load(w_s, n)
            keep = rowmask[n]
            for kx, k, tiles in PARTS:
                diff = jnp.stack([fetch(line(n, 2 + kx), k, b) for b in range(WIDE)])
                xb, xa = x_pair(w, kx, k, masks)
                zb, za = z_pair(w, kx, k, masks)
                ys = w_s[n + 1, tiles] - w_s[n - 1, tiles]
                for c, s in enumerate(((xa - xb) * 0.5, ys * 0.5, (za - zb) * 0.5)):
                    im = keep / (s * s + (stencil_diag * smoothing + damping))
                    s_s[c, n, tiles] = s
                    im_s[c, n, tiles] = im
                    v0[c, n, tiles] = -s * diff * im
            return carry

        for c in range(3):
            for n in (0, 23):
                v0[c, n] = jnp.zeros((16, 8, 128), F32)
        lax.fori_loop(1, 23, begin, 0)

        for e, (edge, step) in enumerate(((0, 2), (23, -2))):
            w = load(w_s, edge)
            for kx, k, tiles in PARTS:
                lines = slice(tiles.start * 8, tiles.stop * 8)
                diff = jnp.stack([fetch(line(edge, 2 + kx), k, b) for b in range(WIDE)])
                xb, xa = x_pair(w, kx, k, masks)
                zb, za = z_pair(w, kx, k, masks)
                for slot, c, s in ((0, 0, (xa - xb) * 0.5), (1, 2, (za - zb) * 0.5)):
                    start = -s * diff / (s * s + (stencil_diag * smoothing + damping))
                    value = chain(c, tiles, edge + 4 * step, step) * start * rowmask[edge]
                    ends[e, slot, lines, :] = value.reshape(WIDE * 8, 128)
                ends[e, 2, lines, :] = (chain(1, tiles, edge + 4 * step, step) * rowmask[edge]).reshape(WIDE * 8, 128)
                ends[e, 3, lines, :] = w_s[edge + step // 2, tiles].reshape(WIDE * 8, 128)
                ends[e, 4, lines, :] = diff.reshape(WIDE * 8, 128)

    def iterate(u_s, v3, v4):
        vs = [v0, v1, v2, v3, v4]

        def copy(j):
            return pltpu.make_async_copy(vs[j].at[:, pl.ds(8 - 2 * j, 8)], vout.at[j], sems.at[j])

        s_copy = pltpu.make_async_copy(s_s.at[:, pl.ds(8, 8)], sout, sems.at[5])
        s_copy.start()
        copy(0).start()

        for j in range(4):
            gain = (1.0 if j == 0 else 2.0) / HALF
            old, new = vs[j], vs[j + 1]
            off = 2 * j

            def first(n, carry):
                scale = rowmask[n] * (gain * smoothing)
                for c in range(3):
                    v = load(old, c, n - off)
                    for kx, k, tiles in PARTS:
                        total = beside(v, kx, k, masks) + (old[c, n - off - 1, tiles] + old[c, n - off + 1, tiles])
                        u_s[c, n - 1, tiles] = (6.0 * v[kx, k] - total) * scale
                return carry

            lax.fori_loop(off + 1, 23 - off, first, 0)

            def second(n, carry):
                dots = {}
                for kx, k, tiles in PARTS:
                    dot = s_s[0, n, tiles] * old[0, n - off, tiles]
                    dot = dot + s_s[1, n, tiles] * old[1, n - off, tiles]
                    dots[kx, k] = (dot + s_s[2, n, tiles] * old[2, n - off, tiles]) * gain
                for c in range(3):
                    u = load(u_s, c, n - 1)
                    for kx, k, tiles in PARTS:
                        total = beside(u, kx, k, masks) + (u_s[c, n - 2, tiles] + u_s[c, n, tiles])
                        v = old[c, n - off, tiles]
                        image = s_s[c, n, tiles] * dots[kx, k] + (6.0 * u[kx, k] - total) + (gain * damping) * v
                        value = im_s[c, n, tiles] * image - (gain * CENTRE) * v
                        if j > 0:
                            value = value - vs[j - 1][c, n - off + 2, tiles]
                        new[c, n - off - 2, tiles] = value
                return carry

            lax.fori_loop(off + 2, 22 - off, second, 0)
            copy(j + 1).start()

        def products(n, sums):
            sums = list(sums)
            for c in range(3):
                for kx, k, tiles in PARTS:
                    s = s_s[c, n, tiles]
                    m = s * s + (stencil_diag * smoothing + damping)
                    v = [vs[j][c, n - 2 * j, tiles] for j in range(5)]
                    for j in range(4):
                        t = m * v[j]
                        for q, other in ((2 * j, v[j]), (2 * j + 1, v[j + 1])):
                            sums[q] = sums[q] + jnp.sum(t * other, axis=0)
            return tuple(sums)

        sums = list(lax.fori_loop(8, 16, products, tuple(jnp.zeros((8, 128), F32) for _ in range(8))))
        for first_row, step in ((8, 2), (15, -2)):
            end = first_row + 4 * step
            for c in range(3):
                for kx, k, tiles in PARTS:
                    share = chain(c, tiles, end, step) * v0[c, first_row, tiles]
                    s = s_s[c, end, tiles]
                    m = s * s + (stencil_diag * smoothing + damping)
                    sums[7] = sums[7] + jnp.sum(m * share * v3[c, end - 6, tiles], axis=0)
        lane = lax.broadcasted_iota(jnp.int32, (1, 128), 1)
        out = jnp.zeros((1, 128), F32)
        for q in range(8):
            out = jnp.where(lane == q, jnp.sum(sums[q], keepdims=True), out)
        mom[...] = jnp.broadcast_to(out, mom.shape)
        s_copy.wait()
        for j in range(5):
            copy(j).wait()

    pl.run_scoped(
        prepare,
        pltpu.VMEM((3, 8, 4, 8, 1024), BF16),
        pltpu.VMEM((8, 768, 128), F32),
        pltpu.VMEM((24, 16, 8, 128), F32),
        pltpu.SemaphoreType.DMA((3,)),
    )
    pl.run_scoped(iterate, field(22), field(12), field(8))


def krylov(chunks, rowmask, peers):
    vmem = pl.BlockSpec(memory_space=pltpu.VMEM)
    hbm = pl.BlockSpec(memory_space=pltpu.HBM)

    return pl.pallas_call(
        krylov_kernel,
        out_shape=(
            jax.ShapeDtypeStruct((peers, 128), F32),
            jax.ShapeDtypeStruct((5, 3, 8, 16, 8, 128), F32),
            jax.ShapeDtypeStruct((3, 8, 16, 8, 128), F32),
            jax.ShapeDtypeStruct((2, 5, 128, 128), F32),
        ),
        in_specs=[pl.BlockSpec(memory_space=pltpu.SMEM)] + [hbm],
        out_specs=(vmem, hbm, hbm, vmem),
        scratch_shapes=[
            field(24),
            field(24),
            field(24),
            field(20),
            field(16),
            pltpu.SemaphoreType.DMA((6,)),
        ],
        compiler_params=pltpu.CompilerParams(vmem_limit_bytes=31 * 1024 * 1024),
        cost_estimate=pl.CostEstimate(flops=400_000_000, bytes_accessed=60_000_000, transcendentals=0),
        name="krylov",
    )(rowmask, *chunks)


def ends_kernel(ends, far0, far1, out, rows):
    for e, far in enumerate((far0, far1)):
        lines = far[...].astype(F32).reshape(16, 1024)
        for kz in range(8):
            rows[kz] = lines[:, kz * 128 : kz * 128 + 128]
        for slot, c in ((0, 0), (1, 2)):
            out[e, c] = ends[e, slot]
        for kx, k, tiles in PARTS:
            for b in range(WIDE):
                at = slice((tiles.start + b) * 8, (tiles.start + b) * 8 + 8)
                beyond = rows[FINE * b + k, pl.ds(kx, 8, stride=2), :]
                near = ends[e, 3, at, :]
                s = (near - beyond) * 0.5 if e == 0 else (beyond - near) * 0.5
                start = -s * ends[e, 4, at, :] / (s * s + (stencil_diag * smoothing + damping))
                out[e, 1, at, :] = ends[e, 2, at, :] * start


def outer_rows(ends, far0, far1):
    vmem = pl.BlockSpec(memory_space=pltpu.VMEM)
    return pl.pallas_call(
        ends_kernel,
        out_shape=jax.ShapeDtypeStruct((2, 3, 128, 128), F32),
        in_specs=[vmem] * 3,
        out_specs=vmem,
        scratch_shapes=[pltpu.VMEM((8, 16, 128), F32)],
        compiler_params=pltpu.CompilerParams(vmem_limit_bytes=4 * 1024 * 1024),
        name="outer_rows",
    )(ends, far0, far1)


def coefficients(m):
    def lam(k):
        if k == 0:
            return CENTRE * m[0] + HALF * m[1]
        return CENTRE * m[k] + (HALF / 2) * (m[k + 1] + m[k - 1])

    lams = [lam(k) for k in range(7)]
    rows = [[0.5 * (lams[i + j] + lams[abs(i - j)]) for j in range(4)] + [m[i]] for i in range(4)]
    for p in range(4):
        inverse = 1.0 / rows[p][p]
        for q in range(p + 1, 4):
            factor = rows[q][p] * inverse
            rows[q] = [rows[q][k] - factor * rows[p][k] if k > p else rows[q][k] for k in range(5)]
    part = [None] * 4
    for p in reversed(range(4)):
        value = rows[p][4]
        for q in range(p + 1, 4):
            value = value - rows[p][q] * part[q]
        part[p] = value / rows[p][p]
    rest = [1.0 - CENTRE * part[0] - (HALF / 2) * part[1]]
    rest.append(-CENTRE * part[1] - HALF * part[0] - (HALF / 2) * part[2])
    rest.append(-CENTRE * part[2] - (HALF / 2) * (part[1] + part[3]))
    rest.append(-CENTRE * part[3] - (HALF / 2) * part[2])
    rest.append(-(HALF / 2) * part[3])
    return part, rest


def combine_kernel(mom, v_hbm, s_hbm, outer, out, v, s, turn, sems):
    loads = []
    for c in range(3):
        loads.append((
            pltpu.make_async_copy(v_hbm.at[:, c], v.at[:, c], sems.at[0, c]),
            pltpu.make_async_copy(s_hbm.at[c], s.at[c], sems.at[1, c]),
        ))
    for pair in loads:
        for each in pair:
            each.start()
    line = jnp.sum(mom[...], axis=0, keepdims=True)
    lane = lax.broadcasted_iota(jnp.int32, (1, 128), 1)
    p = [jnp.sum(jnp.where(lane == k, line, 0.0), axis=1, keepdims=True) for k in range(8)]
    m = [p[0], p[1]] + [2.0 * p[k] - p[k % 2] for k in range(2, 8)]
    part, rest = coefficients(m)
    part = [jnp.broadcast_to(x, (8, 128)) for x in part]
    rest = [jnp.broadcast_to(x, (8, 128)) for x in rest]

    for c in range(3):
        for each in loads[c]:
            each.wait()

        def row(i, carry):
            for kx, k, tiles in PARTS:
                at = pl.ds(pl.multiple_of((kx * 8 + i) * 8, 8), 8)
                for b in range(WIDE):
                    vecs = [v[j, c, i, tiles.start + b] for j in range(5)]
                    slope = s[c, i, tiles.start + b]
                    weight = slope * slope + (stencil_diag * smoothing + damping)
                    turn[c, 0, FINE * b + k, at, :] = sum(part[j] * vecs[j] for j in range(4))
                    turn[c, 1, FINE * b + k, at, :] = weight * sum(rest[j] * vecs[j] for j in range(5))
            return carry

        lax.fori_loop(0, 8, row, 0)
        for e, i in ((0, 0), (1, 7)):
            for kx, k, tiles in PARTS:
                at = slice((kx * 8 + i) * 8, (kx * 8 + i) * 8 + 8)
                for b in range(WIDE):
                    m = tiles.start + b
                    slope = s[c, i, m]
                    weight = slope * slope + (stencil_diag * smoothing + damping)
                    turn[c, 1, FINE * b + k, at, :] += weight * rest[4] * outer[e, c, m * 8 : m * 8 + 8, :]
        for q in range(2):
            for dest in range(8):
                for kz in range(8):
                    lanes = slice(kz * 128, kz * 128 + 128)
                    out[dest, q, c, :, lanes] = turn[c, q, kz, pl.ds(dest, 16, stride=8), :].astype(BF16)


def combine(moments, vectors, slopes, outer):
    vmem = pl.BlockSpec(memory_space=pltpu.VMEM)
    hbm = pl.BlockSpec(memory_space=pltpu.HBM)
    return pl.pallas_call(
        combine_kernel,
        out_shape=jax.ShapeDtypeStruct((8, 2, 3, 16, 1024), BF16),
        in_specs=[vmem, hbm, hbm, vmem],
        out_specs=vmem,
        scratch_shapes=[
            pltpu.VMEM(vectors.shape, F32),
            pltpu.VMEM(slopes.shape, F32),
            pltpu.VMEM((3, 2, 8, 128, 128), F32),
            pltpu.SemaphoreType.DMA((2, 3)),
        ],
        compiler_params=pltpu.CompilerParams(vmem_limit_bytes=24 * 1024 * 1024),
        name="combine",
    )(moments, vectors, slopes, outer)


def finish_kernel(flip, back, perm, sol, res):
    lines = jnp.concatenate([back[src, q, 0] for q in range(2) for src in range(8)], axis=0)
    lines = jnp.concatenate([lines[:, b * SPAN : b * SPAN + SPAN] for b in range(WIDE)], axis=0)
    cells = lax.dot_general(lines, perm[...], (((1,), (1,)), ((), ())), preferred_element_type=F32)
    for b in range(WIDE):
        for q, out in ((0, sol), (1, res)):
            for src in range(8):
                rows = pl.ds(pl.multiple_of((src + flip[0] * (7 - 2 * src)) * 8, 8), 8)
                for kx in range(2):
                    at = b * 256 + q * 128 + src * 16 + kx * 8
                    out[0, kx, rows, b * SPAN : b * SPAN + SPAN] = cells[at : at + 8]


def finish(back, flip, perm):
    shape = jax.ShapeDtypeStruct((3, 2, 64, 1024), F32)
    spec = pl.BlockSpec((1, 2, 64, 1024), lambda c: (c, 0, 0, 0))
    return pl.pallas_call(
        finish_kernel,
        grid=(3,),
        out_shape=(shape, shape),
        in_specs=[
            pl.BlockSpec(memory_space=pltpu.SMEM),
            pl.BlockSpec((8, 2, 1, 16, 1024), lambda c: (0, 0, c, 0, 0)),
            pl.BlockSpec((SPAN, SPAN), lambda c: (0, 0)),
        ],
        out_specs=(spec, spec),
        compiler_params=pltpu.CompilerParams(vmem_limit_bytes=14 * 1024 * 1024),
        name="finish",
    )(flip, back, perm)


def ring(cells, step):
    slabs, rows = lax.axis_size("slab"), lax.axis_size("row")

    def device(chunk):
        row, place = chunk // slabs, chunk % slabs
        return (place if row % 2 == 0 else slabs - 1 - place) * rows + row

    chunks = range(max(0, -step), slabs * rows - max(0, step))
    return lax.ppermute(cells, BOTH, [(device(i), device(i + step)) for i in chunks])


def per_device(moving, fixed, requests, footpoints, offset_x, offset_y, offset_z, fractions):
    depth, height, width = moving.shape
    perm = spread()
    block, slab = lax.axis_index("row"), lax.axis_index("slab")
    flip = block % 2
    start = block * height + (slab + flip * (7 - 2 * slab)) * 8 - 8
    peers, slots = requests.shape[2:]
    asked = jnp.pad(requests[0, 0], ((0, 0), (0, 128 - slots)))
    asked = lax.all_to_all(asked, BOTH, split_axis=0, concat_axis=0, tiled=True)
    outgoing = pick(asked, moving, slots)
    arrived = lax.all_to_all(outgoing, BOTH, split_axis=0, concat_axis=0, tiled=True)
    arrived = arrived.reshape(peers * slots, depth * TY, TZ)
    flip = flip.reshape(1)
    own = warp(
        arrived, footpoints[0, 0], offset_x[0, 0], offset_y[0, 0], offset_z[0, 0], fractions[0, 0], flip, fixed, perm
    )
    own = lax.all_to_all(own, "slab", split_axis=0, concat_axis=0, tiled=True)
    chunks = (jnp.stack([ring(own, 1), own, ring(own, -1)]),)
    rows = start + jnp.arange(24, dtype=jnp.int32)
    rowmask = ((rows >= 0) & (rows < height * lax.axis_size("row"))).astype(F32)
    moments, vectors, slopes, ends = krylov(chunks, rowmask, peers)
    far = (ring(own[:, 0:2, 7], 2), ring(own[:, 0:2, 0], -2))
    moments, far = lax.optimization_barrier((moments, far))
    outer = outer_rows(ends, *far)
    moments, outer = lax.optimization_barrier((moments, outer))
    moments = lax.all_to_all(moments, BOTH, split_axis=0, concat_axis=0, tiled=True)
    back = combine(moments, vectors, slopes, outer)
    back = lax.all_to_all(back, "slab", split_axis=0, concat_axis=0, tiled=True)
    return finish(back, flip, perm)


def solution(mesh):
    return jax.shard_map(
        per_device,
        mesh=mesh,
        in_specs=(
            P("slab", "row", None),
            P("slab", "row", None),
            P("slab", "row", None, None),
            P("slab", "row", None, None),
            P("slab", "row", None),
            P("slab", "row", None),
            P("slab", "row", None),
            P("slab", "row", None, None),
        ),
        out_specs=(P(None, "slab", "row", None), P(None, "slab", "row", None)),
        check_vma=False,
    )
```

time: 197 us -> 167 us (0.85)
  blocking collectives: 41.7 us -> 75.6 us
  waiting for transfers between devices: 62 us -> 32.3 us
  local copies, waits for them, and re-layouts: 23.4 us -> 4.15 us
  starting transfers between devices: 27.7 us -> 14.9 us
  other arithmetic: 4.58 us -> 0.86 us
  Pallas kernels: 35.6 us -> 37.9 us
    all_to_all x0 -> x2, blocking collectives: none -> 33.7 us  [the longest x1 20.9 us: per_device(): asked = lax.all_to_all(asked, BOTH, split_axis=0, concat_axis=0, tiled=True)]
    all_to_all x2 -> x0, waiting for transfers between devices: 30.7 us -> none  [the longest x1 22.2 us: per_device(): lax.all_to_all(windows(own), 'slab', split_axis=0, concat_axis=0, tiled=T...]
    all_to_all x2 -> x0, starting transfers between devices: 18.3 us -> none  [the longest x1 11.5 us: per_device(): lax.all_to_all(requests[0, 0], BOTH, split_axis=0, concat_axis=0, tiled=T...]
    unnamed x26 -> x18, local copies, waits for them, and re-layouts: 10.6 us -> 3.17 us
    concatenate x8 -> x0, local copies, waits for them, and re-layouts: 6.76 us -> none  [windows(): jnp.concatenate([body[2:4].reshape(48, 1024), body[0:2].reshape(48, 1024)...]
    ppermute x2 -> x4, starting transfers between devices: 3.73 us -> 10.3 us  [ring(): lax.ppermute(cells, BOTH, [(device(i), device(i + step)) for i in chunks])]
    another operation x6 -> x0, local copies, waits for them, and re-layouts: 3.37 us -> none  [the longest x4 2.68 us: windows(): jnp.stack([whole[0, 8 * s], whole[0, 8 * s + 25], whole[1, 8 * s], whole[...]
    pallas_call x1, Pallas kernels: 19.1 us -> 22.4 us  [krylov(): pl.pallas_call(krylov_kernel, out_shape=(jax.ShapeDtypeStruct((peers, 128...]
  transfers between devices with their start and end apart: 5 -> 5, of which waited for: 4 -> 2; matrix products, arithmetic and copies ran while one was open for 2% -> 1% of each run, Pallas kernels for 0% -> 13%
where the time goes in v2:
time: 167 us
  blocking collectives  75.6 us (45%)
  Pallas kernels  37.9 us (23%)
  waiting for transfers between devices  32.3 us (19%)
  starting transfers between devices  14.9 us (9%)
  local copies, waits for them, and re-layouts  4.15 us (2%)
    all_to_all x1, waiting for transfers between devices, per_device(): lax.all_to_all(outgoing, BOTH, split_axis=0, concat_axis=0, tiled=True)  28.7 us
    all_to_all x1, blocking collectives, per_device(): back = lax.all_to_all(back, 'slab', split_axis=0, concat_axis=0, tiled=True)  24.2 us
    pallas_call x1, Pallas kernels, krylov(): pl.pallas_call(krylov_kernel, out_shape=(jax.ShapeDtypeStruct((peers, 128...  22.4 us
    all_to_all x1, blocking collectives, per_device(): asked = lax.all_to_all(asked, BOTH, split_axis=0, concat_axis=0, tiled=True)  20.9 us
    all_to_all x1, blocking collectives, per_device(): lax.all_to_all(moments, BOTH, split_axis=0, concat_axis=0, tiled=True)  17.8 us
    all_to_all x1, blocking collectives, per_device(): own = lax.all_to_all(own, 'slab', split_axis=0, concat_axis=0, tiled=True)  12.8 us
    ppermute x4, starting transfers between devices, ring(): lax.ppermute(cells, BOTH, [(device(i), device(i + step)) for i in chunks])  10.3 us
    pallas_call x1, Pallas kernels, warp(): pl.pallas_call(warp_kernel, out_shape=jax.ShapeDtypeStruct((8, 4, 8, 1024...  6.91 us
  transfers between devices with their start and end apart: 5, of which 2 were waited for; matrix products, arithmetic and copies ran while one was open for 1% of the time, Pallas kernels for 13%

profile of v2, /device:TPU:1, one launch (start us, length us, event | category | flops | bytes accessed | tf_op | source)
XLA Modules:
  0.0 166.5 jit_solution(14566420277517257448)
XLA Ops:
  0.6 0.8 copy.20
  1.4 20.9 %all_to_all.37 = s32[128,1,128]{2,1,0:T(1,128)S(1)} all-to-all(s32[128,1,128]{2,1,0:T(1,128)S(1)} %bitcast.41), channel_id=1, replica_groups=mesh['slab'=8,'row'=16] {'slab','row'}, dimensions={0} | all-to-all | bytes 131072 | tf_op jit(solution)/shard_map/all_to_all | solution.py:547
  22.3 0.9 copy-done.2
  23.3 2.9 %pick.1 = bf16[128,2,2,16,128]{4,3,2,1,0:T(8,128)(2,1)S(1)} custom-call(s32[128,128]{1,0:T(8,128)S(1)} %bitcast.33, bf16[2,64,1024]{2,1,0:T(8,128)(2,1)S(1)} %copy-done.2), custom_call_target="tpu_custom_call" | custom-call | tf_op jit(solution)/shard_map/pick/pallas_call | solution.py:59
  26.2 1.3 copy-done
  27.6 0.0 copy-start.4
  27.6 0.0 copy-start.5
  27.6 4.6 %all-to-all-start.1 = ((bf16[128,2,2,16,128]{4,3,2,1,0:T(8,128)(2,1)}), bf16[128,2,2,16,128]{4,3,2,1,0:T(8,128)(2,1)S(1)}, u32[]{:S(2)}, u32[]{:S(2)}) async-start(bf16[128,2,2,16,128]{4,3,2,1,0:T(8,128)(2,1)} %copy-done), calls=%async_computation.1 | async-start | bytes 4194304 | tf_op jit(solution)/shard_map/all_to_all | solution.py:549
  32.2 0.1 copy.18
  32.3 0.1 reshape_squeeze.3.foot
  32.4 0.1 copy.19
  32.5 0.1 reshape.45.wts
  32.7 0.6 fusion.perm
  33.3 28.7 %all-to-all-done.1 = bf16[128,2,2,16,128]{4,3,2,1,0:T(8,128)(2,1)S(1)} async-done(((bf16[128,2,2,16,128]{4,3,2,1,0:T(8,128)(2,1)}), bf16[128,2,2,16,128]{4,3,2,1,0:T(8,128)(2,1)S(1)}, u32[]{:S(2)}, u32[]{:S(2)}) %all-to-all-start.1) | async-done | bytes 2097184 | tf_op jit(solution)/shard_map/all_to_all | solution.py:549
  62.1 6.9 %warp.1 = bf16[8,4,8,1024]{3,2,1,0:T(8,128)(2,1)S(1)} custom-call(s32[256]{0:T(256)S(1)} %reshape_squeeze.3.foot, s32[32]{0:T(128)S(1)} %bitcast.35, s32[32]{0:T(128)S(1)} %bitcast.36, s32[32]{0:T(128)S(1)} %bitcast.37, f32[192]{0:T(256)S(1)} %reshape.45.wts, s32[1]{0:T(128)} %bitcast.flip, bf16[256,32,128]{2,1,0:T(8,128)(2,1)S(1)} %bitcast.31, ...), custom_call_target="tpu_custom_call" | custom-call | tf_op jit(solution)/shard_map/warp/pallas_call | solution.py:125
  69.0 0.4 copy.21
  69.4 12.8 %all_to_all.38 = bf16[8,4,8,1024]{3,1,2,0:T(4,128)(2,1)S(1)} all-to-all(bf16[8,4,8,1024]{3,1,2,0:T(4,128)(2,1)S(1)} %copy.21), channel_id=1, replica_groups=mesh['slab'=8,'row'=16] {'slab'}, dimensions={0} | all-to-all | bytes 1048576 | tf_op jit(solution)/shard_map/all_to_all | solution.py:555
  82.2 0.2 copy.32
  82.4 3.1 %collective-permute-start = (bf16[8,4,8,1024]{3,2,1,0:T(8,128)(2,1)S(1)}, bf16[8,4,8,1024]{3,2,1,0:T(8,128)(2,1)S(1)}, u32[]{:S(2)}, u32[]{:S(2)}) collective-permute-start(bf16[8,4,8,1024]{3,2,1,0:T(8,128)(2,1)S(1)} %copy.32), channel_id=1, source_target_pairs={{0,16},{16,32},{32,48},{48,64},{64,80},{80,96},{96,112},{112,113},... | collective-permute-start | bytes 1572872 | tf_op jit(solution)/shard_map/ppermute | solution.py:536
  85.5 1.9 %collective-permute-start.1 = (bf16[8,4,8,1024]{3,2,1,0:T(8,128)(2,1)S(1)}, bf16[8,4,8,1024]{3,2,1,0:T(8,128)(2,1)S(1)}, u32[]{:S(2)}, u32[]{:S(2)}) collective-permute-start(bf16[8,4,8,1024]{3,2,1,0:T(8,128)(2,1)S(1)} %copy.32), channel_id=1, source_target_pairs={{16,0},{32,16},{48,32},{64,48},{80,64},{96,80},{112,96},{113,112},... | collective-permute-start | bytes 1572872 | tf_op jit(solution)/shard_map/ppermute | solution.py:536
  87.5 1.3 collective-permute-start.3
  88.8 4.0 %collective-permute-start.2 = (bf16[8,2,1024]{2,1,0:T(2,128)(2,1)S(1)}, bf16[8,2,1024]{2,1,0:T(2,128)(2,1)S(1)}, u32[]{:S(2)}, u32[]{:S(2)}) collective-permute-start(bf16[8,2,1024]{2,1,0:T(2,128)(2,1)S(1)} %get-tuple-element.21), channel_id=1, source_target_pairs={{0,32},{16,48},{32,64},{48,80},{64,96},{80,112},{96,113},{112,97},... | collective-permute-start | bytes 98312 | tf_op jit(solution)/shard_map/ppermute | solution.py:536
  92.8 0.0 collective-permute-done
  92.8 3.5 %collective-permute-done.1 = bf16[8,4,8,1024]{3,2,1,0:T(8,128)(2,1)S(1)} collective-permute-done((bf16[8,4,8,1024]{3,2,1,0:T(8,128)(2,1)S(1)}, bf16[8,4,8,1024]{3,2,1,0:T(8,128)(2,1)S(1)}, u32[]{:S(2)}, u32[]{:S(2)}) %collective-permute-start.1) | collective-permute-done | bytes 524320 | tf_op jit(solution)/shard_map/ppermute | solution.py:536
  96.3 0.2 pad_maximum_fusion.chunk3
  96.5 22.4 %krylov.1 = (f32[128,128]{1,0:T(8,128)S(1)}, f32[5,3,8,16,8,128]{5,4,3,2,1,0:T(8,128)S(1)}, f32[3,8,16,8,128]{4,3,2,1,0:T(8,128)S(1)}, f32[2,5,128,128]{3,2,1,0:T(8,128)S(1)}) custom-call(f32[24]{0:T(128)S(1)} %and_convert_fusion.rowmask, bf16[3,8,4,8,1024]{4,3,2,1,0:T(8,128)(2,1)S(1)} %pad_maximum_fusion.chunk3), custom_call_target="tpu_custom_call" | custom-call | flops 400000000 | bytes 60000000 | tf_op jit(solution)/shard_map/krylov/pallas_call | solution.py:348
  119.0 0.0 collective-permute-done.3.far1
  119.0 0.1 outer_rows.1.outer
  119.1 17.8 %all_to_all.39 = f32[128,1,128]{2,1,0:T(1,128)S(1)} all-to-all(f32[128,1,128]{2,1,0:T(1,128)S(1)} %bitcast.34), channel_id=1, replica_groups=mesh['slab'=8,'row'=16] {'slab','row'}, dimensions={0} | all-to-all | bytes 131072 | tf_op jit(solution)/shard_map/all_to_all | solution.py:564
  136.8 2.6 %combine.1 = bf16[8,2,3,16,1024]{4,3,2,1,0:T(8,128)(2,1)S(1)} custom-call(f32[128,128]{1,0:T(8,128)S(1)} %bitcast.32, f32[5,3,8,16,8,128]{5,4,3,2,1,0:T(8,128)S(1)} %get-tuple-element.17.v_hbm, f32[3,8,16,8,128]{4,3,2,1,0:T(8,128)S(1)} %get-tuple-element.18.s_hbm, f32[2,3,128,128]{3,2,1,0:T(8,128)S(1)} %outer_rows.1.outer), custom_call_target="tpu_custom_call" | custom-call | tf_op jit(solution)/shard_map/combine/pallas_call | solution.py:481
  139.5 24.2 %all_to_all.40.back = bf16[8,2,3,16,1024]{4,3,2,1,0:T(8,128)(2,1)S(1)} all-to-all(bf16[8,2,3,16,1024]{4,3,2,1,0:T(8,128)(2,1)S(1)} %combine.1), channel_id=1, replica_groups=mesh['slab'=8,'row'=16] {'slab'}, dimensions={0} | all-to-all | bytes 3145728 | tf_op jit(solution)/shard_map/all_to_all | solution.py:566
  163.6 2.9 %finish.1 = (f32[3,2,64,1024]{3,2,1,0:T(8,128)}, f32[3,2,64,1024]{3,2,1,0:T(8,128)}) custom-call(s32[1]{0:T(128)} %bitcast.flip, bf16[8,2,3,16,1024]{4,3,2,1,0:T(8,128)(2,1)S(1)} %all_to_all.40.back, bf16[512,512]{1,0:T(8,128)(2,1)S(1)} %fusion.perm), custom_call_target="tpu_custom_call" | custom-call | tf_op jit(solution)/shard_map/finish/pallas_call | solution.py:513
  (21 shorter events, 0.1 us)
Async XLA Ops:
  22.3 1.0 copy-start.2
  26.2 1.3 copy-start
  27.6 4.6 %copy-start.6 = (s32[1,1,32,8]{2,3,1,0:T(8,128)S(1)}, s32[1,1,32,8]{2,3,1,0:T(8,128)}, u32[]{:S(2)}) copy-start(s32[1,1,32,8]{2,3,1,0:T(8,128)} %param.11) | copy-start | bytes 3076
  27.6 4.8 %copy-start.7 = (f32[1,1,32,3]{2,1,3,0:T(1,128)S(1)}, f32[1,1,32,3]{2,1,3,0:T(1,128)}, u32[]{:S(2)}) copy-start(f32[1,1,32,3]{2,1,3,0:T(1,128)} %param.15) | copy-start | bytes 1156
  27.6 34.5 %copy-start.1 = (f32[2,64,1024]{2,1,0:T(8,128)S(1)}, f32[2,64,1024]{2,1,0:T(8,128)}, u32[]{:S(2)}) copy-start(f32[2,64,1024]{2,1,0:T(8,128)} %fixed.1) | copy-start | bytes 1572868
  27.6 34.5 %copy-start.3 = (s32[1,1,32]{2,1,0:T(1,128)S(1)}, s32[1,1,32]{2,1,0:T(1,128)}, u32[]{:S(2)}) copy-start(s32[1,1,32]{2,1,0:T(1,128)} %param.12) | copy-start | bytes 388
  27.6 34.5 %copy-start.4 = (s32[1,1,32]{2,1,0:T(1,128)S(1)}, s32[1,1,32]{2,1,0:T(1,128)}, u32[]{:S(2)}) copy-start(s32[1,1,32]{2,1,0:T(1,128)} %param.13) | copy-start | bytes 388
  27.6 34.5 %copy-start.5 = (s32[1,1,32]{2,1,0:T(1,128)S(1)}, s32[1,1,32]{2,1,0:T(1,128)}, u32[]{:S(2)}) copy-start(s32[1,1,32]{2,1,0:T(1,128)} %param.14) | copy-start | bytes 388
  27.6 34.5 %all-to-all-start.1 = ((bf16[128,2,2,16,128]{4,3,2,1,0:T(8,128)(2,1)}), bf16[128,2,2,16,128]{4,3,2,1,0:T(8,128)(2,1)S(1)}, u32[]{:S(2)}, u32[]{:S(2)}) async-start(bf16[128,2,2,16,128]{4,3,2,1,0:T(8,128)(2,1)} %copy-done), calls=%async_computation.1 | async-start | bytes 4194304 | tf_op jit(solution)/shard_map/all_to_all | solution.py:549
  82.4 10.4 %collective-permute-start = (bf16[8,4,8,1024]{3,2,1,0:T(8,128)(2,1)S(1)}, bf16[8,4,8,1024]{3,2,1,0:T(8,128)(2,1)S(1)}, u32[]{:S(2)}, u32[]{:S(2)}) collective-permute-start(bf16[8,4,8,1024]{3,2,1,0:T(8,128)(2,1)S(1)} %copy.32), channel_id=1, source_target_pairs={{0,16},{16,32},{32,48},{48,64},{64,80},{80,96},{96,112},{112,113},... | collective-permute-start | bytes 1572872 | tf_op jit(solution)/shard_map/ppermute | solution.py:536
  85.5 10.9 %collective-permute-start.1 = (bf16[8,4,8,1024]{3,2,1,0:T(8,128)(2,1)S(1)}, bf16[8,4,8,1024]{3,2,1,0:T(8,128)(2,1)S(1)}, u32[]{:S(2)}, u32[]{:S(2)}) collective-permute-start(bf16[8,4,8,1024]{3,2,1,0:T(8,128)(2,1)S(1)} %copy.32), channel_id=1, source_target_pairs={{16,0},{32,16},{48,32},{64,48},{80,64},{96,80},{112,96},{113,112},... | collective-permute-start | bytes 1572872 | tf_op jit(solution)/shard_map/ppermute | solution.py:536
  87.5 31.5 %collective-permute-start.3 = (bf16[8,2,1024]{2,1,0:T(2,128)(2,1)S(1)}, bf16[8,2,1024]{2,1,0:T(2,128)(2,1)S(1)}, u32[]{:S(2)}, u32[]{:S(2)}) collective-permute-start(bf16[8,2,1024]{2,1,0:T(2,128)(2,1)S(1)} %get-tuple-element.20), channel_id=1, source_target_pairs={{32,0},{48,16},{64,32},{80,48},{96,64},{112,80},{113,96},{97,112},... | collective-permute-start | bytes 98312 | tf_op jit(solution)/shard_map/ppermute | solution.py:536
  88.8 30.2 %collective-permute-start.2 = (bf16[8,2,1024]{2,1,0:T(2,128)(2,1)S(1)}, bf16[8,2,1024]{2,1,0:T(2,128)(2,1)S(1)}, u32[]{:S(2)}, u32[]{:S(2)}) collective-permute-start(bf16[8,2,1024]{2,1,0:T(2,128)(2,1)S(1)} %get-tuple-element.21), channel_id=1, source_target_pairs={{0,32},{16,48},{32,64},{48,80},{64,96},{80,112},{96,113},{112,97},... | collective-permute-start | bytes 98312 | tf_op jit(solution)/shard_map/ppermute | solution.py:536

commit v3 on v2

--- a/solution.py
+++ b/solution.py
@@ -36,32 +36,54 @@
     return (target == (source % FINE) * 128 + source // FINE).astype(BF16)
 
 
-def pick_kernel(asked, moving, out):
-    depth = moving.shape[0]
-    along = moving.shape[2] // TZ
+def pick_kernel(asked_hbm, moving, out, asked, block, buf, loads, stores):
+    peers, slots, depth = buf.shape[:3]
+    count = stores.shape[0]
+    first = pltpu.make_async_copy(asked_hbm, asked, loads.at[0])
+    second = pltpu.make_async_copy(moving, block, loads.at[1])
+    first.start()
+    second.start()
+    first.wait()
+    second.wait()
 
     def peer(p, carry):
-        for slot in range(out.shape[1]):
+        for slot in range(slots):
             number = asked[p, slot]
             tile = jnp.maximum(number, 0)
-            rows = pl.ds(pl.multiple_of(lax.div(tile, along) * TY, TY), TY)
-            lanes = pl.ds(pl.multiple_of(lax.rem(tile, along) * TZ, TZ), TZ)
+            rows = pl.ds(pl.multiple_of(lax.shift_right_logical(tile, 3) * TY, TY), TY)
+            lanes = pl.ds(pl.multiple_of(lax.bitwise_and(tile, 7) * TZ, TZ), TZ)
             for x in range(depth):
-                cells = moving[x, rows, lanes]
-                out[p, slot, x] = jnp.where(number >= 0, cells, jnp.zeros_like(cells))
+                cells = block[x, rows, lanes]
+                buf[p, slot, x] = jnp.where(number >= 0, cells, jnp.zeros_like(cells))
         return carry
 
-    lax.fori_loop(0, out.shape[0], peer, 0, unroll=8)
+    part = peers // count
+    sent = []
+    for i in range(count):
+        lax.fori_loop(i * part, (i + 1) * part, peer, 0, unroll=8)
+        mine = pl.ds(i * part, part)
+        sent.append(pltpu.make_async_copy(buf.at[mine], out.at[mine], stores.at[i]))
+        sent[-1].start()
+    for each in sent:
+        each.wait()
 
 
 def pick(asked, moving, slots):
-    vmem = pl.BlockSpec(memory_space=pltpu.VMEM)
+    hbm = pl.BlockSpec(memory_space=pltpu.HBM)
+    shape = (asked.shape[0], slots, moving.shape[0], TY, TZ)
     return pl.pallas_call(
         pick_kernel,
-        out_shape=jax.ShapeDtypeStruct((asked.shape[0], slots, moving.shape[0], TY, TZ), BF16),
-        in_specs=[pl.BlockSpec(memory_space=pltpu.SMEM), vmem],
-        out_specs=vmem,
-        compiler_params=pltpu.CompilerParams(vmem_limit_bytes=8 * 1024 * 1024),
+        out_shape=jax.ShapeDtypeStruct(shape, BF16),
+        in_specs=[hbm, hbm],
+        out_specs=hbm,
+        scratch_shapes=[
+            pltpu.SMEM(asked.shape, jnp.int32),
+            pltpu.VMEM(moving.shape, BF16),
+            pltpu.VMEM(shape, BF16),
+            pltpu.SemaphoreType.DMA((2,)),
+            pltpu.SemaphoreType.DMA((4,)),
+        ],
+        compiler_params=pltpu.CompilerParams(vmem_limit_bytes=62 * 1024 * 1024),
         name="pick",
     )(asked, moving)
 
@@ -77,31 +99,33 @@
         return jnp.where(base == shift, here, jnp.where(base == shift + 1, after, 0.0)).astype(BF16)
 
     def tile_row(j, carry):
+        rows = pl.ds(pl.multiple_of(j * 16, 16), 16)
+        firsts = []
         for k in range(8):
             t = j * 8 + k
             sides = []
             for c in range(2):
-                sides.append(
-                    jnp.concatenate(
-                        [arrived[foot[t * 8 + 4 * a + 2 * b + c]] for a in range(2) for b in range(2)], axis=0
-                    )
-                )
-            patch = jnp.concatenate(sides, axis=1)
+                corners = [arrived[foot[t * 8 + 4 * a + 2 * b + c]] for a in range(2) for b in range(2)]
+                sides.append(jnp.concatenate(corners, axis=0))
             wz = band(base_z, oz[t], wts[t * 6 + 4], wts[t * 6 + 5])
-            first = jnp.dot(patch, wz, preferred_element_type=F32).astype(BF16)
+            firsts.append(jnp.dot(jnp.concatenate(sides, axis=1), wz, preferred_element_type=F32).astype(BF16))
+        seconds = []
+        for k in range(8):
+            t = j * 8 + k
             wy = band(base_y, oy[t], wts[t * 6 + 2], wts[t * 6 + 3])
-            second = jnp.dot(wy, first, preferred_element_type=F32).astype(BF16).astype(F32)
+            seconds.append(jnp.dot(wy, firsts[k], preferred_element_type=F32).astype(BF16).astype(F32))
+        for k in range(8):
+            t = j * 8 + k
             shift = ox[t]
+            lanes = slice(k * 128, (k + 1) * 128)
             for xo in range(2):
                 total = None
                 for p in range(xo, xo + 3):
                     weight = jnp.where(
                         p - xo == shift, wts[t * 6], jnp.where(p - xo == shift + 1, wts[t * 6 + 1], 0.0)
                     )
-                    term = weight * second[p * 16 : (p + 1) * 16]
+                    term = weight * seconds[k][p * 16 : (p + 1) * 16]
                     total = term if total is None else total + term
-                rows = pl.ds(pl.multiple_of(j * 16, 16), 16)
-                lanes = slice(k * 128, (k + 1) * 128)
                 nat[xo, rows, lanes] = total.astype(BF16)
                 nat[2 + xo, rows, lanes] = (total - fixed[xo, rows, lanes]).astype(BF16)
         return carry
@@ -216,7 +240,7 @@
             put_w(n, lambda kx: line(n, kx))
             return carry
 
-        lax.fori_loop(0, 24, fill, 0)
+        lax.fori_loop(0, 24, fill, 0, unroll=4)
 
         def begin(n, carry):
             w = load(w_s, n)
@@ -236,7 +260,7 @@
         for c in range(3):
             for n in (0, 23):
                 v0[c, n] = jnp.zeros((16, 8, 128), F32)
-        lax.fori_loop(1, 23, begin, 0)
+        lax.fori_loop(1, 23, begin, 0, unroll=2)
 
         for e, (edge, step) in enumerate(((0, 2), (23, -2))):
             w = load(w_s, edge)
@@ -277,7 +301,7 @@
                         u_s[c, n - 1, tiles] = (6.0 * v[kx, k] - total) * scale
                 return carry
 
-            lax.fori_loop(off + 1, 23 - off, first, 0)
+            lax.fori_loop(off + 1, 23 - off, first, 0, unroll=2)
 
             def second(n, carry):
                 dots = {}
@@ -297,7 +321,7 @@
                         new[c, n - off - 2, tiles] = value
                 return carry
 
-            lax.fori_loop(off + 2, 22 - off, second, 0)
+            lax.fori_loop(off + 2, 22 - off, second, 0, unroll=2)
             copy(j + 1).start()
 
         def products(n, sums):
@@ -313,7 +337,7 @@
                             sums[q] = sums[q] + jnp.sum(t * other, axis=0)
             return tuple(sums)
 
-        sums = list(lax.fori_loop(8, 16, products, tuple(jnp.zeros((8, 128), F32) for _ in range(8))))
+        sums = list(lax.fori_loop(8, 16, products, tuple(jnp.zeros((8, 128), F32) for _ in range(8)), unroll=2))
         for first_row, step in ((8, 2), (15, -2)):
             end = first_row + 4 * step
             for c in range(3):

time: 167 us -> 160 us (0.958)
  Pallas kernels: 37.9 us -> 32.5 us
  local copies, waits for them, and re-layouts: 4.15 us -> 1.88 us
    pallas_call x1, Pallas kernels: 6.91 us -> 3 us  [warp(): pl.pallas_call(warp_kernel, out_shape=jax.ShapeDtypeStruct((8, 4, 8, 1024...]
    pallas_call x1, Pallas kernels: 22.4 us -> 19.9 us  [krylov(): pl.pallas_call(krylov_kernel, out_shape=(jax.ShapeDtypeStruct((peers, 128...]
    unnamed x18 -> x14, local copies, waits for them, and re-layouts: 3.17 us -> 0.9 us
where the time goes in v3:
time: 160 us; the launch traced here: 159 us
  blocking collectives  75.8 us (47%)
  Pallas kernels  32.5 us (20%)
  waiting for transfers between devices  32.2 us (20%)
  starting transfers between devices  15 us (9%)
  local copies, waits for them, and re-layouts  1.88 us (1%)
    all_to_all x1, waiting for transfers between devices, per_device(): lax.all_to_all(outgoing, BOTH, split_axis=0, concat_axis=0, tiled=True)  28.7 us
    all_to_all x1, blocking collectives, per_device(): back = lax.all_to_all(back, 'slab', split_axis=0, concat_axis=0, tiled=True)  24.2 us
    all_to_all x1, blocking collectives, per_device(): asked = lax.all_to_all(asked, BOTH, split_axis=0, concat_axis=0, tiled=True)  21.1 us
    pallas_call x1, Pallas kernels, krylov(): pl.pallas_call(krylov_kernel, out_shape=(jax.ShapeDtypeStruct((peers, 128...  19.9 us
    all_to_all x1, blocking collectives, per_device(): lax.all_to_all(moments, BOTH, split_axis=0, concat_axis=0, tiled=True)  17.8 us
    all_to_all x1, blocking collectives, per_device(): own = lax.all_to_all(own, 'slab', split_axis=0, concat_axis=0, tiled=True)  12.8 us
    ppermute x4, starting transfers between devices, ring(): lax.ppermute(cells, BOTH, [(device(i), device(i + step)) for i in chunks])  10.3 us
    all_to_all x1, starting transfers between devices, per_device(): lax.all_to_all(outgoing, BOTH, split_axis=0, concat_axis=0, tiled=True)  4.67 us
  transfers between devices with their start and end apart: 5, of which 2 were waited for; matrix products, arithmetic and copies ran while one was open for 1% of the time, Pallas kernels for 13%

profile of v3, /device:TPU:1, one launch (start us, length us, event | category | flops | bytes accessed | tf_op | source)
XLA Modules:
  0.0 159.2 jit_solution(10731514604297632195)
XLA Ops:
  0.6 0.8 copy.20
  1.4 21.1 %all_to_all.37 = s32[128,1,128]{2,1,0:T(1,128)} all-to-all(s32[128,1,128]{2,1,0:T(1,128)S(1)} %bitcast.41), channel_id=1, replica_groups=mesh['slab'=8,'row'=16] {'slab','row'}, dimensions={0} | all-to-all | bytes 131072 | tf_op jit(solution)/shard_map/all_to_all | solution.py:571
  22.6 3.9 %pick.1 = bf16[128,2,2,16,128]{4,3,2,1,0:T(8,128)(2,1)} custom-call(s32[128,128]{1,0:T(8,128)} %bitcast.40, bf16[2,64,1024]{2,1,0:T(8,128)(2,1)} %moving.1), custom_call_target="tpu_custom_call" | custom-call | tf_op jit(solution)/shard_map/pick/pallas_call | solution.py:74
  26.5 0.0 copy-start.4
  26.5 0.0 copy-start.5
  26.5 0.0 copy-start
  26.6 0.0 copy-start.1
  26.6 0.0 copy-start.2
  26.6 0.0 copy-start.3
  26.6 4.7 %all-to-all-start.1 = ((bf16[128,2,2,16,128]{4,3,2,1,0:T(8,128)(2,1)}), bf16[128,2,2,16,128]{4,3,2,1,0:T(8,128)(2,1)S(1)}, u32[]{:S(2)}, u32[]{:S(2)}) async-start(bf16[128,2,2,16,128]{4,3,2,1,0:T(8,128)(2,1)} %pick.1), calls=%async_computation.1 | async-start | bytes 4194304 | tf_op jit(solution)/shard_map/all_to_all | solution.py:573
  31.3 0.1 copy.18
  31.4 0.1 reshape_squeeze.3.foot
  31.5 0.1 copy.19
  31.6 0.1 reshape.45.wts
  31.8 0.6 fusion.perm
  32.5 28.7 %all-to-all-done.1 = bf16[128,2,2,16,128]{4,3,2,1,0:T(8,128)(2,1)S(1)} async-done(((bf16[128,2,2,16,128]{4,3,2,1,0:T(8,128)(2,1)}), bf16[128,2,2,16,128]{4,3,2,1,0:T(8,128)(2,1)S(1)}, u32[]{:S(2)}, u32[]{:S(2)}) %all-to-all-start.1) | async-done | bytes 2097184 | tf_op jit(solution)/shard_map/all_to_all | solution.py:573
  61.2 3.0 %warp.1 = bf16[8,4,8,1024]{3,2,1,0:T(8,128)(2,1)S(1)} custom-call(s32[256]{0:T(256)S(1)} %reshape_squeeze.3.foot, s32[32]{0:T(128)S(1)} %bitcast.34, s32[32]{0:T(128)S(1)} %bitcast.35, s32[32]{0:T(128)S(1)} %bitcast.36, f32[192]{0:T(256)S(1)} %reshape.45.wts, s32[1]{0:T(128)} %bitcast.flip, bf16[256,32,128]{2,1,0:T(8,128)(2,1)S(1)} %bitcast.31, ...), custom_call_target="tpu_custom_call" | custom-call | tf_op jit(solution)/shard_map/warp/pallas_call | solution.py:149
  64.2 0.4 copy.21
  64.6 12.8 %all_to_all.38 = bf16[8,4,8,1024]{3,1,2,0:T(4,128)(2,1)S(1)} all-to-all(bf16[8,4,8,1024]{3,1,2,0:T(4,128)(2,1)S(1)} %copy.21), channel_id=1, replica_groups=mesh['slab'=8,'row'=16] {'slab'}, dimensions={0} | all-to-all | bytes 1048576 | tf_op jit(solution)/shard_map/all_to_all | solution.py:579
  77.4 0.2 copy.32
  77.5 3.1 %collective-permute-start = (bf16[8,4,8,1024]{3,2,1,0:T(8,128)(2,1)S(1)}, bf16[8,4,8,1024]{3,2,1,0:T(8,128)(2,1)S(1)}, u32[]{:S(2)}, u32[]{:S(2)}) collective-permute-start(bf16[8,4,8,1024]{3,2,1,0:T(8,128)(2,1)S(1)} %copy.32), channel_id=1, source_target_pairs={{0,16},{16,32},{32,48},{48,64},{64,80},{80,96},{96,112},{112,113},... | collective-permute-start | bytes 1572872 | tf_op jit(solution)/shard_map/ppermute | solution.py:560
  80.6 1.9 %collective-permute-start.1 = (bf16[8,4,8,1024]{3,2,1,0:T(8,128)(2,1)S(1)}, bf16[8,4,8,1024]{3,2,1,0:T(8,128)(2,1)S(1)}, u32[]{:S(2)}, u32[]{:S(2)}) collective-permute-start(bf16[8,4,8,1024]{3,2,1,0:T(8,128)(2,1)S(1)} %copy.32), channel_id=1, source_target_pairs={{16,0},{32,16},{48,32},{64,48},{80,64},{96,80},{112,96},{113,112},... | collective-permute-start | bytes 1572872 | tf_op jit(solution)/shard_map/ppermute | solution.py:560
  82.7 1.3 collective-permute-start.3
  84.0 4.0 %collective-permute-start.2 = (bf16[8,2,1024]{2,1,0:T(2,128)(2,1)S(1)}, bf16[8,2,1024]{2,1,0:T(2,128)(2,1)S(1)}, u32[]{:S(2)}, u32[]{:S(2)}) collective-permute-start(bf16[8,2,1024]{2,1,0:T(2,128)(2,1)S(1)} %get-tuple-element.21), channel_id=1, source_target_pairs={{0,32},{16,48},{32,64},{48,80},{64,96},{80,112},{96,113},{112,97},... | collective-permute-start | bytes 98312 | tf_op jit(solution)/shard_map/ppermute | solution.py:560
  88.0 3.5 %collective-permute-done.1 = bf16[8,4,8,1024]{3,2,1,0:T(8,128)(2,1)S(1)} collective-permute-done((bf16[8,4,8,1024]{3,2,1,0:T(8,128)(2,1)S(1)}, bf16[8,4,8,1024]{3,2,1,0:T(8,128)(2,1)S(1)}, u32[]{:S(2)}, u32[]{:S(2)}) %collective-permute-start.1) | collective-permute-done | bytes 524320 | tf_op jit(solution)/shard_map/ppermute | solution.py:560
  91.5 0.2 pad_maximum_fusion.chunk3
  91.7 19.9 %krylov.1 = (f32[128,128]{1,0:T(8,128)S(1)}, f32[5,3,8,16,8,128]{5,4,3,2,1,0:T(8,128)S(1)}, f32[3,8,16,8,128]{4,3,2,1,0:T(8,128)S(1)}, f32[2,5,128,128]{3,2,1,0:T(8,128)S(1)}) custom-call(f32[24]{0:T(128)S(1)} %and_convert_fusion.rowmask, bf16[3,8,4,8,1024]{4,3,2,1,0:T(8,128)(2,1)S(1)} %pad_maximum_fusion.chunk3), custom_call_target="tpu_custom_call" | custom-call | flops 400000000 | bytes 60000000 | tf_op jit(solution)/shard_map/krylov/pallas_call | solution.py:372
  111.6 0.1 outer_rows.1.outer
  111.7 17.8 %all_to_all.39 = f32[128,1,128]{2,1,0:T(1,128)S(1)} all-to-all(f32[128,1,128]{2,1,0:T(1,128)S(1)} %bitcast.33), channel_id=1, replica_groups=mesh['slab'=8,'row'=16] {'slab','row'}, dimensions={0} | all-to-all | bytes 131072 | tf_op jit(solution)/shard_map/all_to_all | solution.py:588
  129.5 2.6 %combine.1 = bf16[8,2,3,16,1024]{4,3,2,1,0:T(8,128)(2,1)S(1)} custom-call(f32[128,128]{1,0:T(8,128)S(1)} %bitcast.32, f32[5,3,8,16,8,128]{5,4,3,2,1,0:T(8,128)S(1)} %get-tuple-element.17.v_hbm, f32[3,8,16,8,128]{4,3,2,1,0:T(8,128)S(1)} %get-tuple-element.18.s_hbm, f32[2,3,128,128]{3,2,1,0:T(8,128)S(1)} %outer_rows.1.outer), custom_call_target="tpu_custom_call" | custom-call | tf_op jit(solution)/shard_map/combine/pallas_call | solution.py:505
  132.1 24.2 %all_to_all.40.back = bf16[8,2,3,16,1024]{4,3,2,1,0:T(8,128)(2,1)S(1)} all-to-all(bf16[8,2,3,16,1024]{4,3,2,1,0:T(8,128)(2,1)S(1)} %combine.1), channel_id=1, replica_groups=mesh['slab'=8,'row'=16] {'slab'}, dimensions={0} | all-to-all | bytes 3145728 | tf_op jit(solution)/shard_map/all_to_all | solution.py:590
  156.3 2.9 %finish.1 = (f32[3,2,64,1024]{3,2,1,0:T(8,128)}, f32[3,2,64,1024]{3,2,1,0:T(8,128)}) custom-call(s32[1]{0:T(128)} %bitcast.flip, bf16[8,2,3,16,1024]{4,3,2,1,0:T(8,128)(2,1)S(1)} %all_to_all.40.back, bf16[512,512]{1,0:T(8,128)(2,1)S(1)} %fusion.perm), custom_call_target="tpu_custom_call" | custom-call | tf_op jit(solution)/shard_map/finish/pallas_call | solution.py:537
  (17 shorter events, 0.1 us)
Async XLA Ops:
  26.5 4.8 %copy-start.4 = (s32[1,1,32,8]{2,3,1,0:T(8,128)S(1)}, s32[1,1,32,8]{2,3,1,0:T(8,128)}, u32[]{:S(2)}) copy-start(s32[1,1,32,8]{2,3,1,0:T(8,128)} %param.11) | copy-start | bytes 3076
  26.5 4.9 %copy-start.5 = (f32[1,1,32,3]{2,1,3,0:T(1,128)S(1)}, f32[1,1,32,3]{2,1,3,0:T(1,128)}, u32[]{:S(2)}) copy-start(f32[1,1,32,3]{2,1,3,0:T(1,128)} %param.15) | copy-start | bytes 1156
  26.5 34.6 %copy-start = (f32[2,64,1024]{2,1,0:T(8,128)S(1)}, f32[2,64,1024]{2,1,0:T(8,128)}, u32[]{:S(2)}) copy-start(f32[2,64,1024]{2,1,0:T(8,128)} %fixed.1) | copy-start | bytes 1572868
  26.6 34.6 %copy-start.1 = (s32[1,1,32]{2,1,0:T(1,128)S(1)}, s32[1,1,32]{2,1,0:T(1,128)}, u32[]{:S(2)}) copy-start(s32[1,1,32]{2,1,0:T(1,128)} %param.12) | copy-start | bytes 388
  26.6 34.6 %copy-start.2 = (s32[1,1,32]{2,1,0:T(1,128)S(1)}, s32[1,1,32]{2,1,0:T(1,128)}, u32[]{:S(2)}) copy-start(s32[1,1,32]{2,1,0:T(1,128)} %param.13) | copy-start | bytes 388
  26.6 34.6 %copy-start.3 = (s32[1,1,32]{2,1,0:T(1,128)S(1)}, s32[1,1,32]{2,1,0:T(1,128)}, u32[]{:S(2)}) copy-start(s32[1,1,32]{2,1,0:T(1,128)} %param.14) | copy-start | bytes 388
  26.6 34.5 %all-to-all-start.1 = ((bf16[128,2,2,16,128]{4,3,2,1,0:T(8,128)(2,1)}), bf16[128,2,2,16,128]{4,3,2,1,0:T(8,128)(2,1)S(1)}, u32[]{:S(2)}, u32[]{:S(2)}) async-start(bf16[128,2,2,16,128]{4,3,2,1,0:T(8,128)(2,1)} %pick.1), calls=%async_computation.1 | async-start | bytes 4194304 | tf_op jit(solution)/shard_map/all_to_all | solution.py:573
  77.5 10.4 %collective-permute-start = (bf16[8,4,8,1024]{3,2,1,0:T(8,128)(2,1)S(1)}, bf16[8,4,8,1024]{3,2,1,0:T(8,128)(2,1)S(1)}, u32[]{:S(2)}, u32[]{:S(2)}) collective-permute-start(bf16[8,4,8,1024]{3,2,1,0:T(8,128)(2,1)S(1)} %copy.32), channel_id=1, source_target_pairs={{0,16},{16,32},{32,48},{48,64},{64,80},{80,96},{96,112},{112,113},... | collective-permute-start | bytes 1572872 | tf_op jit(solution)/shard_map/ppermute | solution.py:560
  80.6 10.9 %collective-permute-start.1 = (bf16[8,4,8,1024]{3,2,1,0:T(8,128)(2,1)S(1)}, bf16[8,4,8,1024]{3,2,1,0:T(8,128)(2,1)S(1)}, u32[]{:S(2)}, u32[]{:S(2)}) collective-permute-start(bf16[8,4,8,1024]{3,2,1,0:T(8,128)(2,1)S(1)} %copy.32), channel_id=1, source_target_pairs={{16,0},{32,16},{48,32},{64,48},{80,64},{96,80},{112,96},{113,112},... | collective-permute-start | bytes 1572872 | tf_op jit(solution)/shard_map/ppermute | solution.py:560
  82.7 28.9 %collective-permute-start.3 = (bf16[8,2,1024]{2,1,0:T(2,128)(2,1)S(1)}, bf16[8,2,1024]{2,1,0:T(2,128)(2,1)S(1)}, u32[]{:S(2)}, u32[]{:S(2)}) collective-permute-start(bf16[8,2,1024]{2,1,0:T(2,128)(2,1)S(1)} %get-tuple-element.20), channel_id=1, source_target_pairs={{32,0},{48,16},{64,32},{80,48},{96,64},{112,80},{113,96},{97,112},... | collective-permute-start | bytes 98312 | tf_op jit(solution)/shard_map/ppermute | solution.py:560
  84.0 27.7 %collective-permute-start.2 = (bf16[8,2,1024]{2,1,0:T(2,128)(2,1)S(1)}, bf16[8,2,1024]{2,1,0:T(2,128)(2,1)S(1)}, u32[]{:S(2)}, u32[]{:S(2)}) collective-permute-start(bf16[8,2,1024]{2,1,0:T(2,128)(2,1)S(1)} %get-tuple-element.21), channel_id=1, source_target_pairs={{0,32},{16,48},{32,64},{48,80},{64,96},{80,112},{96,113},{112,97},... | collective-permute-start | bytes 98312 | tf_op jit(solution)/shard_map/ppermute | solution.py:560

commit v4 on v3

--- a/solution.py
+++ b/solution.py
@@ -207,7 +207,7 @@
     return pltpu.VMEM((3, rows, 16, 8, 128), F32)
 
 
-def krylov_kernel(rowmask, chunk3, mom, vout, sout, ends, s_s, im_s, v0, v1, v2, sems):
+def krylov_kernel(place, rowmask, chunks, mom, vout, sout, ends, s_s, im_s, v0, v1, v2, sems):
     masks = edge_masks()
 
     def chain(c, tiles, end, step):
@@ -215,11 +215,13 @@
         return one * (im_s[c, end - 2 * step, tiles] * im_s[c, end - 3 * step, tiles]) * REACH
 
     def prepare(in_s, d_s, w_s, in_sems):
-        chunks = [pltpu.make_async_copy(ref, in_s.at[g], in_sems.at[g]) for g, ref in enumerate((chunk3.at[0], chunk3.at[1], chunk3.at[2]))]
-        for chunk in chunks:
-            chunk.start()
+        odd = lax.bitwise_and(place[0], 1)
+        sources = (2 - 2 * odd, 1, 2 * odd)
+        loads = [pltpu.make_async_copy(chunks.at[src], in_s.at[g], in_sems.at[g]) for g, src in enumerate(sources)]
+        for each in loads:
+            each.start()
         for g in (1, 0, 2):
-            chunks[g].wait()
+            loads[g].wait()
             for src in range(8):
                 lines = in_s[g, src].astype(F32).reshape(32, 1024)
                 for kz in range(8):
@@ -365,7 +367,7 @@
     pl.run_scoped(iterate, field(22), field(12), field(8))
 
 
-def krylov(chunks, rowmask, peers):
+def krylov(chunks, place, rowmask, peers):
     vmem = pl.BlockSpec(memory_space=pltpu.VMEM)
     hbm = pl.BlockSpec(memory_space=pltpu.HBM)
 
@@ -377,7 +379,7 @@
             jax.ShapeDtypeStruct((3, 8, 16, 8, 128), F32),
             jax.ShapeDtypeStruct((2, 5, 128, 128), F32),
         ),
-        in_specs=[pl.BlockSpec(memory_space=pltpu.SMEM)] + [hbm],
+        in_specs=[pl.BlockSpec(memory_space=pltpu.SMEM)] * 2 + [hbm],
         out_specs=(vmem, hbm, hbm, vmem),
         scratch_shapes=[
             field(24),
@@ -390,12 +392,14 @@
         compiler_params=pltpu.CompilerParams(vmem_limit_bytes=31 * 1024 * 1024),
         cost_estimate=pl.CostEstimate(flops=400_000_000, bytes_accessed=60_000_000, transcendentals=0),
         name="krylov",
-    )(rowmask, *chunks)
-
-
-def ends_kernel(ends, far0, far1, out, rows):
-    for e, far in enumerate((far0, far1)):
-        lines = far[...].astype(F32).reshape(16, 1024)
+    )(place, rowmask, chunks)
+
+
+def ends_kernel(place, ends, inner, outer, out, rows):
+    upper = lax.bitwise_and(place[0], 2) == 2
+    both = [x[...].astype(F32).reshape(16, 1024) for x in (inner, outer)]
+    for e in range(2):
+        lines = jnp.where(upper, both[e], both[1 - e])
         for kz in range(8):
             rows[kz] = lines[:, kz * 128 : kz * 128 + 128]
         for slot, c in ((0, 0), (1, 2)):
@@ -410,17 +414,17 @@
                 out[e, 1, at, :] = ends[e, 2, at, :] * start
 
 
-def outer_rows(ends, far0, far1):
+def outer_rows(ends, place, inner, outer):
     vmem = pl.BlockSpec(memory_space=pltpu.VMEM)
     return pl.pallas_call(
         ends_kernel,
         out_shape=jax.ShapeDtypeStruct((2, 3, 128, 128), F32),
-        in_specs=[vmem] * 3,
+        in_specs=[pl.BlockSpec(memory_space=pltpu.SMEM)] + [vmem] * 3,
         out_specs=vmem,
         scratch_shapes=[pltpu.VMEM((8, 16, 128), F32)],
         compiler_params=pltpu.CompilerParams(vmem_limit_bytes=4 * 1024 * 1024),
         name="outer_rows",
-    )(ends, far0, far1)
+    )(place, ends, inner, outer)
 
 
 def coefficients(m):
@@ -549,15 +553,20 @@
     )(flip, back, perm)
 
 
-def ring(cells, step):
+def exchange(cells, distance, inner):
     slabs, rows = lax.axis_size("slab"), lax.axis_size("row")
 
     def device(chunk):
         row, place = chunk // slabs, chunk % slabs
         return (place if row % 2 == 0 else slabs - 1 - place) * rows + row
 
-    chunks = range(max(0, -step), slabs * rows - max(0, step))
-    return lax.ppermute(cells, BOTH, [(device(i), device(i + step)) for i in chunks])
+    pairs = []
+    for i in range(slabs * rows):
+        low = (i // distance) % 2 == 0
+        other = i + distance if low == inner else i - distance
+        if 0 <= other < slabs * rows:
+            pairs.append((device(i), device(other)))
+    return lax.ppermute(cells, BOTH, pairs)
 
 
 def per_device(moving, fixed, requests, footpoints, offset_x, offset_y, offset_z, fractions):
@@ -577,13 +586,17 @@
         arrived, footpoints[0, 0], offset_x[0, 0], offset_y[0, 0], offset_z[0, 0], fractions[0, 0], flip, fixed, perm
     )
     own = lax.all_to_all(own, "slab", split_axis=0, concat_axis=0, tiled=True)
-    chunks = (jnp.stack([ring(own, 1), own, ring(own, -1)]),)
+    chunks = jnp.stack([exchange(own, 1, True), own, exchange(own, 1, False)])
+    place = (slab + flip[0] * (7 - 2 * slab)).reshape(1)
     rows = start + jnp.arange(24, dtype=jnp.int32)
     rowmask = ((rows >= 0) & (rows < height * lax.axis_size("row"))).astype(F32)
-    moments, vectors, slopes, ends = krylov(chunks, rowmask, peers)
-    far = (ring(own[:, 0:2, 7], 2), ring(own[:, 0:2, 0], -2))
+    moments, vectors, slopes, ends = krylov(chunks, place, rowmask, peers)
+    upper = place[0] // 2 % 2 == 1
+    inwards = jnp.where(upper, own[:, 0:2, 0], own[:, 0:2, 7])
+    outwards = jnp.where(upper, own[:, 0:2, 7], own[:, 0:2, 0])
+    far = (exchange(inwards, 2, True), exchange(outwards, 2, False))
     moments, far = lax.optimization_barrier((moments, far))
-    outer = outer_rows(ends, *far)
+    outer = outer_rows(ends, place, *far)
     moments, outer = lax.optimization_barrier((moments, outer))
     moments = lax.all_to_all(moments, BOTH, split_axis=0, concat_axis=0, tiled=True)
     back = combine(moments, vectors, slopes, outer)

time: 160 us -> 155 us (0.969)
  starting transfers between devices: 15 us -> 11.3 us
  blocking collectives: 75.8 us -> 73 us
    ppermute x4, starting transfers between devices: 10.3 us -> 6.66 us  [exchange(): return lax.ppermute(cells, BOTH, pairs)]
    all_to_all x1, blocking collectives: 17.8 us -> 14.9 us  [per_device(): lax.all_to_all(moments, BOTH, split_axis=0, concat_axis=0, tiled=True)]
    ppermute x4, waiting for transfers between devices: 3.54 us -> 5.16 us  [exchange(): return lax.ppermute(cells, BOTH, pairs)]
where the time goes in v4:
time: 155 us; the launch traced here: 154 us
  blocking collectives  73 us (47%)
  waiting for transfers between devices  33.8 us (22%)
  Pallas kernels  32.5 us (21%)
  starting transfers between devices  11.3 us (7%)
  local copies, waits for them, and re-layouts  1.83 us (1%)
    all_to_all x1, waiting for transfers between devices, per_device(): lax.all_to_all(outgoing, BOTH, split_axis=0, concat_axis=0, tiled=True)  28.7 us
    all_to_all x1, blocking collectives, per_device(): back = lax.all_to_all(back, 'slab', split_axis=0, concat_axis=0, tiled=True)  24.2 us
    all_to_all x1, blocking collectives, per_device(): asked = lax.all_to_all(asked, BOTH, split_axis=0, concat_axis=0, tiled=True)  21.1 us
    pallas_call x1, Pallas kernels, krylov(): pl.pallas_call(krylov_kernel, out_shape=(jax.ShapeDtypeStruct((peers, 128...  19.9 us
    all_to_all x1, blocking collectives, per_device(): lax.all_to_all(moments, BOTH, split_axis=0, concat_axis=0, tiled=True)  14.9 us
    all_to_all x1, blocking collectives, per_device(): own = lax.all_to_all(own, 'slab', split_axis=0, concat_axis=0, tiled=True)  12.8 us
    ppermute x4, starting transfers between devices, exchange(): return lax.ppermute(cells, BOTH, pairs)  6.66 us
    ppermute x4, waiting for transfers between devices, exchange(): return lax.ppermute(cells, BOTH, pairs)  5.16 us
  transfers between devices with their start and end apart: 5, of which 2 were waited for; matrix products, arithmetic and copies ran while one was open for 1% of the time, Pallas kernels for 13%

profile of v4, /device:TPU:1, one launch (start us, length us, event | category | flops | bytes accessed | tf_op | source)
XLA Modules:
  0.0 154.3 jit_solution(2695083516783224117)
XLA Ops:
  0.6 0.8 copy.20
  1.4 21.1 %all_to_all.37 = s32[128,1,128]{2,1,0:T(1,128)} all-to-all(s32[128,1,128]{2,1,0:T(1,128)S(1)} %bitcast.50), channel_id=1, replica_groups=mesh['slab'=8,'row'=16] {'slab','row'}, dimensions={0} | all-to-all | bytes 131072 | tf_op jit(solution)/shard_map/all_to_all | solution.py:580
  22.6 3.9 %pick.1 = bf16[128,2,2,16,128]{4,3,2,1,0:T(8,128)(2,1)} custom-call(s32[128,128]{1,0:T(8,128)} %bitcast.49, bf16[2,64,1024]{2,1,0:T(8,128)(2,1)} %moving.1), custom_call_target="tpu_custom_call" | custom-call | tf_op jit(solution)/shard_map/pick/pallas_call | solution.py:74
  26.5 0.0 copy-start.4
  26.5 0.0 copy-start.5
  26.5 0.0 copy-start
  26.6 0.0 copy-start.1
  26.6 0.0 copy-start.2
  26.6 4.7 %all-to-all-start.1 = ((bf16[128,2,2,16,128]{4,3,2,1,0:T(8,128)(2,1)}), bf16[128,2,2,16,128]{4,3,2,1,0:T(8,128)(2,1)S(1)}, u32[]{:S(2)}, u32[]{:S(2)}) async-start(bf16[128,2,2,16,128]{4,3,2,1,0:T(8,128)(2,1)} %pick.1), calls=%async_computation.1 | async-start | bytes 4194304 | tf_op jit(solution)/shard_map/all_to_all | solution.py:582
  31.3 0.1 copy.18
  31.4 0.1 reshape_squeeze.3.foot
  31.5 0.1 copy.19
  31.6 0.1 reshape.53.wts
  31.8 0.6 fusion.perm
  32.5 28.7 %all-to-all-done.1 = bf16[128,2,2,16,128]{4,3,2,1,0:T(8,128)(2,1)S(1)} async-done(((bf16[128,2,2,16,128]{4,3,2,1,0:T(8,128)(2,1)}), bf16[128,2,2,16,128]{4,3,2,1,0:T(8,128)(2,1)S(1)}, u32[]{:S(2)}, u32[]{:S(2)}) %all-to-all-start.1) | async-done | bytes 2097184 | tf_op jit(solution)/shard_map/all_to_all | solution.py:582
  61.2 3.0 %warp.1 = bf16[8,4,8,1024]{3,2,1,0:T(8,128)(2,1)S(1)} custom-call(s32[256]{0:T(256)S(1)} %reshape_squeeze.3.foot, s32[32]{0:T(128)S(1)} %bitcast.43, s32[32]{0:T(128)S(1)} %bitcast.44, s32[32]{0:T(128)S(1)} %bitcast.45, f32[192]{0:T(256)S(1)} %reshape.53.wts, s32[1]{0:T(128)} %bitcast.flip, bf16[256,32,128]{2,1,0:T(8,128)(2,1)S(1)} %bitcast.40, ...), custom_call_target="tpu_custom_call" | custom-call | tf_op jit(solution)/shard_map/warp/pallas_call | solution.py:149
  64.2 0.4 copy.21
  64.6 12.8 %all_to_all.38 = bf16[8,4,8,1024]{3,1,2,0:T(4,128)(2,1)S(1)} all-to-all(bf16[8,4,8,1024]{3,1,2,0:T(4,128)(2,1)S(1)} %copy.21), channel_id=1, replica_groups=mesh['slab'=8,'row'=16] {'slab'}, dimensions={0} | all-to-all | bytes 1048576 | tf_op jit(solution)/shard_map/all_to_all | solution.py:588
  77.4 0.2 copy.32
  77.5 1.1 collective-permute-start
  78.6 2.1 %collective-permute-start.1 = (bf16[8,4,8,1024]{3,2,1,0:T(8,128)(2,1)S(1)}, bf16[8,4,8,1024]{3,2,1,0:T(8,128)(2,1)S(1)}, u32[]{:S(2)}, u32[]{:S(2)}) collective-permute-start(bf16[8,4,8,1024]{3,2,1,0:T(8,128)(2,1)S(1)} %copy.32), channel_id=1, source_target_pairs={{16,32},{32,16},{48,64},{64,48},{80,96},{96,80},{112,113},{113,112... | collective-permute-start | bytes 1572872 | tf_op jit(solution)/shard_map/ppermute | solution.py:569
  80.8 0.1 fusion.2
  80.9 0.7 collective-permute-start.3
  81.5 2.8 %collective-permute-start.2 = (bf16[8,2,1024]{2,1,0:T(2,128)(2,1)S(1)}, bf16[8,2,1024]{2,1,0:T(2,128)(2,1)S(1)}, u32[]{:S(2)}, u32[]{:S(2)}) collective-permute-start(bf16[8,2,1024]{2,1,0:T(2,128)(2,1)S(1)} %get-tuple-element.21), channel_id=1, source_target_pairs={{0,32},{16,48},{32,0},{48,16},{64,96},{80,112},{96,64},{112,80},{1... | collective-permute-start | bytes 98312 | tf_op jit(solution)/shard_map/ppermute | solution.py:569
  84.3 5.2 %collective-permute-done.1 = bf16[8,4,8,1024]{3,2,1,0:T(8,128)(2,1)S(1)} collective-permute-done((bf16[8,4,8,1024]{3,2,1,0:T(8,128)(2,1)S(1)}, bf16[8,4,8,1024]{3,2,1,0:T(8,128)(2,1)S(1)}, u32[]{:S(2)}, u32[]{:S(2)}) %collective-permute-start.1) | collective-permute-done | bytes 524320 | tf_op jit(solution)/shard_map/ppermute | solution.py:569
  89.5 0.2 pad_maximum_fusion.chunks
  89.7 19.9 %krylov.1 = (f32[128,128]{1,0:T(8,128)S(1)}, f32[5,3,8,16,8,128]{5,4,3,2,1,0:T(8,128)S(1)}, f32[3,8,16,8,128]{4,3,2,1,0:T(8,128)S(1)}, f32[2,5,128,128]{3,2,1,0:T(8,128)S(1)}) custom-call(s32[1]{0:T(128)} %bitcast.1.place, f32[24]{0:T(128)S(1)} %and_convert_fusion.rowmask, bf16[3,8,4,8,1024]{4,3,2,1,0:T(8,128)(2,1)S(1)} %pad_maximum_fusion.chunks), custom_call_target="tpu_custom_call" | custom-call | flops 400000000 | bytes 60000000 | tf_op jit(solution)/shard_map/krylov/pallas_call | solution.py:374
  109.6 0.1 outer_rows.1.outer
  109.7 14.9 %all_to_all.39 = f32[128,1,128]{2,1,0:T(1,128)S(1)} all-to-all(f32[128,1,128]{2,1,0:T(1,128)S(1)} %bitcast.42), channel_id=1, replica_groups=mesh['slab'=8,'row'=16] {'slab','row'}, dimensions={0} | all-to-all | bytes 131072 | tf_op jit(solution)/shard_map/all_to_all | solution.py:601
  124.6 2.6 %combine.1 = bf16[8,2,3,16,1024]{4,3,2,1,0:T(8,128)(2,1)S(1)} custom-call(f32[128,128]{1,0:T(8,128)S(1)} %bitcast.41, f32[5,3,8,16,8,128]{5,4,3,2,1,0:T(8,128)S(1)} %get-tuple-element.17.v_hbm, f32[3,8,16,8,128]{4,3,2,1,0:T(8,128)S(1)} %get-tuple-element.18.s_hbm, f32[2,3,128,128]{3,2,1,0:T(8,128)S(1)} %outer_rows.1.outer), custom_call_target="tpu_custom_call" | custom-call | tf_op jit(solution)/shard_map/combine/pallas_call | solution.py:509
  127.2 24.2 %all_to_all.40.back = bf16[8,2,3,16,1024]{4,3,2,1,0:T(8,128)(2,1)S(1)} all-to-all(bf16[8,2,3,16,1024]{4,3,2,1,0:T(8,128)(2,1)S(1)} %combine.1), channel_id=1, replica_groups=mesh['slab'=8,'row'=16] {'slab'}, dimensions={0} | all-to-all | bytes 3145728 | tf_op jit(solution)/shard_map/all_to_all | solution.py:603
  151.4 2.9 %finish.1 = (f32[3,2,64,1024]{3,2,1,0:T(8,128)}, f32[3,2,64,1024]{3,2,1,0:T(8,128)}) custom-call(s32[1]{0:T(128)} %bitcast.flip, bf16[8,2,3,16,1024]{4,3,2,1,0:T(8,128)(2,1)S(1)} %all_to_all.40.back, bf16[512,512]{1,0:T(8,128)(2,1)S(1)} %fusion.perm), custom_call_target="tpu_custom_call" | custom-call | tf_op jit(solution)/shard_map/finish/pallas_call | solution.py:541
  (17 shorter events, 0.1 us)
Async XLA Ops:
  26.5 4.8 %copy-start.4 = (s32[1,1,32,8]{2,3,1,0:T(8,128)S(1)}, s32[1,1,32,8]{2,3,1,0:T(8,128)}, u32[]{:S(2)}) copy-start(s32[1,1,32,8]{2,3,1,0:T(8,128)} %param.11) | copy-start | bytes 3076
  26.5 4.9 %copy-start.5 = (f32[1,1,32,3]{2,1,3,0:T(1,128)S(1)}, f32[1,1,32,3]{2,1,3,0:T(1,128)}, u32[]{:S(2)}) copy-start(f32[1,1,32,3]{2,1,3,0:T(1,128)} %param.15) | copy-start | bytes 1156
  26.5 34.6 %copy-start = (f32[2,64,1024]{2,1,0:T(8,128)S(1)}, f32[2,64,1024]{2,1,0:T(8,128)}, u32[]{:S(2)}) copy-start(f32[2,64,1024]{2,1,0:T(8,128)} %fixed.1) | copy-start | bytes 1572868
  26.6 34.6 %copy-start.1 = (s32[1,1,32]{2,1,0:T(1,128)S(1)}, s32[1,1,32]{2,1,0:T(1,128)}, u32[]{:S(2)}) copy-start(s32[1,1,32]{2,1,0:T(1,128)} %param.12) | copy-start | bytes 388
  26.6 34.6 %copy-start.2 = (s32[1,1,32]{2,1,0:T(1,128)S(1)}, s32[1,1,32]{2,1,0:T(1,128)}, u32[]{:S(2)}) copy-start(s32[1,1,32]{2,1,0:T(1,128)} %param.13) | copy-start | bytes 388
  26.6 34.6 %copy-start.3 = (s32[1,1,32]{2,1,0:T(1,128)S(1)}, s32[1,1,32]{2,1,0:T(1,128)}, u32[]{:S(2)}) copy-start(s32[1,1,32]{2,1,0:T(1,128)} %param.14) | copy-start | bytes 388
  26.6 34.5 %all-to-all-start.1 = ((bf16[128,2,2,16,128]{4,3,2,1,0:T(8,128)(2,1)}), bf16[128,2,2,16,128]{4,3,2,1,0:T(8,128)(2,1)S(1)}, u32[]{:S(2)}, u32[]{:S(2)}) async-start(bf16[128,2,2,16,128]{4,3,2,1,0:T(8,128)(2,1)} %pick.1), calls=%async_computation.1 | async-start | bytes 4194304 | tf_op jit(solution)/shard_map/all_to_all | solution.py:582
  77.5 6.8 %collective-permute-start = (bf16[8,4,8,1024]{3,2,1,0:T(8,128)(2,1)S(1)}, bf16[8,4,8,1024]{3,2,1,0:T(8,128)(2,1)S(1)}, u32[]{:S(2)}, u32[]{:S(2)}) collective-permute-start(bf16[8,4,8,1024]{3,2,1,0:T(8,128)(2,1)S(1)} %copy.32), channel_id=1, source_target_pairs={{0,16},{16,0},{32,48},{48,32},{64,80},{80,64},{96,112},{112,96},{1... | collective-permute-start | bytes 1572872 | tf_op jit(solution)/shard_map/ppermute | solution.py:569
  78.6 10.8 %collective-permute-start.1 = (bf16[8,4,8,1024]{3,2,1,0:T(8,128)(2,1)S(1)}, bf16[8,4,8,1024]{3,2,1,0:T(8,128)(2,1)S(1)}, u32[]{:S(2)}, u32[]{:S(2)}) collective-permute-start(bf16[8,4,8,1024]{3,2,1,0:T(8,128)(2,1)S(1)} %copy.32), channel_id=1, source_target_pairs={{16,32},{32,16},{48,64},{64,48},{80,96},{96,80},{112,113},{113,112... | collective-permute-start | bytes 1572872 | tf_op jit(solution)/shard_map/ppermute | solution.py:569
  80.9 28.7 %collective-permute-start.3 = (bf16[8,2,1024]{2,1,0:T(2,128)(2,1)S(1)}, bf16[8,2,1024]{2,1,0:T(2,128)(2,1)S(1)}, u32[]{:S(2)}, u32[]{:S(2)}) collective-permute-start(bf16[8,2,1024]{2,1,0:T(2,128)(2,1)S(1)} %get-tuple-element.20), channel_id=1, source_target_pairs={{32,64},{48,80},{64,32},{80,48},{96,113},{112,97},{113,96},{97,112... | collective-permute-start | bytes 98312 | tf_op jit(solution)/shard_map/ppermute | solution.py:569
  81.5 28.0 %collective-permute-start.2 = (bf16[8,2,1024]{2,1,0:T(2,128)(2,1)S(1)}, bf16[8,2,1024]{2,1,0:T(2,128)(2,1)S(1)}, u32[]{:S(2)}, u32[]{:S(2)}) collective-permute-start(bf16[8,2,1024]{2,1,0:T(2,128)(2,1)S(1)} %get-tuple-element.21), channel_id=1, source_target_pairs={{0,32},{16,48},{32,0},{48,16},{64,96},{80,112},{96,64},{112,80},{1... | collective-permute-start | bytes 98312 | tf_op jit(solution)/shard_map/ppermute | solution.py:569

commit v5 on v4

--- a/solution.py
+++ b/solution.py
@@ -214,16 +214,12 @@
         one = im_s[c, end, tiles] * im_s[c, end - step, tiles]
         return one * (im_s[c, end - 2 * step, tiles] * im_s[c, end - 3 * step, tiles]) * REACH
 
-    def prepare(in_s, d_s, w_s, in_sems):
+    def prepare(d_s, w_s):
         odd = lax.bitwise_and(place[0], 1)
         sources = (2 - 2 * odd, 1, 2 * odd)
-        loads = [pltpu.make_async_copy(chunks.at[src], in_s.at[g], in_sems.at[g]) for g, src in enumerate(sources)]
-        for each in loads:
-            each.start()
-        for g in (1, 0, 2):
-            loads[g].wait()
+        for g in range(3):
             for src in range(8):
-                lines = in_s[g, src].astype(F32).reshape(32, 1024)
+                lines = chunks[sources[g], src].astype(F32).reshape(32, 1024)
                 for kz in range(8):
                     d_s[kz, src * 96 + g * 32 : src * 96 + g * 32 + 32, :] = lines[:, kz * 128 : kz * 128 + 128]
 
@@ -359,10 +355,8 @@
 
     pl.run_scoped(
         prepare,
-        pltpu.VMEM((3, 8, 4, 8, 1024), BF16),
         pltpu.VMEM((8, 768, 128), F32),
         pltpu.VMEM((24, 16, 8, 128), F32),
-        pltpu.SemaphoreType.DMA((3,)),
     )
     pl.run_scoped(iterate, field(22), field(12), field(8))
 
@@ -379,7 +373,7 @@
             jax.ShapeDtypeStruct((3, 8, 16, 8, 128), F32),
             jax.ShapeDtypeStruct((2, 5, 128, 128), F32),
         ),
-        in_specs=[pl.BlockSpec(memory_space=pltpu.SMEM)] * 2 + [hbm],
+        in_specs=[pl.BlockSpec(memory_space=pltpu.SMEM)] * 2 + [vmem],
         out_specs=(vmem, hbm, hbm, vmem),
         scratch_shapes=[
             field(24),
@@ -389,7 +383,7 @@
             field(16),
             pltpu.SemaphoreType.DMA((6,)),
         ],
-        compiler_params=pltpu.CompilerParams(vmem_limit_bytes=31 * 1024 * 1024),
+        compiler_params=pltpu.CompilerParams(vmem_limit_bytes=33 * 1024 * 1024),
         cost_estimate=pl.CostEstimate(flops=400_000_000, bytes_accessed=60_000_000, transcendentals=0),
         name="krylov",
     )(place, rowmask, chunks)
@@ -454,16 +448,7 @@
     return part, rest
 
 
-def combine_kernel(mom, v_hbm, s_hbm, outer, out, v, s, turn, sems):
-    loads = []
-    for c in range(3):
-        loads.append((
-            pltpu.make_async_copy(v_hbm.at[:, c], v.at[:, c], sems.at[0, c]),
-            pltpu.make_async_copy(s_hbm.at[c], s.at[c], sems.at[1, c]),
-        ))
-    for pair in loads:
-        for each in pair:
-            each.start()
+def combine_kernel(mom, v, s, outer, out, turn):
     line = jnp.sum(mom[...], axis=0, keepdims=True)
     lane = lax.broadcasted_iota(jnp.int32, (1, 128), 1)
     p = [jnp.sum(jnp.where(lane == k, line, 0.0), axis=1, keepdims=True) for k in range(8)]
@@ -473,8 +458,6 @@
     rest = [jnp.broadcast_to(x, (8, 128)) for x in rest]
 
     for c in range(3):
-        for each in loads[c]:
-            each.wait()
 
         def row(i, carry):
             for kx, k, tiles in PARTS:
@@ -505,50 +488,47 @@
 
 def combine(moments, vectors, slopes, outer):
     vmem = pl.BlockSpec(memory_space=pltpu.VMEM)
-    hbm = pl.BlockSpec(memory_space=pltpu.HBM)
     return pl.pallas_call(
         combine_kernel,
         out_shape=jax.ShapeDtypeStruct((8, 2, 3, 16, 1024), BF16),
-        in_specs=[vmem, hbm, hbm, vmem],
+        in_specs=[vmem] * 4,
         out_specs=vmem,
-        scratch_shapes=[
-            pltpu.VMEM(vectors.shape, F32),
-            pltpu.VMEM(slopes.shape, F32),
-            pltpu.VMEM((3, 2, 8, 128, 128), F32),
-            pltpu.SemaphoreType.DMA((2, 3)),
-        ],
+        scratch_shapes=[pltpu.VMEM((3, 2, 8, 128, 128), F32)],
         compiler_params=pltpu.CompilerParams(vmem_limit_bytes=24 * 1024 * 1024),
         name="combine",
     )(moments, vectors, slopes, outer)
 
 
-def finish_kernel(flip, back, perm, sol, res):
-    lines = jnp.concatenate([back[src, q, 0] for q in range(2) for src in range(8)], axis=0)
-    lines = jnp.concatenate([lines[:, b * SPAN : b * SPAN + SPAN] for b in range(WIDE)], axis=0)
-    cells = lax.dot_general(lines, perm[...], (((1,), (1,)), ((), ())), preferred_element_type=F32)
-    for b in range(WIDE):
+def finish_kernel(flip, back, perm, sol, res, cells_s, sems):
+    stores = []
+    for c in range(3):
+        lines = jnp.concatenate([back[src, q, c] for q in range(2) for src in range(8)], axis=0)
+        lines = jnp.concatenate([lines[:, b * SPAN : b * SPAN + SPAN] for b in range(WIDE)], axis=0)
+        cells = lax.dot_general(lines, perm[...], (((1,), (1,)), ((), ())), preferred_element_type=F32)
         for q, out in ((0, sol), (1, res)):
-            for src in range(8):
-                rows = pl.ds(pl.multiple_of((src + flip[0] * (7 - 2 * src)) * 8, 8), 8)
-                for kx in range(2):
-                    at = b * 256 + q * 128 + src * 16 + kx * 8
-                    out[0, kx, rows, b * SPAN : b * SPAN + SPAN] = cells[at : at + 8]
+            for b in range(WIDE):
+                for src in range(8):
+                    rows = pl.ds(pl.multiple_of((src + flip[0] * (7 - 2 * src)) * 8, 8), 8)
+                    for kx in range(2):
+                        at = b * 256 + q * 128 + src * 16 + kx * 8
+                        cells_s[q, c, kx, rows, b * SPAN : b * SPAN + SPAN] = cells[at : at + 8]
+            stores.append(pltpu.make_async_copy(cells_s.at[q, c], out.at[c], sems.at[q, c]))
+            stores[-1].start()
+    for each in stores:
+        each.wait()
 
 
 def finish(back, flip, perm):
     shape = jax.ShapeDtypeStruct((3, 2, 64, 1024), F32)
-    spec = pl.BlockSpec((1, 2, 64, 1024), lambda c: (c, 0, 0, 0))
+    vmem = pl.BlockSpec(memory_space=pltpu.VMEM)
+    hbm = pl.BlockSpec(memory_space=pltpu.HBM)
     return pl.pallas_call(
         finish_kernel,
-        grid=(3,),
         out_shape=(shape, shape),
-        in_specs=[
-            pl.BlockSpec(memory_space=pltpu.SMEM),
-            pl.BlockSpec((8, 2, 1, 16, 1024), lambda c: (0, 0, c, 0, 0)),
-            pl.BlockSpec((SPAN, SPAN), lambda c: (0, 0)),
-        ],
-        out_specs=(spec, spec),
-        compiler_params=pltpu.CompilerParams(vmem_limit_bytes=14 * 1024 * 1024),
+        in_specs=[pl.BlockSpec(memory_space=pltpu.SMEM), vmem, vmem],
+        out_specs=(hbm, hbm),
+        scratch_shapes=[pltpu.VMEM((2, *shape.shape), F32), pltpu.SemaphoreType.DMA((2, 3))],
+        compiler_params=pltpu.CompilerParams(vmem_limit_bytes=24 * 1024 * 1024),
         name="finish",
     )(flip, back, perm)
 

time: 155 us -> 153 us (0.987)
  Pallas kernels: 32.5 us -> 30.9 us
where the time goes in v5:
time: 153 us
  blocking collectives  73 us (48%)
  waiting for transfers between devices  33.8 us (22%)
  Pallas kernels  30.9 us (20%)
  starting transfers between devices  11.3 us (7%)
  local copies, waits for them, and re-layouts  1.83 us (1%)
    all_to_all x1, waiting for transfers between devices, per_device(): lax.all_to_all(outgoing, BOTH, split_axis=0, concat_axis=0, tiled=True)  28.7 us
    all_to_all x1, blocking collectives, per_device(): back = lax.all_to_all(back, 'slab', split_axis=0, concat_axis=0, tiled=True)  24.2 us
    all_to_all x1, blocking collectives, per_device(): asked = lax.all_to_all(asked, BOTH, split_axis=0, concat_axis=0, tiled=True)  21.1 us
    pallas_call x1, Pallas kernels, krylov(): pl.pallas_call(krylov_kernel, out_shape=(jax.ShapeDtypeStruct((peers, 128...  19.8 us
    all_to_all x1, blocking collectives, per_device(): lax.all_to_all(moments, BOTH, split_axis=0, concat_axis=0, tiled=True)  14.9 us
    all_to_all x1, blocking collectives, per_device(): own = lax.all_to_all(own, 'slab', split_axis=0, concat_axis=0, tiled=True)  12.8 us
    ppermute x4, starting transfers between devices, exchange(): return lax.ppermute(cells, BOTH, pairs)  6.66 us
    ppermute x4, waiting for transfers between devices, exchange(): return lax.ppermute(cells, BOTH, pairs)  5.16 us
  transfers between devices with their start and end apart: 5, of which 2 were waited for; matrix products, arithmetic and copies ran while one was open for 1% of the time, Pallas kernels for 13%

profile of v5, /device:TPU:1, one launch (start us, length us, event | category | flops | bytes accessed | tf_op | source)
XLA Modules:
  0.0 152.7 jit_solution(16327722478207751067)
XLA Ops:
  0.6 0.8 copy.20
  1.4 21.1 %all_to_all.37 = s32[128,1,128]{2,1,0:T(1,128)} all-to-all(s32[128,1,128]{2,1,0:T(1,128)S(1)} %bitcast.50), channel_id=1, replica_groups=mesh['slab'=8,'row'=16] {'slab','row'}, dimensions={0} | all-to-all | bytes 131072 | tf_op jit(solution)/shard_map/all_to_all | solution.py:560
  22.6 3.9 %pick.1 = bf16[128,2,2,16,128]{4,3,2,1,0:T(8,128)(2,1)} custom-call(s32[128,128]{1,0:T(8,128)} %bitcast.49, bf16[2,64,1024]{2,1,0:T(8,128)(2,1)} %moving.1), custom_call_target="tpu_custom_call" | custom-call | tf_op jit(solution)/shard_map/pick/pallas_call | solution.py:74
  26.5 0.0 copy-start.4
  26.5 0.0 copy-start.5
  26.5 0.0 copy-start
  26.6 0.0 copy-start.1
  26.6 0.0 copy-start.2
  26.6 4.7 %all-to-all-start.1 = ((bf16[128,2,2,16,128]{4,3,2,1,0:T(8,128)(2,1)}), bf16[128,2,2,16,128]{4,3,2,1,0:T(8,128)(2,1)S(1)}, u32[]{:S(2)}, u32[]{:S(2)}) async-start(bf16[128,2,2,16,128]{4,3,2,1,0:T(8,128)(2,1)} %pick.1), calls=%async_computation.1 | async-start | bytes 4194304 | tf_op jit(solution)/shard_map/all_to_all | solution.py:562
  31.3 0.1 copy.18
  31.4 0.1 reshape_squeeze.3.foot
  31.5 0.1 copy.19
  31.6 0.1 reshape.53.wts
  31.8 0.6 fusion.perm
  32.5 28.7 %all-to-all-done.1 = bf16[128,2,2,16,128]{4,3,2,1,0:T(8,128)(2,1)S(1)} async-done(((bf16[128,2,2,16,128]{4,3,2,1,0:T(8,128)(2,1)}), bf16[128,2,2,16,128]{4,3,2,1,0:T(8,128)(2,1)S(1)}, u32[]{:S(2)}, u32[]{:S(2)}) %all-to-all-start.1) | async-done | bytes 2097184 | tf_op jit(solution)/shard_map/all_to_all | solution.py:562
  61.2 3.0 %warp.1 = bf16[8,4,8,1024]{3,2,1,0:T(8,128)(2,1)S(1)} custom-call(s32[256]{0:T(256)S(1)} %reshape_squeeze.3.foot, s32[32]{0:T(128)S(1)} %bitcast.43, s32[32]{0:T(128)S(1)} %bitcast.44, s32[32]{0:T(128)S(1)} %bitcast.45, f32[192]{0:T(256)S(1)} %reshape.53.wts, s32[1]{0:T(128)} %bitcast.flip, bf16[256,32,128]{2,1,0:T(8,128)(2,1)S(1)} %bitcast.40, ...), custom_call_target="tpu_custom_call" | custom-call | tf_op jit(solution)/shard_map/warp/pallas_call | solution.py:149
  64.2 0.4 copy.21
  64.6 12.8 %all_to_all.38 = bf16[8,4,8,1024]{3,1,2,0:T(4,128)(2,1)S(1)} all-to-all(bf16[8,4,8,1024]{3,1,2,0:T(4,128)(2,1)S(1)} %copy.21), channel_id=1, replica_groups=mesh['slab'=8,'row'=16] {'slab'}, dimensions={0} | all-to-all | bytes 1048576 | tf_op jit(solution)/shard_map/all_to_all | solution.py:568
  77.4 0.2 copy.32
  77.5 1.1 collective-permute-start
  78.6 2.1 %collective-permute-start.1 = (bf16[8,4,8,1024]{3,2,1,0:T(8,128)(2,1)S(1)}, bf16[8,4,8,1024]{3,2,1,0:T(8,128)(2,1)S(1)}, u32[]{:S(2)}, u32[]{:S(2)}) collective-permute-start(bf16[8,4,8,1024]{3,2,1,0:T(8,128)(2,1)S(1)} %copy.32), channel_id=1, source_target_pairs={{16,32},{32,16},{48,64},{64,48},{80,96},{96,80},{112,113},{113,112... | collective-permute-start | bytes 1572872 | tf_op jit(solution)/shard_map/ppermute | solution.py:549
  80.8 0.1 fusion.2
  80.9 0.7 collective-permute-start.3
  81.5 2.8 %collective-permute-start.2 = (bf16[8,2,1024]{2,1,0:T(2,128)(2,1)S(1)}, bf16[8,2,1024]{2,1,0:T(2,128)(2,1)S(1)}, u32[]{:S(2)}, u32[]{:S(2)}) collective-permute-start(bf16[8,2,1024]{2,1,0:T(2,128)(2,1)S(1)} %get-tuple-element.21), channel_id=1, source_target_pairs={{0,32},{16,48},{32,0},{48,16},{64,96},{80,112},{96,64},{112,80},{1... | collective-permute-start | bytes 98312 | tf_op jit(solution)/shard_map/ppermute | solution.py:549
  84.3 5.2 %collective-permute-done.1 = bf16[8,4,8,1024]{3,2,1,0:T(8,128)(2,1)S(1)} collective-permute-done((bf16[8,4,8,1024]{3,2,1,0:T(8,128)(2,1)S(1)}, bf16[8,4,8,1024]{3,2,1,0:T(8,128)(2,1)S(1)}, u32[]{:S(2)}, u32[]{:S(2)}) %collective-permute-start.1) | collective-permute-done | bytes 524320 | tf_op jit(solution)/shard_map/ppermute | solution.py:549
  89.5 0.2 pad_maximum_fusion.chunks
  89.7 19.8 %krylov.1 = (f32[128,128]{1,0:T(8,128)S(1)}, f32[5,3,8,16,8,128]{5,4,3,2,1,0:T(8,128)S(1)}, f32[3,8,16,8,128]{4,3,2,1,0:T(8,128)S(1)}, f32[2,5,128,128]{3,2,1,0:T(8,128)S(1)}) custom-call(s32[1]{0:T(128)} %bitcast.1.place, f32[24]{0:T(128)S(1)} %and_convert_fusion.rowmask, bf16[3,8,4,8,1024]{4,3,2,1,0:T(8,128)(2,1)S(1)} %pad_maximum_fusion.chunks), custom_call_target="tpu_custom_call" | custom-call | flops 400000000 | bytes 60000000 | tf_op jit(solution)/shard_map/krylov/pallas_call | solution.py:368
  109.5 0.1 outer_rows.1.outer
  109.6 14.9 %all_to_all.39 = f32[128,1,128]{2,1,0:T(1,128)S(1)} all-to-all(f32[128,1,128]{2,1,0:T(1,128)S(1)} %bitcast.42), channel_id=1, replica_groups=mesh['slab'=8,'row'=16] {'slab','row'}, dimensions={0} | all-to-all | bytes 131072 | tf_op jit(solution)/shard_map/all_to_all | solution.py:581
  124.5 1.9 %combine.1 = bf16[8,2,3,16,1024]{4,3,2,1,0:T(8,128)(2,1)S(1)} custom-call(f32[128,128]{1,0:T(8,128)S(1)} %bitcast.41, f32[5,3,8,16,8,128]{5,4,3,2,1,0:T(8,128)S(1)} %get-tuple-element.17.v, f32[3,8,16,8,128]{4,3,2,1,0:T(8,128)S(1)} %get-tuple-element.18.s, f32[2,3,128,128]{3,2,1,0:T(8,128)S(1)} %outer_rows.1.outer), custom_call_target="tpu_custom_call" | custom-call | tf_op jit(solution)/shard_map/combine/pallas_call | solution.py:491
  126.4 24.2 %all_to_all.40.back = bf16[8,2,3,16,1024]{4,3,2,1,0:T(8,128)(2,1)S(1)} all-to-all(bf16[8,2,3,16,1024]{4,3,2,1,0:T(8,128)(2,1)S(1)} %combine.1), channel_id=1, replica_groups=mesh['slab'=8,'row'=16] {'slab'}, dimensions={0} | all-to-all | bytes 3145728 | tf_op jit(solution)/shard_map/all_to_all | solution.py:583
  150.6 2.1 %finish.1 = (f32[3,2,64,1024]{3,2,1,0:T(8,128)}, f32[3,2,64,1024]{3,2,1,0:T(8,128)}) custom-call(s32[1]{0:T(128)} %bitcast.flip, bf16[8,2,3,16,1024]{4,3,2,1,0:T(8,128)(2,1)S(1)} %all_to_all.40.back, bf16[512,512]{1,0:T(8,128)(2,1)S(1)} %fusion.perm), custom_call_target="tpu_custom_call" | custom-call | tf_op jit(solution)/shard_map/finish/pallas_call | solution.py:525
  (17 shorter events, 0.1 us)
Async XLA Ops:
  26.5 4.8 %copy-start.4 = (s32[1,1,32,8]{2,3,1,0:T(8,128)S(1)}, s32[1,1,32,8]{2,3,1,0:T(8,128)}, u32[]{:S(2)}) copy-start(s32[1,1,32,8]{2,3,1,0:T(8,128)} %param.11) | copy-start | bytes 3076
  26.5 4.9 %copy-start.5 = (f32[1,1,32,3]{2,1,3,0:T(1,128)S(1)}, f32[1,1,32,3]{2,1,3,0:T(1,128)}, u32[]{:S(2)}) copy-start(f32[1,1,32,3]{2,1,3,0:T(1,128)} %param.15) | copy-start | bytes 1156
  26.5 34.6 %copy-start = (f32[2,64,1024]{2,1,0:T(8,128)S(1)}, f32[2,64,1024]{2,1,0:T(8,128)}, u32[]{:S(2)}) copy-start(f32[2,64,1024]{2,1,0:T(8,128)} %fixed.1) | copy-start | bytes 1572868
  26.6 34.6 %copy-start.1 = (s32[1,1,32]{2,1,0:T(1,128)S(1)}, s32[1,1,32]{2,1,0:T(1,128)}, u32[]{:S(2)}) copy-start(s32[1,1,32]{2,1,0:T(1,128)} %param.12) | copy-start | bytes 388
  26.6 34.6 %copy-start.2 = (s32[1,1,32]{2,1,0:T(1,128)S(1)}, s32[1,1,32]{2,1,0:T(1,128)}, u32[]{:S(2)}) copy-start(s32[1,1,32]{2,1,0:T(1,128)} %param.13) | copy-start | bytes 388
  26.6 34.6 %copy-start.3 = (s32[1,1,32]{2,1,0:T(1,128)S(1)}, s32[1,1,32]{2,1,0:T(1,128)}, u32[]{:S(2)}) copy-start(s32[1,1,32]{2,1,0:T(1,128)} %param.14) | copy-start | bytes 388
  26.6 34.5 %all-to-all-start.1 = ((bf16[128,2,2,16,128]{4,3,2,1,0:T(8,128)(2,1)}), bf16[128,2,2,16,128]{4,3,2,1,0:T(8,128)(2,1)S(1)}, u32[]{:S(2)}, u32[]{:S(2)}) async-start(bf16[128,2,2,16,128]{4,3,2,1,0:T(8,128)(2,1)} %pick.1), calls=%async_computation.1 | async-start | bytes 4194304 | tf_op jit(solution)/shard_map/all_to_all | solution.py:562
  77.5 6.8 %collective-permute-start = (bf16[8,4,8,1024]{3,2,1,0:T(8,128)(2,1)S(1)}, bf16[8,4,8,1024]{3,2,1,0:T(8,128)(2,1)S(1)}, u32[]{:S(2)}, u32[]{:S(2)}) collective-permute-start(bf16[8,4,8,1024]{3,2,1,0:T(8,128)(2,1)S(1)} %copy.32), channel_id=1, source_target_pairs={{0,16},{16,0},{32,48},{48,32},{64,80},{80,64},{96,112},{112,96},{1... | collective-permute-start | bytes 1572872 | tf_op jit(solution)/shard_map/ppermute | solution.py:549
  78.6 10.8 %collective-permute-start.1 = (bf16[8,4,8,1024]{3,2,1,0:T(8,128)(2,1)S(1)}, bf16[8,4,8,1024]{3,2,1,0:T(8,128)(2,1)S(1)}, u32[]{:S(2)}, u32[]{:S(2)}) collective-permute-start(bf16[8,4,8,1024]{3,2,1,0:T(8,128)(2,1)S(1)} %copy.32), channel_id=1, source_target_pairs={{16,32},{32,16},{48,64},{64,48},{80,96},{96,80},{112,113},{113,112... | collective-permute-start | bytes 1572872 | tf_op jit(solution)/shard_map/ppermute | solution.py:549
  80.9 28.6 %collective-permute-start.3 = (bf16[8,2,1024]{2,1,0:T(2,128)(2,1)S(1)}, bf16[8,2,1024]{2,1,0:T(2,128)(2,1)S(1)}, u32[]{:S(2)}, u32[]{:S(2)}) collective-permute-start(bf16[8,2,1024]{2,1,0:T(2,128)(2,1)S(1)} %get-tuple-element.20), channel_id=1, source_target_pairs={{32,64},{48,80},{64,32},{80,48},{96,113},{112,97},{113,96},{97,112... | collective-permute-start | bytes 98312 | tf_op jit(solution)/shard_map/ppermute | solution.py:549
  81.5 27.9 %collective-permute-start.2 = (bf16[8,2,1024]{2,1,0:T(2,128)(2,1)S(1)}, bf16[8,2,1024]{2,1,0:T(2,128)(2,1)S(1)}, u32[]{:S(2)}, u32[]{:S(2)}) collective-permute-start(bf16[8,2,1024]{2,1,0:T(2,128)(2,1)S(1)} %get-tuple-element.21), channel_id=1, source_target_pairs={{0,32},{16,48},{32,0},{48,16},{64,96},{80,112},{96,64},{112,80},{1... | collective-permute-start | bytes 98312 | tf_op jit(solution)/shard_map/ppermute | solution.py:549

commit v6 on v5

--- a/solution.py
+++ b/solution.py
@@ -207,7 +207,7 @@
     return pltpu.VMEM((3, rows, 16, 8, 128), F32)
 
 
-def krylov_kernel(place, rowmask, chunks, mom, vout, sout, ends, s_s, im_s, v0, v1, v2, sems):
+def krylov_kernel(place, rowmask, chunks, mom, vout, sout, ends, v4, s_s, im_s, v0, v1, v2, sems):
     masks = edge_masks()
 
     def chain(c, tiles, end, step):
@@ -275,7 +275,7 @@
                 ends[e, 3, lines, :] = w_s[edge + step // 2, tiles].reshape(WIDE * 8, 128)
                 ends[e, 4, lines, :] = diff.reshape(WIDE * 8, 128)
 
-    def iterate(u_s, v3, v4):
+    def iterate(u_s, v3):
         vs = [v0, v1, v2, v3, v4]
 
         def copy(j):
@@ -320,7 +320,8 @@
                 return carry
 
             lax.fori_loop(off + 2, 22 - off, second, 0, unroll=2)
-            copy(j + 1).start()
+            if j < 3:
+                copy(j + 1).start()
 
         def products(n, sums):
             sums = list(sums)
@@ -350,7 +351,7 @@
             out = jnp.where(lane == q, jnp.sum(sums[q], keepdims=True), out)
         mom[...] = jnp.broadcast_to(out, mom.shape)
         s_copy.wait()
-        for j in range(5):
+        for j in range(4):
             copy(j).wait()
 
     pl.run_scoped(
@@ -358,7 +359,7 @@
         pltpu.VMEM((8, 768, 128), F32),
         pltpu.VMEM((24, 16, 8, 128), F32),
     )
-    pl.run_scoped(iterate, field(22), field(12), field(8))
+    pl.run_scoped(iterate, field(22), field(12))
 
 
 def krylov(chunks, place, rowmask, peers):
@@ -369,12 +370,13 @@
         krylov_kernel,
         out_shape=(
             jax.ShapeDtypeStruct((peers, 128), F32),
-            jax.ShapeDtypeStruct((5, 3, 8, 16, 8, 128), F32),
+            jax.ShapeDtypeStruct((4, 3, 8, 16, 8, 128), F32),
             jax.ShapeDtypeStruct((3, 8, 16, 8, 128), F32),
             jax.ShapeDtypeStruct((2, 5, 128, 128), F32),
+            jax.ShapeDtypeStruct((3, 8, 16, 8, 128), F32),
         ),
         in_specs=[pl.BlockSpec(memory_space=pltpu.SMEM)] * 2 + [vmem],
-        out_specs=(vmem, hbm, hbm, vmem),
+        out_specs=(vmem, hbm, hbm, vmem, vmem),
         scratch_shapes=[
             field(24),
             field(24),
@@ -448,7 +450,7 @@
     return part, rest
 
 
-def combine_kernel(mom, v, s, outer, out, turn):
+def combine_kernel(mom, v, last, s, outer, out, turn):
     line = jnp.sum(mom[...], axis=0, keepdims=True)
     lane = lax.broadcasted_iota(jnp.int32, (1, 128), 1)
     p = [jnp.sum(jnp.where(lane == k, line, 0.0), axis=1, keepdims=True) for k in range(8)]
@@ -463,7 +465,7 @@
             for kx, k, tiles in PARTS:
                 at = pl.ds(pl.multiple_of((kx * 8 + i) * 8, 8), 8)
                 for b in range(WIDE):
-                    vecs = [v[j, c, i, tiles.start + b] for j in range(5)]
+                    vecs = [v[j, c, i, tiles.start + b] for j in range(4)] + [last[c, i, tiles.start + b]]
                     slope = s[c, i, tiles.start + b]
                     weight = slope * slope + (stencil_diag * smoothing + damping)
                     turn[c, 0, FINE * b + k, at, :] = sum(part[j] * vecs[j] for j in range(4))
@@ -486,17 +488,17 @@
                     out[dest, q, c, :, lanes] = turn[c, q, kz, pl.ds(dest, 16, stride=8), :].astype(BF16)
 
 
-def combine(moments, vectors, slopes, outer):
+def combine(moments, vectors, last, slopes, outer):
     vmem = pl.BlockSpec(memory_space=pltpu.VMEM)
     return pl.pallas_call(
         combine_kernel,
         out_shape=jax.ShapeDtypeStruct((8, 2, 3, 16, 1024), BF16),
-        in_specs=[vmem] * 4,
+        in_specs=[vmem] * 5,
         out_specs=vmem,
         scratch_shapes=[pltpu.VMEM((3, 2, 8, 128, 128), F32)],
         compiler_params=pltpu.CompilerParams(vmem_limit_bytes=24 * 1024 * 1024),
         name="combine",
-    )(moments, vectors, slopes, outer)
+    )(moments, vectors, last, slopes, outer)
 
 
 def finish_kernel(flip, back, perm, sol, res, cells_s, sems):
@@ -570,7 +572,7 @@
     place = (slab + flip[0] * (7 - 2 * slab)).reshape(1)
     rows = start + jnp.arange(24, dtype=jnp.int32)
     rowmask = ((rows >= 0) & (rows < height * lax.axis_size("row"))).astype(F32)
-    moments, vectors, slopes, ends = krylov(chunks, place, rowmask, peers)
+    moments, vectors, slopes, ends, last = krylov(chunks, place, rowmask, peers)
     upper = place[0] // 2 % 2 == 1
     inwards = jnp.where(upper, own[:, 0:2, 0], own[:, 0:2, 7])
     outwards = jnp.where(upper, own[:, 0:2, 7], own[:, 0:2, 0])
@@ -579,7 +581,7 @@
     outer = outer_rows(ends, place, *far)
     moments, outer = lax.optimization_barrier((moments, outer))
     moments = lax.all_to_all(moments, BOTH, split_axis=0, concat_axis=0, tiled=True)
-    back = combine(moments, vectors, slopes, outer)
+    back = combine(moments, vectors, last, slopes, outer)
     back = lax.all_to_all(back, "slab", split_axis=0, concat_axis=0, tiled=True)
     return finish(back, flip, perm)
 

time: 153 us -> 153 us (level)
  no operation moved by 1% of the time
where the time goes in v6:
time: 153 us
  blocking collectives  73 us (48%)
  waiting for transfers between devices  33.8 us (22%)
  Pallas kernels  30.9 us (20%)
  starting transfers between devices  11.3 us (7%)
  local copies, waits for them, and re-layouts  1.83 us (1%)
    all_to_all x1, waiting for transfers between devices, per_device(): lax.all_to_all(outgoing, BOTH, split_axis=0, concat_axis=0, tiled=True)  28.7 us
    all_to_all x1, blocking collectives, per_device(): back = lax.all_to_all(back, 'slab', split_axis=0, concat_axis=0, tiled=True)  24.2 us
    all_to_all x1, blocking collectives, per_device(): asked = lax.all_to_all(asked, BOTH, split_axis=0, concat_axis=0, tiled=True)  21.1 us
    pallas_call x1, Pallas kernels, krylov(): pl.pallas_call(krylov_kernel, out_shape=(jax.ShapeDtypeStruct((peers, 128...  19.7 us
    all_to_all x1, blocking collectives, per_device(): lax.all_to_all(moments, BOTH, split_axis=0, concat_axis=0, tiled=True)  14.9 us
    all_to_all x1, blocking collectives, per_device(): own = lax.all_to_all(own, 'slab', split_axis=0, concat_axis=0, tiled=True)  12.8 us
    ppermute x4, starting transfers between devices, exchange(): return lax.ppermute(cells, BOTH, pairs)  6.66 us
    ppermute x4, waiting for transfers between devices, exchange(): return lax.ppermute(cells, BOTH, pairs)  5.16 us
  transfers between devices with their start and end apart: 5, of which 2 were waited for; matrix products, arithmetic and copies ran while one was open for 1% of the time, Pallas kernels for 13%

profile of v6, /device:TPU:1, one launch (start us, length us, event | category | flops | bytes accessed | tf_op | source)
XLA Modules:
  0.0 152.7 jit_solution(16599823592678634915)
XLA Ops:
  0.6 0.8 copy.20
  1.4 21.1 %all_to_all.37 = s32[128,1,128]{2,1,0:T(1,128)} all-to-all(s32[128,1,128]{2,1,0:T(1,128)S(1)} %bitcast.50), channel_id=1, replica_groups=mesh['slab'=8,'row'=16] {'slab','row'}, dimensions={0} | all-to-all | bytes 131072 | tf_op jit(solution)/shard_map/all_to_all | solution.py:562
  22.6 3.9 %pick.1 = bf16[128,2,2,16,128]{4,3,2,1,0:T(8,128)(2,1)} custom-call(s32[128,128]{1,0:T(8,128)} %bitcast.49, bf16[2,64,1024]{2,1,0:T(8,128)(2,1)} %moving.1), custom_call_target="tpu_custom_call" | custom-call | tf_op jit(solution)/shard_map/pick/pallas_call | solution.py:74
  26.5 0.0 copy-start.4
  26.5 0.0 copy-start.5
  26.5 0.0 copy-start
  26.6 0.0 copy-start.1
  26.6 0.0 copy-start.3
  26.6 4.7 %all-to-all-start.1 = ((bf16[128,2,2,16,128]{4,3,2,1,0:T(8,128)(2,1)}), bf16[128,2,2,16,128]{4,3,2,1,0:T(8,128)(2,1)S(1)}, u32[]{:S(2)}, u32[]{:S(2)}) async-start(bf16[128,2,2,16,128]{4,3,2,1,0:T(8,128)(2,1)} %pick.1), calls=%async_computation.1 | async-start | bytes 4194304 | tf_op jit(solution)/shard_map/all_to_all | solution.py:564
  31.3 0.1 copy.18
  31.4 0.1 reshape_squeeze.3.foot
  31.5 0.1 copy.19
  31.6 0.1 reshape.53.wts
  31.8 0.6 fusion.perm
  32.5 28.7 %all-to-all-done.1 = bf16[128,2,2,16,128]{4,3,2,1,0:T(8,128)(2,1)S(1)} async-done(((bf16[128,2,2,16,128]{4,3,2,1,0:T(8,128)(2,1)}), bf16[128,2,2,16,128]{4,3,2,1,0:T(8,128)(2,1)S(1)}, u32[]{:S(2)}, u32[]{:S(2)}) %all-to-all-start.1) | async-done | bytes 2097184 | tf_op jit(solution)/shard_map/all_to_all | solution.py:564
  61.2 3.0 %warp.1 = bf16[8,4,8,1024]{3,2,1,0:T(8,128)(2,1)S(1)} custom-call(s32[256]{0:T(256)S(1)} %reshape_squeeze.3.foot, s32[32]{0:T(128)S(1)} %bitcast.43, s32[32]{0:T(128)S(1)} %bitcast.44, s32[32]{0:T(128)S(1)} %bitcast.45, f32[192]{0:T(256)S(1)} %reshape.53.wts, s32[1]{0:T(128)} %bitcast.flip, bf16[256,32,128]{2,1,0:T(8,128)(2,1)S(1)} %bitcast.40, ...), custom_call_target="tpu_custom_call" | custom-call | tf_op jit(solution)/shard_map/warp/pallas_call | solution.py:149
  64.2 0.4 copy.21
  64.6 12.8 %all_to_all.38 = bf16[8,4,8,1024]{3,1,2,0:T(4,128)(2,1)S(1)} all-to-all(bf16[8,4,8,1024]{3,1,2,0:T(4,128)(2,1)S(1)} %copy.21), channel_id=1, replica_groups=mesh['slab'=8,'row'=16] {'slab'}, dimensions={0} | all-to-all | bytes 1048576 | tf_op jit(solution)/shard_map/all_to_all | solution.py:570
  77.4 0.2 copy.32
  77.5 1.1 collective-permute-start
  78.6 2.1 %collective-permute-start.1 = (bf16[8,4,8,1024]{3,2,1,0:T(8,128)(2,1)S(1)}, bf16[8,4,8,1024]{3,2,1,0:T(8,128)(2,1)S(1)}, u32[]{:S(2)}, u32[]{:S(2)}) collective-permute-start(bf16[8,4,8,1024]{3,2,1,0:T(8,128)(2,1)S(1)} %copy.32), channel_id=1, source_target_pairs={{16,32},{32,16},{48,64},{64,48},{80,96},{96,80},{112,113},{113,112... | collective-permute-start | bytes 1572872 | tf_op jit(solution)/shard_map/ppermute | solution.py:551
  80.8 0.1 fusion.2
  80.9 0.7 collective-permute-start.3
  81.5 2.8 %collective-permute-start.2 = (bf16[8,2,1024]{2,1,0:T(2,128)(2,1)S(1)}, bf16[8,2,1024]{2,1,0:T(2,128)(2,1)S(1)}, u32[]{:S(2)}, u32[]{:S(2)}) collective-permute-start(bf16[8,2,1024]{2,1,0:T(2,128)(2,1)S(1)} %get-tuple-element.23), channel_id=1, source_target_pairs={{0,32},{16,48},{32,0},{48,16},{64,96},{80,112},{96,64},{112,80},{1... | collective-permute-start | bytes 98312 | tf_op jit(solution)/shard_map/ppermute | solution.py:551
  84.3 5.2 %collective-permute-done.1 = bf16[8,4,8,1024]{3,2,1,0:T(8,128)(2,1)S(1)} collective-permute-done((bf16[8,4,8,1024]{3,2,1,0:T(8,128)(2,1)S(1)}, bf16[8,4,8,1024]{3,2,1,0:T(8,128)(2,1)S(1)}, u32[]{:S(2)}, u32[]{:S(2)}) %collective-permute-start.1) | collective-permute-done | bytes 524320 | tf_op jit(solution)/shard_map/ppermute | solution.py:551
  89.5 0.2 pad_maximum_fusion.chunks
  89.7 19.7 %krylov.1 = (f32[128,128]{1,0:T(8,128)S(1)}, f32[4,3,8,16,8,128]{5,4,3,2,1,0:T(8,128)S(1)}, f32[3,8,16,8,128]{4,3,2,1,0:T(8,128)S(1)}, f32[2,5,128,128]{3,2,1,0:T(8,128)S(1)}, f32[3,8,16,8,128]{4,3,2,1,0:T(8,128)S(1)}) custom-call(s32[1]{0:T(128)} %bitcast.1.place, f32[24]{0:T(128)S(1)} %and_convert_fusion.rowmask, ...), custom_call_target="tpu_custom_call" | custom-call | flops 400000000 | bytes 60000000 | tf_op jit(solution)/shard_map/krylov/pallas_call | solution.py:369
  109.4 0.1 outer_rows.1.outer
  109.5 14.9 %all_to_all.39 = f32[128,1,128]{2,1,0:T(1,128)S(1)} all-to-all(f32[128,1,128]{2,1,0:T(1,128)S(1)} %bitcast.42), channel_id=1, replica_groups=mesh['slab'=8,'row'=16] {'slab','row'}, dimensions={0} | all-to-all | bytes 131072 | tf_op jit(solution)/shard_map/all_to_all | solution.py:583
  124.4 1.9 %combine.1 = bf16[8,2,3,16,1024]{4,3,2,1,0:T(8,128)(2,1)S(1)} custom-call(f32[128,128]{1,0:T(8,128)S(1)} %bitcast.41, f32[4,3,8,16,8,128]{5,4,3,2,1,0:T(8,128)S(1)} %get-tuple-element.18.v, f32[3,8,16,8,128]{4,3,2,1,0:T(8,128)S(1)} %get-tuple-element.19.last, f32[3,8,16,8,128]{4,3,2,1,0:T(8,128)S(1)} %get-tuple-element.20.s, ...), custom_call_target="tpu_custom_call" | custom-call | tf_op jit(solution)/shard_map/combine/pallas_call | solution.py:493
  126.3 24.2 %all_to_all.40.back = bf16[8,2,3,16,1024]{4,3,2,1,0:T(8,128)(2,1)S(1)} all-to-all(bf16[8,2,3,16,1024]{4,3,2,1,0:T(8,128)(2,1)S(1)} %combine.1), channel_id=1, replica_groups=mesh['slab'=8,'row'=16] {'slab'}, dimensions={0} | all-to-all | bytes 3145728 | tf_op jit(solution)/shard_map/all_to_all | solution.py:585
  150.5 2.1 %finish.1 = (f32[3,2,64,1024]{3,2,1,0:T(8,128)}, f32[3,2,64,1024]{3,2,1,0:T(8,128)}) custom-call(s32[1]{0:T(128)} %bitcast.flip, bf16[8,2,3,16,1024]{4,3,2,1,0:T(8,128)(2,1)S(1)} %all_to_all.40.back, bf16[512,512]{1,0:T(8,128)(2,1)S(1)} %fusion.perm), custom_call_target="tpu_custom_call" | custom-call | tf_op jit(solution)/shard_map/finish/pallas_call | solution.py:527
  (17 shorter events, 0.1 us)
Async XLA Ops:
  26.5 4.8 %copy-start.4 = (s32[1,1,32,8]{2,3,1,0:T(8,128)S(1)}, s32[1,1,32,8]{2,3,1,0:T(8,128)}, u32[]{:S(2)}) copy-start(s32[1,1,32,8]{2,3,1,0:T(8,128)} %param.11) | copy-start | bytes 3076
  26.5 4.9 %copy-start.5 = (f32[1,1,32,3]{2,1,3,0:T(1,128)S(1)}, f32[1,1,32,3]{2,1,3,0:T(1,128)}, u32[]{:S(2)}) copy-start(f32[1,1,32,3]{2,1,3,0:T(1,128)} %param.15) | copy-start | bytes 1156
  26.5 34.6 %copy-start = (f32[2,64,1024]{2,1,0:T(8,128)S(1)}, f32[2,64,1024]{2,1,0:T(8,128)}, u32[]{:S(2)}) copy-start(f32[2,64,1024]{2,1,0:T(8,128)} %fixed.1) | copy-start | bytes 1572868
  26.6 34.6 %copy-start.1 = (s32[1,1,32]{2,1,0:T(1,128)S(1)}, s32[1,1,32]{2,1,0:T(1,128)}, u32[]{:S(2)}) copy-start(s32[1,1,32]{2,1,0:T(1,128)} %param.12) | copy-start | bytes 388
  26.6 34.6 %copy-start.2 = (s32[1,1,32]{2,1,0:T(1,128)S(1)}, s32[1,1,32]{2,1,0:T(1,128)}, u32[]{:S(2)}) copy-start(s32[1,1,32]{2,1,0:T(1,128)} %param.13) | copy-start | bytes 388
  26.6 34.6 %copy-start.3 = (s32[1,1,32]{2,1,0:T(1,128)S(1)}, s32[1,1,32]{2,1,0:T(1,128)}, u32[]{:S(2)}) copy-start(s32[1,1,32]{2,1,0:T(1,128)} %param.14) | copy-start | bytes 388
  26.6 34.5 %all-to-all-start.1 = ((bf16[128,2,2,16,128]{4,3,2,1,0:T(8,128)(2,1)}), bf16[128,2,2,16,128]{4,3,2,1,0:T(8,128)(2,1)S(1)}, u32[]{:S(2)}, u32[]{:S(2)}) async-start(bf16[128,2,2,16,128]{4,3,2,1,0:T(8,128)(2,1)} %pick.1), calls=%async_computation.1 | async-start | bytes 4194304 | tf_op jit(solution)/shard_map/all_to_all | solution.py:564
  77.5 6.8 %collective-permute-start = (bf16[8,4,8,1024]{3,2,1,0:T(8,128)(2,1)S(1)}, bf16[8,4,8,1024]{3,2,1,0:T(8,128)(2,1)S(1)}, u32[]{:S(2)}, u32[]{:S(2)}) collective-permute-start(bf16[8,4,8,1024]{3,2,1,0:T(8,128)(2,1)S(1)} %copy.32), channel_id=1, source_target_pairs={{0,16},{16,0},{32,48},{48,32},{64,80},{80,64},{96,112},{112,96},{1... | collective-permute-start | bytes 1572872 | tf_op jit(solution)/shard_map/ppermute | solution.py:551
  78.6 10.8 %collective-permute-start.1 = (bf16[8,4,8,1024]{3,2,1,0:T(8,128)(2,1)S(1)}, bf16[8,4,8,1024]{3,2,1,0:T(8,128)(2,1)S(1)}, u32[]{:S(2)}, u32[]{:S(2)}) collective-permute-start(bf16[8,4,8,1024]{3,2,1,0:T(8,128)(2,1)S(1)} %copy.32), channel_id=1, source_target_pairs={{16,32},{32,16},{48,64},{64,48},{80,96},{96,80},{112,113},{113,112... | collective-permute-start | bytes 1572872 | tf_op jit(solution)/shard_map/ppermute | solution.py:551
  80.9 28.5 %collective-permute-start.3 = (bf16[8,2,1024]{2,1,0:T(2,128)(2,1)S(1)}, bf16[8,2,1024]{2,1,0:T(2,128)(2,1)S(1)}, u32[]{:S(2)}, u32[]{:S(2)}) collective-permute-start(bf16[8,2,1024]{2,1,0:T(2,128)(2,1)S(1)} %get-tuple-element.22), channel_id=1, source_target_pairs={{32,64},{48,80},{64,32},{80,48},{96,113},{112,97},{113,96},{97,112... | collective-permute-start | bytes 98312 | tf_op jit(solution)/shard_map/ppermute | solution.py:551
  81.5 27.9 %collective-permute-start.2 = (bf16[8,2,1024]{2,1,0:T(2,128)(2,1)S(1)}, bf16[8,2,1024]{2,1,0:T(2,128)(2,1)S(1)}, u32[]{:S(2)}, u32[]{:S(2)}) collective-permute-start(bf16[8,2,1024]{2,1,0:T(2,128)(2,1)S(1)} %get-tuple-element.23), channel_id=1, source_target_pairs={{0,32},{16,48},{32,0},{48,16},{64,96},{80,112},{96,64},{112,80},{1... | collective-permute-start | bytes 98312 | tf_op jit(solution)/shard_map/ppermute | solution.py:551

commit v7 on v6

--- a/solution.py
+++ b/solution.py
@@ -48,7 +48,7 @@
 
     def peer(p, carry):
         for slot in range(slots):
-            number = asked[p, slot]
+            number = asked[p * slots + slot]
             tile = jnp.maximum(number, 0)
             rows = pl.ds(pl.multiple_of(lax.shift_right_logical(tile, 3) * TY, TY), TY)
             lanes = pl.ds(pl.multiple_of(lax.bitwise_and(tile, 7) * TZ, TZ), TZ)
@@ -71,6 +71,7 @@
 def pick(asked, moving, slots):
     hbm = pl.BlockSpec(memory_space=pltpu.HBM)
     shape = (asked.shape[0], slots, moving.shape[0], TY, TZ)
+    asked = asked[:, :slots].reshape(-1)
     return pl.pallas_call(
         pick_kernel,
         out_shape=jax.ShapeDtypeStruct(shape, BF16),

time: 153 us -> 153 us (level)
  no operation moved by 1% of the time
where the time goes in v7:
time: 153 us; the launch traced here: 152 us
  blocking collectives  72.7 us (48%)
  waiting for transfers between devices  33.9 us (22%)
  Pallas kernels  30.1 us (20%)
  starting transfers between devices  11.2 us (7%)
  local copies, waits for them, and re-layouts  2.53 us (2%)
    all_to_all x1, waiting for transfers between devices, per_device(): lax.all_to_all(outgoing, BOTH, split_axis=0, concat_axis=0, tiled=True)  28.7 us
    all_to_all x1, blocking collectives, per_device(): back = lax.all_to_all(back, 'slab', split_axis=0, concat_axis=0, tiled=True)  24.2 us
    all_to_all x1, blocking collectives, per_device(): asked = lax.all_to_all(asked, BOTH, split_axis=0, concat_axis=0, tiled=True)  20.9 us
    pallas_call x1, Pallas kernels, krylov(): pl.pallas_call(krylov_kernel, out_shape=(jax.ShapeDtypeStruct((peers, 128...  19.7 us
    all_to_all x1, blocking collectives, per_device(): lax.all_to_all(moments, BOTH, split_axis=0, concat_axis=0, tiled=True)  14.9 us
    all_to_all x1, blocking collectives, per_device(): own = lax.all_to_all(own, 'slab', split_axis=0, concat_axis=0, tiled=True)  12.8 us
    ppermute x4, starting transfers between devices, exchange(): return lax.ppermute(cells, BOTH, pairs)  6.66 us
    ppermute x4, waiting for transfers between devices, exchange(): return lax.ppermute(cells, BOTH, pairs)  5.16 us
  transfers between devices with their start and end apart: 5, of which 2 were waited for; matrix products, arithmetic and copies ran while one was open for 1% of the time, Pallas kernels for 13%

profile of v7, /device:TPU:1, one launch (start us, length us, event | category | flops | bytes accessed | tf_op | source)
XLA Modules:
  0.0 152.2 jit_solution(5343499516993075049)
XLA Ops:
  0.6 0.8 copy.19
  1.4 20.9 %all_to_all.38 = s32[128,1,128]{2,1,0:T(1,128)S(1)} all-to-all(s32[128,1,128]{2,1,0:T(1,128)S(1)} %bitcast.50), channel_id=1, replica_groups=mesh['slab'=8,'row'=16] {'slab','row'}, dimensions={0} | all-to-all | bytes 131072 | tf_op jit(solution)/shard_map/all_to_all | solution.py:563
  22.3 0.7 reshape.57.asked_hbm
  23.0 3.1 %pick.1 = bf16[128,2,2,16,128]{4,3,2,1,0:T(8,128)(2,1)} custom-call(s32[256]{0:T(256)} %reshape.57.asked_hbm, bf16[2,64,1024]{2,1,0:T(8,128)(2,1)} %moving.1), custom_call_target="tpu_custom_call" | custom-call | tf_op jit(solution)/shard_map/pick/pallas_call | solution.py:75
  26.2 0.0 copy-start.4
  26.2 0.0 copy-start.5
  26.2 0.0 copy-start
  26.2 0.0 copy-start.3
  26.2 4.6 %all-to-all-start.1 = ((bf16[128,2,2,16,128]{4,3,2,1,0:T(8,128)(2,1)}), bf16[128,2,2,16,128]{4,3,2,1,0:T(8,128)(2,1)S(1)}, u32[]{:S(2)}, u32[]{:S(2)}) async-start(bf16[128,2,2,16,128]{4,3,2,1,0:T(8,128)(2,1)} %pick.1), calls=%async_computation.1 | async-start | bytes 4194304 | tf_op jit(solution)/shard_map/all_to_all | solution.py:565
  30.8 0.1 copy.17
  30.9 0.1 reshape_squeeze.3.foot
  31.0 0.1 copy.18
  31.1 0.1 reshape.56.wts
  31.3 0.6 fusion.perm
  32.0 28.7 %all-to-all-done.1 = bf16[128,2,2,16,128]{4,3,2,1,0:T(8,128)(2,1)S(1)} async-done(((bf16[128,2,2,16,128]{4,3,2,1,0:T(8,128)(2,1)}), bf16[128,2,2,16,128]{4,3,2,1,0:T(8,128)(2,1)S(1)}, u32[]{:S(2)}, u32[]{:S(2)}) %all-to-all-start.1) | async-done | bytes 2097184 | tf_op jit(solution)/shard_map/all_to_all | solution.py:565
  60.7 3.0 %warp.1 = bf16[8,4,8,1024]{3,2,1,0:T(8,128)(2,1)S(1)} custom-call(s32[256]{0:T(256)S(1)} %reshape_squeeze.3.foot, s32[32]{0:T(128)S(1)} %bitcast.44, s32[32]{0:T(128)S(1)} %bitcast.45, s32[32]{0:T(128)S(1)} %bitcast.46, f32[192]{0:T(256)S(1)} %reshape.56.wts, s32[1]{0:T(128)} %bitcast.flip, bf16[256,32,128]{2,1,0:T(8,128)(2,1)S(1)} %bitcast.41, ...), custom_call_target="tpu_custom_call" | custom-call | tf_op jit(solution)/shard_map/warp/pallas_call | solution.py:150
  63.7 0.4 copy.20
  64.2 12.8 %all_to_all.39 = bf16[8,4,8,1024]{3,1,2,0:T(4,128)(2,1)S(1)} all-to-all(bf16[8,4,8,1024]{3,1,2,0:T(4,128)(2,1)S(1)} %copy.20), channel_id=1, replica_groups=mesh['slab'=8,'row'=16] {'slab'}, dimensions={0} | all-to-all | bytes 1048576 | tf_op jit(solution)/shard_map/all_to_all | solution.py:571
  76.9 0.2 copy.31
  77.1 1.1 collective-permute-start
  78.2 2.1 %collective-permute-start.1 = (bf16[8,4,8,1024]{3,2,1,0:T(8,128)(2,1)S(1)}, bf16[8,4,8,1024]{3,2,1,0:T(8,128)(2,1)S(1)}, u32[]{:S(2)}, u32[]{:S(2)}) collective-permute-start(bf16[8,4,8,1024]{3,2,1,0:T(8,128)(2,1)S(1)} %copy.31), channel_id=1, source_target_pairs={{16,32},{32,16},{48,64},{64,48},{80,96},{96,80},{112,113},{113,112... | collective-permute-start | bytes 1572872 | tf_op jit(solution)/shard_map/ppermute | solution.py:552
  80.4 0.1 fusion.2
  80.5 0.7 collective-permute-start.3
  81.1 2.8 %collective-permute-start.2 = (bf16[8,2,1024]{2,1,0:T(2,128)(2,1)S(1)}, bf16[8,2,1024]{2,1,0:T(2,128)(2,1)S(1)}, u32[]{:S(2)}, u32[]{:S(2)}) collective-permute-start(bf16[8,2,1024]{2,1,0:T(2,128)(2,1)S(1)} %get-tuple-element.23), channel_id=1, source_target_pairs={{0,32},{16,48},{32,0},{48,16},{64,96},{80,112},{96,64},{112,80},{1... | collective-permute-start | bytes 98312 | tf_op jit(solution)/shard_map/ppermute | solution.py:552
  83.9 5.2 %collective-permute-done.1 = bf16[8,4,8,1024]{3,2,1,0:T(8,128)(2,1)S(1)} collective-permute-done((bf16[8,4,8,1024]{3,2,1,0:T(8,128)(2,1)S(1)}, bf16[8,4,8,1024]{3,2,1,0:T(8,128)(2,1)S(1)}, u32[]{:S(2)}, u32[]{:S(2)}) %collective-permute-start.1) | collective-permute-done | bytes 524320 | tf_op jit(solution)/shard_map/ppermute | solution.py:552
  89.1 0.2 pad_maximum_fusion.chunks
  89.2 19.7 %krylov.1 = (f32[128,128]{1,0:T(8,128)S(1)}, f32[4,3,8,16,8,128]{5,4,3,2,1,0:T(8,128)S(1)}, f32[3,8,16,8,128]{4,3,2,1,0:T(8,128)S(1)}, f32[2,5,128,128]{3,2,1,0:T(8,128)S(1)}, f32[3,8,16,8,128]{4,3,2,1,0:T(8,128)S(1)}) custom-call(s32[1]{0:T(128)} %bitcast.1.place, f32[24]{0:T(128)S(1)} %and_convert_fusion.rowmask, ...), custom_call_target="tpu_custom_call" | custom-call | flops 400000000 | bytes 60000000 | tf_op jit(solution)/shard_map/krylov/pallas_call | solution.py:370
  109.0 0.1 outer_rows.1.outer
  109.1 14.9 %all_to_all.40 = f32[128,1,128]{2,1,0:T(1,128)S(1)} all-to-all(f32[128,1,128]{2,1,0:T(1,128)S(1)} %bitcast.43), channel_id=1, replica_groups=mesh['slab'=8,'row'=16] {'slab','row'}, dimensions={0} | all-to-all | bytes 131072 | tf_op jit(solution)/shard_map/all_to_all | solution.py:584
  124.0 1.9 %combine.1 = bf16[8,2,3,16,1024]{4,3,2,1,0:T(8,128)(2,1)S(1)} custom-call(f32[128,128]{1,0:T(8,128)S(1)} %bitcast.42, f32[4,3,8,16,8,128]{5,4,3,2,1,0:T(8,128)S(1)} %get-tuple-element.18.v, f32[3,8,16,8,128]{4,3,2,1,0:T(8,128)S(1)} %get-tuple-element.19.last, f32[3,8,16,8,128]{4,3,2,1,0:T(8,128)S(1)} %get-tuple-element.20.s, ...), custom_call_target="tpu_custom_call" | custom-call | tf_op jit(solution)/shard_map/combine/pallas_call | solution.py:494
  125.9 24.2 %all_to_all.41.back = bf16[8,2,3,16,1024]{4,3,2,1,0:T(8,128)(2,1)S(1)} all-to-all(bf16[8,2,3,16,1024]{4,3,2,1,0:T(8,128)(2,1)S(1)} %combine.1), channel_id=1, replica_groups=mesh['slab'=8,'row'=16] {'slab'}, dimensions={0} | all-to-all | bytes 3145728 | tf_op jit(solution)/shard_map/all_to_all | solution.py:586
  150.1 2.1 %finish.1 = (f32[3,2,64,1024]{3,2,1,0:T(8,128)}, f32[3,2,64,1024]{3,2,1,0:T(8,128)}) custom-call(s32[1]{0:T(128)} %bitcast.flip, bf16[8,2,3,16,1024]{4,3,2,1,0:T(8,128)(2,1)S(1)} %all_to_all.41.back, bf16[512,512]{1,0:T(8,128)(2,1)S(1)} %fusion.perm), custom_call_target="tpu_custom_call" | custom-call | tf_op jit(solution)/shard_map/finish/pallas_call | solution.py:528
  (18 shorter events, 0.1 us)
Async XLA Ops:
  26.2 4.7 %copy-start.4 = (s32[1,1,32,8]{2,3,1,0:T(8,128)S(1)}, s32[1,1,32,8]{2,3,1,0:T(8,128)}, u32[]{:S(2)}) copy-start(s32[1,1,32,8]{2,3,1,0:T(8,128)} %param.11) | copy-start | bytes 3076
  26.2 4.8 %copy-start.5 = (f32[1,1,32,3]{2,1,3,0:T(1,128)S(1)}, f32[1,1,32,3]{2,1,3,0:T(1,128)}, u32[]{:S(2)}) copy-start(f32[1,1,32,3]{2,1,3,0:T(1,128)} %param.15) | copy-start | bytes 1156
  26.2 34.5 %copy-start = (f32[2,64,1024]{2,1,0:T(8,128)S(1)}, f32[2,64,1024]{2,1,0:T(8,128)}, u32[]{:S(2)}) copy-start(f32[2,64,1024]{2,1,0:T(8,128)} %fixed.1) | copy-start | bytes 1572868
  26.2 34.5 %copy-start.1 = (s32[1,1,32]{2,1,0:T(1,128)S(1)}, s32[1,1,32]{2,1,0:T(1,128)}, u32[]{:S(2)}) copy-start(s32[1,1,32]{2,1,0:T(1,128)} %param.12) | copy-start | bytes 388
  26.2 34.5 %copy-start.2 = (s32[1,1,32]{2,1,0:T(1,128)S(1)}, s32[1,1,32]{2,1,0:T(1,128)}, u32[]{:S(2)}) copy-start(s32[1,1,32]{2,1,0:T(1,128)} %param.13) | copy-start | bytes 388
  26.2 34.5 %copy-start.3 = (s32[1,1,32]{2,1,0:T(1,128)S(1)}, s32[1,1,32]{2,1,0:T(1,128)}, u32[]{:S(2)}) copy-start(s32[1,1,32]{2,1,0:T(1,128)} %param.14) | copy-start | bytes 388
  26.2 34.5 %all-to-all-start.1 = ((bf16[128,2,2,16,128]{4,3,2,1,0:T(8,128)(2,1)}), bf16[128,2,2,16,128]{4,3,2,1,0:T(8,128)(2,1)S(1)}, u32[]{:S(2)}, u32[]{:S(2)}) async-start(bf16[128,2,2,16,128]{4,3,2,1,0:T(8,128)(2,1)} %pick.1), calls=%async_computation.1 | async-start | bytes 4194304 | tf_op jit(solution)/shard_map/all_to_all | solution.py:565
  77.1 6.8 %collective-permute-start = (bf16[8,4,8,1024]{3,2,1,0:T(8,128)(2,1)S(1)}, bf16[8,4,8,1024]{3,2,1,0:T(8,128)(2,1)S(1)}, u32[]{:S(2)}, u32[]{:S(2)}) collective-permute-start(bf16[8,4,8,1024]{3,2,1,0:T(8,128)(2,1)S(1)} %copy.31), channel_id=1, source_target_pairs={{0,16},{16,0},{32,48},{48,32},{64,80},{80,64},{96,112},{112,96},{1... | collective-permute-start | bytes 1572872 | tf_op jit(solution)/shard_map/ppermute | solution.py:552
  78.2 10.8 %collective-permute-start.1 = (bf16[8,4,8,1024]{3,2,1,0:T(8,128)(2,1)S(1)}, bf16[8,4,8,1024]{3,2,1,0:T(8,128)(2,1)S(1)}, u32[]{:S(2)}, u32[]{:S(2)}) collective-permute-start(bf16[8,4,8,1024]{3,2,1,0:T(8,128)(2,1)S(1)} %copy.31), channel_id=1, source_target_pairs={{16,32},{32,16},{48,64},{64,48},{80,96},{96,80},{112,113},{113,112... | collective-permute-start | bytes 1572872 | tf_op jit(solution)/shard_map/ppermute | solution.py:552
  80.5 28.5 %collective-permute-start.3 = (bf16[8,2,1024]{2,1,0:T(2,128)(2,1)S(1)}, bf16[8,2,1024]{2,1,0:T(2,128)(2,1)S(1)}, u32[]{:S(2)}, u32[]{:S(2)}) collective-permute-start(bf16[8,2,1024]{2,1,0:T(2,128)(2,1)S(1)} %get-tuple-element.22), channel_id=1, source_target_pairs={{32,64},{48,80},{64,32},{80,48},{96,113},{112,97},{113,96},{97,112... | collective-permute-start | bytes 98312 | tf_op jit(solution)/shard_map/ppermute | solution.py:552
  81.1 27.9 %collective-permute-start.2 = (bf16[8,2,1024]{2,1,0:T(2,128)(2,1)S(1)}, bf16[8,2,1024]{2,1,0:T(2,128)(2,1)S(1)}, u32[]{:S(2)}, u32[]{:S(2)}) collective-permute-start(bf16[8,2,1024]{2,1,0:T(2,128)(2,1)S(1)} %get-tuple-element.23), channel_id=1, source_target_pairs={{0,32},{16,48},{32,0},{48,16},{64,96},{80,112},{96,64},{112,80},{1... | collective-permute-start | bytes 98312 | tf_op jit(solution)/shard_map/ppermute | solution.py:552
